TPU v7x, 128 devices: a whole 4x4x4 slice. The times are simulated.
128 devices in a mesh: seq: 16 (over z, x), table: 8 (over y, core).
Axes of the slice: x: 4, y: 4, z: 4, core: 2. Of those that a mesh axis runs over, the one named last changes fastest.
Arguments:
- hidden: bfloat16 [65536, 768], P(('seq', 'table')), may hold values from -6 to 6
- gain: float32 [768], replicated, may hold values from 0.5 to 1.5
- queries: bfloat16 [65536, 768], P(('seq', 'table')), may hold values from -40 to 40
- keys: bfloat16 [65536, 768], P(('seq', 'table')), may hold values from -40 to 40
- values: bfloat16 [65536, 768], P(('seq', 'table')), may hold values from -6 to 6
- w_query: bfloat16 [768, 768], replicated, may hold values from -0.21875 to 0.21875
- w_key: bfloat16 [768, 768], replicated, may hold values from -0.21875 to 0.21875
- w_value: bfloat16 [768, 768], replicated, may hold values from -0.21875 to 0.21875
- w_out: bfloat16 [768, 768], replicated, may hold values from -0.21875 to 0.21875
- grad_out: bfloat16 [65536, 768], P(('seq', 'table')), may hold values from -6 to 6
- doc_lengths: int32 [64], replicated, may hold values from 1 to 4096, 65536 in all
- hash_ids: int32 [2, 65536], P(None, ('seq', 'table')), may hold values from 0 to 262143, as said below
Outputs:
- grad_hidden: bfloat16 [65536, 768], P(('seq', 'table'))
- table_grads: bfloat16 [2, 262144, 768], P(None, ('seq', 'table'))
Inputs may be any that keep to these rules, and one draw needn't show every extreme that they name: `hash_ids`: rows owner * 2048 to owner * 2048 + 2047 belong to device owner of seq+table. Among the 512 bytes of one device, at most 20 have their row of one table at one owner, and these name at most 5 distinct rows; in every table each device sends exactly 20 bytes naming exactly 5 distinct rows to some owner.
All inputs are finite; a program needn't handle non-finite values.
Results may differ from a plain program's by a relative error of at most 0.0094.
Values may be sent and summed in bfloat16 or wider, within the bound.
No kernel may reach another device: no remote copies, remote signals or barrier semaphores. Data moves between devices by JAX's collectives and lax.ppermute only.
A program may use at most 192 MiB of HBM per device.

v0:
```python
import jax
import jax.numpy as jnp
from jax import lax
from jax.sharding import PartitionSpec as P

HEADS = 12
HD = 64
WINDOW = 512
NG = 2
ROWS_DEV = 2048
HOT = 16


EPS = 1e-06
NEG = -1e30


def shifted(shard, axis, by):
    count = lax.axis_size(axis)
    pairs = [(i, i + by) for i in range(count) if 0 <= i + by < count]
    return lax.ppermute(shard, axis, pairs)


def times_transpose(left, weight):
    return lax.dot_general(
        left, weight, (((1,), (1,)), ((), ())), preferred_element_type=jnp.float32
    )


def doc_index(positions, ends):
    return jnp.sum((positions[:, None] >= ends[None, :]).astype(jnp.int32), axis=1)


def allowed(qpos, kpos, ends):
    diff = qpos[:, None] - kpos[None, :]
    same = doc_index(qpos, ends)[:, None] == doc_index(kpos, ends)[None, :]
    return (diff >= 0) & (diff < WINDOW) & (kpos[None, :] >= 0) & same


def tile_grads(qb, kb, vb, dab, mask):
    scale = HD ** (-0.5)
    rows = qb.shape[0]
    cols = kb.shape[0]
    q = qb.reshape(rows, HEADS, HD)
    k = kb.reshape(cols, HEADS, HD)
    v = vb.reshape(cols, HEADS, HD)
    da = dab.reshape(rows, HEADS, HD)
    score = jnp.einsum("qhd,khd->hqk", q, k, preferred_element_type=jnp.float32) * scale
    score = jnp.where(mask[None], score, NEG)
    top = jnp.max(score, axis=2, keepdims=True)
    expo = jnp.where(mask[None], jnp.exp(score - top), 0.0)
    total = jnp.sum(expo, axis=2, keepdims=True)
    prob = expo / total
    lowprob = prob.astype(jnp.bfloat16)
    attn = jnp.einsum("hqk,khd->qhd", lowprob, v, preferred_element_type=jnp.float32)
    delta = jnp.sum(attn * da.astype(jnp.float32), axis=2)
    dprob = jnp.einsum("qhd,khd->hqk", da, v, preferred_element_type=jnp.float32)
    dscore = (prob * (dprob - jnp.transpose(delta)[:, :, None]) * scale).astype(jnp.bfloat16)
    grad_q = jnp.einsum("hqk,khd->qhd", dscore, k, preferred_element_type=jnp.float32)
    grad_k = jnp.einsum("hqk,qhd->khd", dscore, q, preferred_element_type=jnp.float32)
    grad_v = jnp.einsum("hqk,qhd->khd", lowprob, da, preferred_element_type=jnp.float32)
    return (grad_q.reshape(rows, -1), grad_k.reshape(cols, -1), grad_v.reshape(cols, -1))


def collect(pieces):
    rows, labels = pieces
    number = rows.shape[0]
    rows = rows.reshape(number, -1, rows.shape[-1])
    labels = labels.reshape(number, -1)

    def one_table(part_rows, part_labels):
        empty = jnp.zeros((ROWS_DEV, part_rows.shape[-1]), jnp.float32)
        return empty.at[part_labels].add(part_rows.astype(jnp.float32), mode="drop")

    return jax.vmap(one_table)(rows, labels)


def slot_places(owner, devices, capacity, active):
    onehot = (
        (owner[:, :, None] == jnp.arange(devices, dtype=jnp.int32)[None, None, :])
        & active[:, :, None]
    ).astype(jnp.int32)
    place = jnp.sum(jnp.cumsum(onehot, axis=1) * onehot, axis=2) - 1
    return jnp.where(active, owner * capacity + place, devices * capacity)


def shards(
    hidden,
    gain,
    queries,
    keys,
    values,
    w_query,
    w_key,
    w_value,
    w_out,
    grad_out,
    doc_lengths,
    hash_ids,
):
    count = hidden.shape[0]
    width = hidden.shape[1]
    seq_size = lax.axis_size("seq")
    table_size = lax.axis_size("table")
    devices = seq_size * table_size
    first = lax.axis_index(("seq", "table")) * count
    ends = jnp.cumsum(doc_lengths)
    prev_keys, prev_values = shifted((keys, values), ("seq", "table"), 1)
    grad_attn = times_transpose(grad_out, w_out).astype(jnp.bfloat16)
    ext_keys = jnp.concatenate([prev_keys, keys], axis=0)
    ext_values = jnp.concatenate([prev_values, values], axis=0)
    block = min(512, count)
    dk_ext = jnp.zeros((count + WINDOW, width), jnp.float32)
    dv_ext = jnp.zeros((count + WINDOW, width), jnp.float32)
    qpos = first + 0 + jnp.arange(block, dtype=jnp.int32)
    kpos = first + 0 - WINDOW + jnp.arange(block + WINDOW, dtype=jnp.int32)
    grad_q, grad_k, grad_v = tile_grads(
        queries, ext_keys, ext_values, grad_attn, allowed(qpos, kpos, ends)
    )
    dq_parts = grad_q.astype(jnp.bfloat16)
    dk_ext = dk_ext.at[0 : block + WINDOW].add(grad_k)
    dv_ext = dv_ext.at[0 : block + WINDOW].add(grad_v)
    back_keys, back_values = shifted((dk_ext[:WINDOW], dv_ext[:WINDOW]), ("seq", "table"), -1)
    grad_k16 = dk_ext[WINDOW:].at[count - WINDOW :].add(back_keys).astype(jnp.bfloat16)
    grad_v16 = dv_ext[WINDOW:].at[count - WINDOW :].add(back_values).astype(jnp.bfloat16)
    grad_norm = (
        times_transpose(dq_parts, w_query)
        + times_transpose(grad_k16, w_key)
        + times_transpose(grad_v16, w_value)
    )
    full = hidden.astype(jnp.float32)
    inverse = lax.rsqrt(jnp.mean(full * full, axis=1, keepdims=True) + EPS)
    unit = full * inverse
    scaled = grad_norm * gain[None, :]
    through = inverse * (scaled - unit * jnp.mean(scaled * unit, axis=1, keepdims=True))
    grad_hidden = (grad_out.astype(jnp.float32) + through).astype(jnp.bfloat16)
    owner = hash_ids // ROWS_DEV
    local_row = hash_ids - owner * ROWS_DEV
    capacity = HOT + (count - HOT + devices - 1) // devices
    slot = slot_places(owner, devices, capacity, jnp.ones(owner.shape, bool))

    def fill(slot_row, row_ids):
        sent_rows = (
            jnp.zeros((devices * capacity, width), jnp.bfloat16).at[slot_row].set(grad_hidden)
        )
        sent_labels = jnp.full((devices * capacity,), ROWS_DEV, jnp.int32).at[slot_row].set(row_ids)
        return (sent_rows, sent_labels)

    sent_rows, sent_labels = jax.vmap(fill)(slot, local_row)
    tables = collect(
        (
            lax.all_to_all(
                sent_rows.reshape(NG, devices, capacity, width),
                ("seq", "table"),
                split_axis=1,
                concat_axis=1,
                tiled=True,
            ),
            lax.all_to_all(
                sent_labels.reshape(NG, devices, capacity),
                ("seq", "table"),
                split_axis=1,
                concat_axis=1,
                tiled=True,
            ),
        )
    )
    return (grad_hidden, tables.astype(jnp.bfloat16))


def solution(mesh):
    return jax.shard_map(
        shards,
        mesh=mesh,
        in_specs=(
            P(("seq", "table"), None),
            P(),
            P(("seq", "table"), None),
            P(("seq", "table"), None),
            P(("seq", "table"), None),
            P(),
            P(),
            P(),
            P(),
            P(("seq", "table"), None),
            P(),
            P(None, ("seq", "table")),
        ),
        out_specs=(P(("seq", "table"), None), P(None, ("seq", "table"), None)),
        check_vma=False,
    )
```

profile of v0, /device:TPU:1, one launch (start us, length us, event | category | flops | bytes accessed | tf_op | source)
XLA Modules:
  0.0 384.8 jit_solution(10300802499978751166)
XLA Ops:
  0.6 0.8 subtract_bitcast_fusion
  1.6 0.4 fusion.27
  2.9 0.6 copy-done.12
  3.5 4.3 %scatter_custom_fusion = s32[5120]{0:T(1024)S(1)} fusion(s32[1024]{0:T(1024)S(1)} %bitcast.96, s32[1024]{0:T(1024)S(1)} %bitcast.98, s32[]{:T(128)} %constant.201.clone.1), kind=kCustom, calls=%fused_computation.63 | custom fusion | bytes 20484
  8.0 0.8 copy.84
  8.8 12.0 %all-to-all-start = ((s32[2,128,20]{2,0,1:T(2,128)}), s32[2,128,20]{2,0,1:T(2,128)}, u32[]{:S(2)}, u32[]{:S(2)}) async-start(s32[2,128,20]{2,0,1:T(2,128)} %copy.84), calls=%async_computation | async-start | bytes 262144 | tf_op jit(solution)/shard_map/all_to_all | solution.py:159
  20.7 3.5 collective-permute-start
  24.3 2.1 collective-permute-start.1
  27.0 3.0 convolution_convert_fusion
  30.4 1.4 copy.75
  31.9 1.2 fusion.12
  33.5 2.6 pad_maximum_fusion
  36.1 2.6 copy.72
  38.7 3.2 collective-permute-done.1
  41.9 2.6 pad_maximum_fusion.1
  44.5 2.6 copy.76
  47.1 16.8 %fusion.37 = (f32[12,512]{1,0:T(8,128)S(1)}, f32[12,512,1024]{1,2,0:T(8,128)}) fusion(pred[512,1024]{0,1:T(8,128)(4,1)S(1)} %fusion.12, bf16[1024,12,64]{0,2,1:T(8,128)(2,1)} %bitcast.85, bf16[512,12,64]{0,2,1:T(8,128)(2,1)S(1)} %bitcast.90), kind=kOutput, calls=%fused_computation.85 | convolution fusion | flops 836764672 | bytes 28073984 | tf_op jit(solution)/shard_map/sub | solution.py:51
  64.0 9.6 %fusion.5 = bf16[12,512,1024]{1,2,0:T(8,128)(2,1)S(1)} fusion(f32[12,512,1024]{1,2,0:T(8,128)} %get-tuple-element.89, f32[12,512]{1,0:T(8,128)S(1)} %get-tuple-element.88), kind=kLoop, calls=%fused_computation.12 | loop fusion | flops 12582912 | bytes 37773312 | tf_op jit(solution)/shard_map/convert_element_type | solution.py:54
  73.6 2.2 fusion.25
  75.8 2.4 copy-done.1
  78.1 14.3 %multiply_convert_fusion = bf16[12,512,1024]{1,2,0:T(8,128)(2,1)} fusion(f32[12,512]{1,0:T(8,128)S(1)} %bitcast.95, f32[12,512,1024]{1,2,0:T(8,128)} %get-tuple-element.89, f32[12,512]{1,0:T(8,128)S(1)} %get-tuple-element.88, bf16[512,12,64]{0,2,1:T(8,128)(2,1)S(1)} %bitcast.83, bf16[1024,12,64]{0,2,1:T(8,128)(2,1)} %bitcast.87), kind=kOutput, calls=%fused_computation.5 | convolution fusion | flops 836763648 | bytes 40157184 | tf_op jit(solution)/shard_map/qhd,khd->hqk/dot_general | solution.py:57
  92.4 10.1 %convolution_bitcast_fusion.1 = f32[1024,12,64]{0,2,1:T(8,128)} fusion(bf16[12,512,1024]{1,2,0:T(8,128)(2,1)} %multiply_convert_fusion, bf16[512,12,64]{0,2,1:T(8,128)(2,1)S(1)} %bitcast.91), kind=kOutput, calls=%fused_computation.26 | convolution fusion | flops 805306368 | bytes 16515072 | tf_op jit(solution)/shard_map/hqk,qhd->khd/dot_general | solution.py:60
  102.5 4.2 %fusion.36 = (f32[512,12,64]{0,2,1:T(8,128)}, f32[512,12,64]{0,2,1:T(8,128)}) fusion(f32[1024,12,64]{0,2,1:T(8,128)} %convolution_bitcast_fusion.1), kind=kLoop, calls=%fused_computation.84 | loop fusion | bytes 6291456 | tf_op jit(solution)/shard_map/slice | solution.py:124
  106.7 2.3 collective-permute-start.2
  109.0 10.3 %convolution_bitcast_fusion = f32[1024,12,64]{0,2,1:T(8,128)} fusion(bf16[512,12,64]{0,2,1:T(8,128)(2,1)S(1)} %bitcast.84, bf16[12,512,1024]{1,2,0:T(8,128)(2,1)} %copy-done.1), kind=kOutput, calls=%fused_computation.25 | convolution fusion | flops 805306368 | bytes 16515072 | tf_op jit(solution)/shard_map/hqk,qhd->khd/dot_general | solution.py:61
  119.3 2.4 fusion.35
  121.6 2.1 collective-permute-start.3
  123.7 2.2 convolution_convert_fusion.1
  125.9 0.8 fusion.38
  126.8 3.1 collective-permute-done.2
  129.9 1.7 fusion.24
  131.6 0.8 fusion.39
  132.5 14.2 %collective-permute-done.3 = f32[512,768]{0,1:T(8,128)S(1)} collective-permute-done((f32[512,768]{0,1:T(8,128)S(1)}, f32[512,768]{0,1:T(8,128)S(1)}, u32[]{:S(2)}, u32[]{:S(2)}) %collective-permute-start.3) | collective-permute-done | bytes 1572896 | tf_op jit(solution)/shard_map/ppermute | solution.py:21
  146.6 0.4 fusion.23
  147.0 0.7 copy-done.5
  147.8 1.2 fusion.17
  148.9 0.5 fusion.21
  149.5 10.3 %scatter_custom_fusion.1 = bf16[5120,768]{1,0:T(8,128)(2,1)} fusion(s32[1024]{0:T(1024)} %bitcast.97, bf16[1024,768]{1,0:T(8,128)(2,1)S(1)} %bitcast.92, bf16[]{:T(256)} %constant.208.clone.1), kind=kCustom, calls=%fused_computation.16 | custom fusion | bytes 7864832
  159.8 12.4 %reshape.315 = bf16[2,128,20,768]{3,2,1,0:T(8,128)(2,1)} reshape(bf16[5120,768]{1,0:T(8,128)(2,1)} %scatter_custom_fusion.1) | data formatting | bytes 15728640 | tf_op jit(solution)/shard_map/reshape | solution.py:153
  172.3 12.8 %copy.86 = bf16[2,128,20,768]{3,0,2,1:T(2,128)(2,1)} copy(bf16[2,128,20,768]{3,2,1,0:T(8,128)(2,1)} %reshape.315) | data formatting | bytes 15728640 | tf_op jit(solution)/shard_map/reshape | solution.py:153
  185.1 13.5 %all-to-all-start.1 = ((bf16[2,128,20,768]{3,0,2,1:T(2,128)(2,1)}), bf16[2,128,20,768]{3,0,2,1:T(2,128)(2,1)}, u32[]{:S(2)}, u32[]{:S(2)}) async-start(bf16[2,128,20,768]{3,0,2,1:T(2,128)(2,1)} %copy.86), calls=%async_computation.1 | async-start | bytes 15728640 | tf_op jit(solution)/shard_map/all_to_all | solution.py:152
  198.7 0.9 copy.85
  200.0 91.0 %all-to-all-done.1 = bf16[2,128,20,768]{3,0,2,1:T(2,128)(2,1)} async-done(((bf16[2,128,20,768]{3,0,2,1:T(2,128)(2,1)}), bf16[2,128,20,768]{3,0,2,1:T(2,128)(2,1)}, u32[]{:S(2)}, u32[]{:S(2)}) %all-to-all-start.1) | async-done | bytes 7864352 | tf_op jit(solution)/shard_map/all_to_all | solution.py:152
  291.0 10.8 %copy_convert_fusion = f32[2,128,20,768]{3,1,2,0:T(8,128)} fusion(bf16[2,128,20,768]{3,0,2,1:T(2,128)(2,1)} %all-to-all-done.1), kind=kLoop, calls=%fused_computation.13 | loop fusion | flops 3932160 | bytes 23592960 | tf_op jit(solution)/shard_map/vmap()/convert_element_type | solution.py:73
  301.7 18.0 %copy.88 = f32[2,128,20,768]{3,2,1,0:T(8,128)} copy(f32[2,128,20,768]{3,1,2,0:T(8,128)} %copy_convert_fusion) | data formatting | bytes 31457280 | tf_op jit(solution)/shard_map/vmap()/convert_element_type | solution.py:73
  319.7 17.7 %reshape.346 = f32[5120,768]{1,0:T(8,128)} reshape(f32[2,128,20,768]{3,2,1,0:T(8,128)} %copy.88) | data formatting | bytes 31457280 | tf_op jit(solution)/shard_map/vmap()/convert_element_type | solution.py:73
  337.4 39.4 %scatter_custom_fusion.2 = f32[4096,768]{1,0:T(8,128)} fusion(s32[5120]{0:T(1024)S(1)} %reshape.344, f32[5120,768]{1,0:T(8,128)} %reshape.346, f32[]{:T(128)} %constant.188.clone.1), kind=kCustom, calls=%fused_computation.14 | custom fusion | flops 3932160 | bytes 12583424
  376.8 7.9 %convert_element_type.75 = bf16[4096,768]{1,0:T(8,128)(2,1)} convert(f32[4096,768]{1,0:T(8,128)} %scatter_custom_fusion.2) | non-fusion elementwise | flops 3145728 | bytes 18874368 | tf_op jit(solution)/shard_map/convert_element_type | solution.py:168
  (82 shorter events, 3.0 us)
Async XLA Ops:
  0.6 146.4 %copy-start = (bf16[768,768]{1,0:T(8,128)(2,1)S(1)}, bf16[768,768]{1,0:T(8,128)(2,1)}, u32[]{:S(2)}) copy-start(bf16[768,768]{1,0:T(8,128)(2,1)} %param.35) | copy-start | bytes 3538948
  1.6 1.1 copy-start.17
  1.6 1.2 copy-start.16
  2.1 24.2 %copy-start.4 = (bf16[512,768]{1,0:T(8,128)(2,1)S(1)}, bf16[512,768]{1,0:T(8,128)(2,1)}, u32[]{:S(2)}) copy-start(bf16[512,768]{1,0:T(8,128)(2,1)} %param.28) | copy-start | bytes 2359300
  2.2 24.4 %copy-start.13 = (s32[64]{0:T(128)S(1)}, s32[64]{0:T(128)}, u32[]{:S(2)}) copy-start(s32[64]{0:T(128)} %param.38) | copy-start | bytes 772
  2.3 24.8 %copy-start.9 = (bf16[512,768]{1,0:T(8,128)(2,1)S(1)}, bf16[512,768]{1,0:T(8,128)(2,1)}, u32[]{:S(2)}) copy-start(bf16[512,768]{1,0:T(8,128)(2,1)} %param.37) | copy-start | bytes 2359300
  2.9 0.6 copy-start.12
  8.8 176.4 %all-to-all-start = ((s32[2,128,20]{2,0,1:T(2,128)}), s32[2,128,20]{2,0,1:T(2,128)}, u32[]{:S(2)}, u32[]{:S(2)}) async-start(s32[2,128,20]{2,0,1:T(2,128)} %copy.84), calls=%async_computation | async-start | bytes 262144 | tf_op jit(solution)/shard_map/all_to_all | solution.py:159
  20.7 12.8 %collective-permute-start = (bf16[512,768]{1,0:T(8,128)(2,1)}, bf16[512,768]{1,0:T(8,128)(2,1)}, u32[]{:S(2)}, u32[]{:S(2)}) collective-permute-start(bf16[512,768]{1,0:T(8,128)(2,1)} %param.31), channel_id=1, source_target_pairs={{0,1},{1,2},{2,3},{3,4},{4,5},{5,6},{6,7},{7,8},{8,9},{9,10},{10,1... | collective-permute-start | bytes 2359304 | tf_op jit(solution)/shard_map/ppermute | solution.py:21
  24.3 17.7 %collective-permute-start.1 = (bf16[512,768]{1,0:T(8,128)(2,1)}, bf16[512,768]{1,0:T(8,128)(2,1)}, u32[]{:S(2)}, u32[]{:S(2)}) collective-permute-start(bf16[512,768]{1,0:T(8,128)(2,1)} %param.32), channel_id=1, source_target_pairs={{0,1},{1,2},{2,3},{3,4},{4,5},{5,6},{6,7},{7,8},{8,9},{9,10},{10,1... | collective-permute-start | bytes 2359304 | tf_op jit(solution)/shard_map/ppermute | solution.py:21
  27.0 3.1 copy-start.8
  64.0 9.6 %copy-start.3 = (bf16[1024,768]{0,1:T(8,128)(2,1)S(1)}, bf16[1024,768]{0,1:T(8,128)(2,1)}, u32[]{:S(2)}) copy-start(bf16[1024,768]{0,1:T(8,128)(2,1)} %copy.76) | copy-start | bytes 4718596
  73.5 4.6 %copy-start.1 = (bf16[12,512,1024]{1,2,0:T(8,128)(2,1)}, bf16[12,512,1024]{1,2,0:T(8,128)(2,1)S(1)}, u32[]{:S(2)}) copy-start(bf16[12,512,1024]{1,2,0:T(8,128)(2,1)S(1)} %fusion.5) | copy-start | bytes 37748740
  102.5 21.2 %slice-start = ((s8[12582912]{0:T(1024)(128)(4,1)}), s8[4194304]{0:T(1024)(128)(4,1)S(1)}, s32[]{:S(2)}) async-start(s8[12582912]{0:T(1024)(128)(4,1)} %bitcast.80), calls=%async_computation.2 | async-start | bytes 8388608
  106.7 17.0 %slice-start.1 = ((s8[12582912]{0:T(1024)(128)(4,1)}), s8[4194304]{0:T(1024)(128)(4,1)S(1)}, s32[]{:S(2)}) async-start(s8[12582912]{0:T(1024)(128)(4,1)} %bitcast.80), calls=%async_computation.3 | async-start | bytes 8388608
  106.7 17.0 %slice-start.2 = ((s8[12582912]{0:T(1024)(128)(4,1)}), s8[4194304]{0:T(1024)(128)(4,1)S(1)}, s32[]{:S(2)}) async-start(s8[12582912]{0:T(1024)(128)(4,1)} %bitcast.80), calls=%async_computation.4 | async-start | bytes 8388608
  106.7 23.2 %collective-permute-start.2 = (f32[512,768]{0,1:T(8,128)}, f32[512,768]{0,1:T(8,128)}, u32[]{:S(2)}, u32[]{:S(2)}) collective-permute-start(f32[512,768]{0,1:T(8,128)} %bitcast.12), channel_id=1, source_target_pairs={{1,0},{2,1},{3,2},{4,3},{5,4},{6,5},{7,6},{8,7},{9,8},{10,9},{11,1... | collective-permute-start | bytes 4718600 | tf_op jit(solution)/shard_map/ppermute | solution.py:21
  119.3 4.5 %copy-start.2 = (bf16[1024,768]{0,1:T(8,128)(2,1)S(1)}, bf16[1024,768]{0,1:T(8,128)(2,1)}, u32[]{:S(2)}) copy-start(bf16[1024,768]{0,1:T(8,128)(2,1)} %copy.72) | copy-start | bytes 4718596
  121.6 4.3 %copy-start.18 = (bf16[768,768]{1,0:T(8,128)(2,1)S(1)}, bf16[768,768]{1,0:T(8,128)(2,1)}, u32[]{:S(2)}) copy-start(bf16[768,768]{1,0:T(8,128)(2,1)} %param.33) | copy-start | bytes 3538948
  121.6 25.0 %collective-permute-start.3 = (f32[512,768]{0,1:T(8,128)S(1)}, f32[512,768]{0,1:T(8,128)S(1)}, u32[]{:S(2)}, u32[]{:S(2)}) collective-permute-start(f32[512,768]{0,1:T(8,128)S(1)} %bitcast.93), channel_id=1, source_target_pairs={{1,0},{2,1},{3,2},{4,3},{5,4},{6,5},{7,6},{8,7},{9,8},{10,9},{11,1... | collective-permute-start | bytes 4718600 | tf_op jit(solution)/shard_map/ppermute | solution.py:21
  125.9 4.0 %copy-start.6 = (f32[512,12,64]{0,2,1:T(8,128)S(1)}, f32[512,12,64]{0,2,1:T(8,128)}, u32[]{:S(2)}) copy-start(f32[512,12,64]{0,2,1:T(8,128)} %get-tuple-element.86) | copy-start | bytes 4718596
  129.9 1.7 copy-start.19
  146.6 1.1 copy-start.5
  146.6 1.1 copy-start.11
  147.8 1.2 copy-start.10
  149.4 10.4 %copy-start.7 = (bf16[512,768]{1,0:T(8,128)(2,1)}, bf16[512,768]{1,0:T(8,128)(2,1)S(1)}, u32[]{:S(2)}) copy-start(bf16[512,768]{1,0:T(8,128)(2,1)S(1)} %fusion.21) | copy-start | bytes 2359300
  185.1 14.6 %copy-start.15 = (s32[2]{0:T(128)S(1)}, s32[2]{0:T(128)}, u32[]{:S(2)}) copy-start(s32[2]{0:T(128)} %constant.221) | copy-start | bytes 28
  185.1 14.7 %copy-start.14 = (s32[2]{0:T(128)S(1)}, s32[2]{0:T(128)}, u32[]{:S(2)}) copy-start(s32[2]{0:T(128)} %constant.224) | copy-start | bytes 28
  185.1 105.8 %all-to-all-start.1 = ((bf16[2,128,20,768]{3,0,2,1:T(2,128)(2,1)}), bf16[2,128,20,768]{3,0,2,1:T(2,128)(2,1)}, u32[]{:S(2)}, u32[]{:S(2)}) async-start(bf16[2,128,20,768]{3,0,2,1:T(2,128)(2,1)} %copy.86), calls=%async_computation.1 | async-start | bytes 15728640 | tf_op jit(solution)/shard_map/all_to_all | solution.py:152
where the time goes:
time: 391 us; the launch traced here: 385 us
  waiting for transfers between devices  112 us (29%)
  local copies, waits for them, and re-layouts  95.1 us (24%)
  other arithmetic  79.4 us (20%)
  matrix products  61.7 us (16%)
  starting transfers between devices  35.4 us (9%)
    all_to_all x1, waiting for transfers between devices, shards(): lax.all_to_all(sent_rows.reshape(NG, devices, capacity, width), ('seq', '...  91 us
    unnamed x9, other arithmetic  40.6 us
    convert_element_type x2, local copies, waits for them, and re-layouts, one_table(): return empty.at[part_labels].add(part_rows.astype(jnp.float32), mode='drop')  35.6 us
    reshape x2, local copies, waits for them, and re-layouts, shards(): sent_rows.reshape(NG, devices, capacity, width)  25.3 us
    ppermute x4, waiting for transfers between devices, shifted(): return lax.ppermute(shard, axis, pairs)  20.8 us
    unnamed x54, local copies, waits for them, and re-layouts  18.7 us
    sub x1, matrix products, tile_grads(): expo = jnp.where(mask[None], jnp.exp(score - top), 0.0)  16.8 us
    dot_general x1, matrix products, tile_grads(): jnp.einsum('qhd,khd->hqk', da, v, preferred_element_type=jnp.float32)  14.3 us
  transfers between devices with their start and end apart: 6, of which 5 were waited for; matrix products, arithmetic and copies ran while one was open for 34% of the time, Pallas kernels for 0%

commit v1 on v0

v1 whole, which is shorter than its diff:
```python
import functools

import jax
import jax.numpy as jnp
from jax import lax
from jax.experimental import pallas as pl
from jax.experimental.pallas import tpu as pltpu
from jax.sharding import PartitionSpec as P

HD = 64
WINDOW = 512
NG = 2
ROWS_DEV = 2048
SLOTS = 5
EPS = 1e-06
NEG = -1e30
AXES = ("seq", "table")
LANES = 128
BF16 = jnp.bfloat16
F32 = jnp.float32
I32 = jnp.int32
VMEM_BYTES = 56 * 1024 * 1024


def iota(shape, dim):
    return lax.broadcasted_iota(I32, shape, dim)


def dot(left, right, left_dim, right_dim):
    return lax.dot_general(
        left, right, (((left_dim,), (right_dim,)), ((), ())), preferred_element_type=F32
    )


def params():
    return pltpu.CompilerParams(vmem_limit_bytes=VMEM_BYTES)


def shifted(shard, by):
    count = lax.axis_size(AXES)
    pairs = [(i, i + by) for i in range(count) if 0 <= i + by < count]
    return lax.ppermute(shard, AXES, pairs)


def slots_kernel(row_ref, col_ref, slot_ref, label_ref):
    count = row_ref.shape[1]
    places = label_ref.shape[1]
    labels = jnp.full((1, places), ROWS_DEV, I32)
    sub = iota((count, count), 0)
    lane = iota((count, count), 1)
    for table in range(NG):
        row = row_ref[table : table + 1, :]
        col = col_ref[:, table : table + 1]
        same = col == row
        first_col = jnp.sum((same & (lane < sub)).astype(I32), axis=1, keepdims=True) == 0
        first_row = jnp.sum((same & (sub < lane)).astype(I32), axis=0, keepdims=True) == 0
        row_owner = row // ROWS_DEV
        col_owner = col // ROWS_DEV
        mates = row_owner == col_owner
        place_row = jnp.sum((first_col & mates & (col < row)).astype(I32), axis=0, keepdims=True)
        place_col = jnp.sum((first_row & mates & (row < col)).astype(I32), axis=1, keepdims=True)
        base = table * SLOTS
        slot_ref[table : table + 1, :] = row_owner * (NG * SLOTS) + base + place_row
        slot_col = col_owner * (NG * SLOTS) + base + place_col
        local_col = col - col_owner * ROWS_DEV
        hit = slot_col == iota((count, places), 1)
        labels = jnp.minimum(
            labels, jnp.min(jnp.where(hit, local_col, ROWS_DEV), axis=0, keepdims=True)
        )
    label_ref[...] = labels


def make_slots(hash_ids, devices):
    count = hash_ids.shape[1]
    places = devices * NG * SLOTS
    return pl.pallas_call(
        slots_kernel,
        out_shape=(
            jax.ShapeDtypeStruct((NG, count), I32),
            jax.ShapeDtypeStruct((1, places), I32),
        ),
        compiler_params=params(),
        name="slots",
    )(hash_ids, jnp.transpose(hash_ids))


QT = 256
KT = QT + WINDOW


def attention_kernel(
    first_ref, len_ref, q_ref, kp_ref, ko_ref, vp_ref, vo_ref, da_ref,
    dq_ref, dkp_ref, dvp_ref, dko_ref, dvo_ref,
    bias_ref, kx_ref, vx_ref, dk_ref, dv_ref,
):
    count = q_ref.shape[0]
    tiles = count // QT

    @pl.when(pl.program_id(0) == 0)
    def _():
        docs = len_ref.shape[1]
        first = first_ref[0]
        upto = iota((docs, docs), 1) <= iota((docs, docs), 0)
        ends = jnp.sum(jnp.where(upto, len_ref[...], 0), axis=1, keepdims=True)
        qpos = first + iota((1, count), 1)
        start = jnp.max(jnp.where(ends <= qpos, ends, 0), axis=0, keepdims=True)
        low = jnp.maximum(start, qpos - (WINDOW - 1))
        for tile in range(tiles):
            cols = slice(tile * QT, (tile + 1) * QT)
            kpos = first - WINDOW + tile * QT + iota((KT, QT), 0)
            ok = (kpos >= low[:, cols]) & (kpos <= qpos[:, cols])
            bias_ref[tile] = jnp.where(ok, 0.0, NEG)

    kx_ref[:WINDOW] = kp_ref[...]
    kx_ref[WINDOW:] = ko_ref[...]
    vx_ref[:WINDOW] = vp_ref[...]
    vx_ref[WINDOW:] = vo_ref[...]
    lane = iota((QT, LANES), 1)
    scale = HD ** (-0.5)
    zero = jnp.zeros((QT, LANES), BF16)
    for tile in range(tiles):
        rows = slice(tile * QT, (tile + 1) * QT)
        span = slice(tile * QT, tile * QT + KT)
        q = q_ref[rows, :] * jnp.asarray(scale, BF16)
        da = da_ref[rows, :]
        k = kx_ref[span, :]
        v = vx_ref[span, :]
        dq = dk = dv = None
        for half in range(LANES // HD):
            mine = (lane // HD) == half
            qh = jnp.where(mine, q, zero)
            dah = jnp.where(mine, da, zero)
            score = dot(k, qh, 1, 1) + bias_ref[tile]
            top = jnp.max(score, axis=0, keepdims=True)
            expo = jnp.exp(score - top)
            total = jnp.sum(expo, axis=0, keepdims=True)
            prob = expo * (1.0 / total)
            lowprob = prob.astype(BF16)
            dprob = dot(v, dah, 1, 1)
            delta = jnp.sum(lowprob.astype(F32) * dprob, axis=0, keepdims=True)
            dscore = (prob * (dprob - delta)).astype(BF16)
            dvh = dot(lowprob, dah, 1, 0)
            dkh = dot(dscore, qh, 1, 0)
            dqh = jnp.where(mine, dot(dscore, k, 0, 0), 0.0)
            dv = dvh if dv is None else dv + dvh
            dk = dkh if dk is None else dk + dkh
            dq = dqh if dq is None else dq + dqh
        dq_ref[rows, :] = (dq * scale).astype(BF16)
        if tile == 0:
            dk_ref[span, :] = dk
            dv_ref[span, :] = dv
        else:
            seen = slice(tile * QT, (tile - 1) * QT + KT)
            fresh = slice((tile - 1) * QT + KT, tile * QT + KT)
            both = KT - QT
            dk_ref[seen, :] += dk[:both]
            dv_ref[seen, :] += dv[:both]
            dk_ref[fresh, :] = dk[both:]
            dv_ref[fresh, :] = dv[both:]
    dkp_ref[...] = dk_ref[:WINDOW].astype(BF16)
    dvp_ref[...] = dv_ref[:WINDOW].astype(BF16)
    dko_ref[...] = dk_ref[WINDOW:]
    dvo_ref[...] = dv_ref[WINDOW:]


def attention_grads(first, doc_lengths, queries, prev_keys, keys, prev_values, values, grad_attn):
    count, width = queries.shape
    pairs = width // LANES
    ext = count + WINDOW
    tiles = count // QT
    column = lambda n: pl.BlockSpec((n, LANES), lambda i: (0, i))
    docs = doc_lengths.shape[0]
    return pl.pallas_call(
        attention_kernel,
        grid=(pairs,),
        in_specs=[
            pl.BlockSpec(memory_space=pltpu.SMEM),
            pl.BlockSpec((1, docs), lambda i: (0, 0)),
            column(count), column(WINDOW), column(count), column(WINDOW), column(count), column(count),
        ],
        out_specs=[column(count), column(WINDOW), column(WINDOW), column(count), column(count)],
        out_shape=[
            jax.ShapeDtypeStruct((count, width), BF16),
            jax.ShapeDtypeStruct((WINDOW, width), BF16),
            jax.ShapeDtypeStruct((WINDOW, width), BF16),
            jax.ShapeDtypeStruct((count, width), F32),
            jax.ShapeDtypeStruct((count, width), F32),
        ],
        scratch_shapes=[
            pltpu.VMEM((tiles, KT, QT), F32),
            pltpu.VMEM((ext, LANES), BF16),
            pltpu.VMEM((ext, LANES), BF16),
            pltpu.VMEM((ext, LANES), F32),
            pltpu.VMEM((ext, LANES), F32),
        ],
        compiler_params=params(),
        cost_estimate=pl.CostEstimate(
            flops=10 * count * KT * width, bytes_accessed=20 * count * width,
            transcendentals=count * KT * width // HD,
        ),
        name="attention",
    )(first, doc_lengths.reshape(1, docs), queries, prev_keys, keys, prev_values, values, grad_attn)


PACK = 256


def finish_kernel(
    dq_ref, dk_ref, dv_ref, bk_ref, bv_ref, wq_ref, wk_ref, wv_ref,
    hidden_ref, gain_ref, out_ref, slot_ref, gh_ref, sent_ref,
):
    count = hidden_ref.shape[0]
    grad_k = (dk_ref[...] + bk_ref[...].astype(F32)).astype(BF16)
    grad_v = (dv_ref[...] + bv_ref[...].astype(F32)).astype(BF16)
    norm = dot(dq_ref[...], wq_ref[...], 1, 1)
    norm = norm + dot(grad_k, wk_ref[...], 1, 1)
    norm = norm + dot(grad_v, wv_ref[...], 1, 1)
    full = hidden_ref[...].astype(F32)
    inverse = lax.rsqrt(jnp.mean(full * full, axis=1, keepdims=True) + EPS)
    unit = full * inverse
    scaled = norm * gain_ref[...]
    through = inverse * (scaled - unit * jnp.mean(scaled * unit, axis=1, keepdims=True))
    grad_hidden = (out_ref[...].astype(F32) + through).astype(BF16)
    gh_ref[...] = grad_hidden
    slots = sent_ref.shape[0]
    for at in range(0, slots, PACK):
        place = at + iota((PACK, count), 0)
        hit = place == slot_ref[0:1, :]
        for table in range(1, NG):
            hit = hit | (place == slot_ref[table : table + 1, :])
        sent_ref[at : at + PACK, :] = dot(
            jnp.where(hit, 1.0, 0.0).astype(BF16), grad_hidden, 1, 0
        ).astype(BF16)


def finish(dq, dk, dv, bk, bv, wq, wk, wv, hidden, gain, grad_out, slot, devices):
    count, width = hidden.shape
    places = devices * NG * SLOTS
    return pl.pallas_call(
        finish_kernel,
        out_shape=(
            jax.ShapeDtypeStruct((count, width), BF16),
            jax.ShapeDtypeStruct((places, width), BF16),
        ),
        compiler_params=params(),
        name="finish",
    )(dq, dk, dv, bk, bv, wq, wk, wv, hidden, gain.reshape(1, width), grad_out, slot)


COLLECT = 512


def collect_kernel(label_ref, rows_ref, out_ref):
    place = pl.program_id(1) * COLLECT + iota((COLLECT, label_ref.shape[2]), 0)
    hit = jnp.where(place == label_ref[0], 1.0, 0.0).astype(BF16)
    out_ref[0] = dot(hit, rows_ref[0], 1, 0).astype(BF16)


def collect(labels, rows):
    tables, number, width = rows.shape
    return pl.pallas_call(
        collect_kernel,
        grid=(tables, ROWS_DEV // COLLECT),
        in_specs=[
            pl.BlockSpec((1, 1, number), lambda t, i: (t, 0, 0)),
            pl.BlockSpec((1, number, width), lambda t, i: (t, 0, 0)),
        ],
        out_specs=pl.BlockSpec((1, COLLECT, width), lambda t, i: (t, i, 0)),
        out_shape=jax.ShapeDtypeStruct((tables, ROWS_DEV, width), BF16),
        compiler_params=params(),
        name="collect",
    )(labels, rows)


def exchanged(part):
    return lax.all_to_all(part, AXES, split_axis=0, concat_axis=0, tiled=True)


def shards(
    hidden,
    gain,
    queries,
    keys,
    values,
    w_query,
    w_key,
    w_value,
    w_out,
    grad_out,
    doc_lengths,
    hash_ids,
):
    count, width = hidden.shape
    devices = lax.axis_size(AXES)
    first = (lax.axis_index(AXES) * count).astype(I32).reshape(1)
    prev_keys, prev_values = shifted((keys, values), 1)
    slot, labels = make_slots(hash_ids, devices)
    labels = exchanged(labels.reshape(devices, NG, SLOTS))
    labels = jnp.transpose(labels, (1, 0, 2)).reshape(NG, 1, devices * SLOTS)
    grad_attn = dot(grad_out, w_out, 1, 1).astype(BF16)
    dq, dkp, dvp, dko, dvo = attention_grads(
        first, doc_lengths, queries, prev_keys, keys, prev_values, values, grad_attn
    )
    back_keys, back_values = shifted((dkp, dvp), -1)
    grad_hidden, sent = finish(
        dq, dko, dvo, back_keys, back_values, w_query, w_key, w_value,
        hidden, gain, grad_out, slot, devices,
    )
    rows = exchanged(sent.reshape(devices, NG, SLOTS, width))
    rows = jnp.transpose(rows, (1, 0, 2, 3)).reshape(NG, devices * SLOTS, width)
    return grad_hidden, collect(labels, rows)


def solution(mesh):
    spread = P(AXES, None)
    return jax.shard_map(
        shards,
        mesh=mesh,
        in_specs=(
            spread, P(), spread, spread, spread, P(), P(), P(), P(), spread, P(), P(None, AXES),
        ),
        out_specs=(spread, P(None, AXES, None)),
        check_vma=False,
    )
```

time: 391 us -> 150 us (0.38); the launches traced: 385 us -> 149 us
  local copies, waits for them, and re-layouts: 95.1 us -> 16.4 us
  other arithmetic: 79.4 us -> 0.71 us
  waiting for transfers between devices: 112 us -> 41.2 us
  matrix products: 61.7 us -> 2.85 us
  Pallas kernels: 0 us -> 51.2 us
    all_to_all x2, waiting for transfers between devices: 91 us -> 28.3 us  [exchanged(): return lax.all_to_all(part, AXES, split_axis=0, concat_axis=0, tiled=True)]
    pallas_call x0 -> x4, Pallas kernels: none -> 51.2 us  [the longest x1 27.4 us: attention_grads(): pl.pallas_call(attention_kernel, grid=(pairs,), in_specs=[pl.BlockSpec(me...]
    dot_general x9 -> x1, matrix products: 44.8 us -> 2.85 us  [dot(): lax.dot_general(left, right, (((left_dim,), (right_dim,)), ((), ())), pre...]
    unnamed x9 -> x0, other arithmetic: 40.6 us -> none
    convert_element_type x3 -> x0, local copies, waits for them, and re-layouts: 37.1 us -> none  [the longest x2 35.6 us: one_table(): return empty.at[part_labels].add(part_rows.astype(jnp.float32), mode='drop')]
    convert_element_type x6 -> x0, other arithmetic: 30.8 us -> none  [the longest x1 10.8 us: one_table(): return empty.at[part_labels].add(part_rows.astype(jnp.float32), mode='drop')]
    sub x1 -> x0, matrix products: 16.8 us -> none  [tile_grads(): expo = jnp.where(mask[None], jnp.exp(score - top), 0.0)]
    unnamed x54 -> x15, local copies, waits for them, and re-layouts: 18.7 us -> 2.92 us
  transfers between devices with their start and end apart: 6 -> 6, of which waited for: 5 -> 3; matrix products, arithmetic and copies ran while one was open for 34% -> 11% of each run, Pallas kernels for 0% -> 10%
where the time goes in v1:
time: 150 us; the launch traced here: 149 us
  Pallas kernels  51.2 us (34%)
  waiting for transfers between devices  41.2 us (27%)
  starting transfers between devices  36.3 us (24%)
  local copies, waits for them, and re-layouts  16.4 us (11%)
  matrix products  2.85 us (2%)
    all_to_all x2, waiting for transfers between devices, exchanged(): return lax.all_to_all(part, AXES, split_axis=0, concat_axis=0, tiled=True)  28.3 us
    pallas_call x1, Pallas kernels, attention_grads(): pl.pallas_call(attention_kernel, grid=(pairs,), in_specs=[pl.BlockSpec(me...  27.4 us
    all_to_all x2, starting transfers between devices, exchanged(): return lax.all_to_all(part, AXES, split_axis=0, concat_axis=0, tiled=True)  25.8 us
    ppermute x4, waiting for transfers between devices, shifted(): return lax.ppermute(shard, AXES, pairs)  12.9 us
    ppermute x4, starting transfers between devices, shifted(): return lax.ppermute(shard, AXES, pairs)  10.5 us
    pallas_call x1, Pallas kernels, finish(): pl.pallas_call(finish_kernel, out_shape=(jax.ShapeDtypeStruct((count, wid...  10.1 us
    reshape x2, local copies, waits for them, and re-layouts, shards(): rows = exchanged(sent.reshape(devices, NG, SLOTS, width))  9.62 us
    pallas_call x1, Pallas kernels, collect(): pl.pallas_call(collect_kernel, grid=(tables, ROWS_DEV // COLLECT), in_spe...  9.29 us
  transfers between devices with their start and end apart: 6, of which 3 were waited for; matrix products, arithmetic and copies ran while one was open for 11% of the time, Pallas kernels for 10%

profile of v1, /device:TPU:1, one launch (start us, length us, event | category | flops | bytes accessed | tf_op | source)
XLA Modules:
  0.0 149.3 jit_solution(10224121059445093498)
XLA Ops:
  0.6 0.0 copy-start
  0.6 4.7 %collective-permute-start = (bf16[512,768]{1,0:T(8,128)(2,1)}, bf16[512,768]{1,0:T(8,128)(2,1)S(1)}, u32[]{:S(2)}, u32[]{:S(2)}) collective-permute-start(bf16[512,768]{1,0:T(8,128)(2,1)} %ko_ref.1), channel_id=1, source_target_pairs={{0,1},{1,2},{2,3},{3,4},{4,5},{5,6},{6,7},{7,8},{8,9},{9,10},{10,1... | collective-permute-start | bytes 2359304 | tf_op jit(solution)/shard_map/ppermute | solution.py:42
  5.4 1.9 %collective-permute-start.1 = (bf16[512,768]{1,0:T(8,128)(2,1)}, bf16[512,768]{1,0:T(8,128)(2,1)S(1)}, u32[]{:S(2)}, u32[]{:S(2)}) collective-permute-start(bf16[512,768]{1,0:T(8,128)(2,1)} %vo_ref.1), channel_id=1, source_target_pairs={{0,1},{1,2},{2,3},{3,4},{4,5},{5,6},{6,7},{7,8},{8,9},{9,10},{10,1... | collective-permute-start | bytes 2359304 | tf_op jit(solution)/shard_map/ppermute | solution.py:42
  7.3 0.0 copy-done
  7.3 2.9 %convolution_convert_fusion.da_ref = bf16[512,768]{1,0:T(8,128)(2,1)} fusion(bf16[512,768]{1,0:T(8,128)(2,1)} %out_ref.1, bf16[768,768]{1,0:T(8,128)(2,1)S(1)} %copy-done), kind=kOutput, calls=%fused_computation | convolution fusion | flops 604372992 | bytes 2752512 | tf_op jit(solution)/shard_map/dot_general | solution.py:30
  10.2 4.4 %collective-permute-done.kp_ref = bf16[512,768]{1,0:T(8,128)(2,1)S(1)} collective-permute-done((bf16[512,768]{1,0:T(8,128)(2,1)}, bf16[512,768]{1,0:T(8,128)(2,1)S(1)}, u32[]{:S(2)}, u32[]{:S(2)}) %collective-permute-start) | collective-permute-done | bytes 786464 | tf_op jit(solution)/shard_map/ppermute | solution.py:42
  14.6 0.0 copy-start.5
  14.6 8.4 %collective-permute-done.1.vp_ref = bf16[512,768]{1,0:T(8,128)(2,1)S(1)} collective-permute-done((bf16[512,768]{1,0:T(8,128)(2,1)}, bf16[512,768]{1,0:T(8,128)(2,1)S(1)}, u32[]{:S(2)}, u32[]{:S(2)}) %collective-permute-start.1) | collective-permute-done | bytes 786464 | tf_op jit(solution)/shard_map/ppermute | solution.py:42
  23.0 0.0 copy-start.6
  23.0 0.0 copy-done.5
  23.0 0.9 copy-done.6
  23.9 0.0 copy-start.3
  23.9 0.0 copy-start.4
  23.9 27.4 %attention.1 = (bf16[512,768]{1,0:T(8,128)(2,1)}, bf16[512,768]{1,0:T(8,128)(2,1)}, bf16[512,768]{1,0:T(8,128)(2,1)}, f32[512,768]{1,0:T(8,128)}, f32[512,768]{1,0:T(8,128)}) custom-call(s32[1]{0:T(128)} %bitcast.first_ref, s32[1,64]{1,0:T(1,128)} %bitcast.12, bf16[512,768]{1,0:T(8,128)(2,1)} %q_ref.1, bf16[512,768]{1,0:T(8,128)(2,1)} %copy-done.5, ...), custom_call_target="tpu_custom_call" | custom-call | flops 3019898880 | bytes 7864320 | tf_op jit(solution)/shard_map/attention/pallas_call | solution.py:173
  51.3 1.9 %collective-permute-start.2 = (bf16[512,768]{1,0:T(8,128)(2,1)}, bf16[512,768]{1,0:T(8,128)(2,1)S(1)}, u32[]{:S(2)}, u32[]{:S(2)}) collective-permute-start(bf16[512,768]{1,0:T(8,128)(2,1)} %get-tuple-element.14), channel_id=1, source_target_pairs={{1,0},{2,1},{3,2},{4,3},{5,4},{6,5},{7,6},{8,7},{9,8},{10,9},{11,1... | collective-permute-start | bytes 2359304 | tf_op jit(solution)/shard_map/ppermute | solution.py:42
  53.2 1.9 %collective-permute-start.3 = (bf16[512,768]{1,0:T(8,128)(2,1)}, bf16[512,768]{1,0:T(8,128)(2,1)S(1)}, u32[]{:S(2)}, u32[]{:S(2)}) collective-permute-start(bf16[512,768]{1,0:T(8,128)(2,1)} %get-tuple-element.15), channel_id=1, source_target_pairs={{1,0},{2,1},{3,2},{4,3},{5,4},{6,5},{7,6},{8,7},{9,8},{10,9},{11,1... | collective-permute-start | bytes 2359304 | tf_op jit(solution)/shard_map/ppermute | solution.py:42
  55.1 0.0 copy-done.3
  55.1 0.9 copy.22
  56.0 4.4 %slots.1 = (s32[2,512]{1,0:T(2,128)}, s32[1,1280]{1,0:T(1,128)}) custom-call(s32[2,512]{1,0:T(2,128)} %row_ref.1, s32[512,2]{1,0:T(8,128)} %bitcast.10), custom_call_target="tpu_custom_call" | custom-call | tf_op jit(solution)/shard_map/slots/pallas_call | solution.py:76
  60.4 0.7 reduce
  61.1 0.9 reshape.28
  62.0 12.2 %all-to-all-start = ((s32[128,2,5]{2,1,0:T(2,128)}), s32[128,2,5]{2,1,0:T(2,128)S(1)}, u32[]{:S(2)}, u32[]{:S(2)}) async-start(s32[128,2,5]{2,1,0:T(2,128)} %reshape.28), calls=%async_computation | async-start | bytes 262144 | tf_op jit(solution)/shard_map/all_to_all | solution.py:276
  74.2 0.0 copy-done.4
  74.2 0.6 reshape.27.gain_ref
  74.8 0.0 collective-permute-done.2.bk_ref
  74.8 0.0 copy-start.1
  74.8 0.0 collective-permute-done.3.bv_ref
  74.8 0.0 copy-start.2
  74.8 0.9 copy-done.1
  75.7 0.3 copy-done.2
  76.0 10.1 %finish.1 = (bf16[512,768]{1,0:T(8,128)(2,1)}, bf16[1280,768]{1,0:T(8,128)(2,1)}) custom-call(bf16[512,768]{1,0:T(8,128)(2,1)} %get-tuple-element.11.dq_ref, f32[512,768]{1,0:T(8,128)} %get-tuple-element.12.dk_ref, f32[512,768]{1,0:T(8,128)} %get-tuple-element.13.dv_ref, bf16[512,768]{1,0:T(8,128)(2,1)} %copy-done.1, bf16[512,768]{1,0:T(8,128)(2,1)} %copy-done.2, ...), custom_call_target="tpu_custom_call" | custom-call | tf_op jit(solution)/shard_map/finish/pallas_call | solution.py:239
  86.1 4.8 %reshape.30 = bf16[128,2,5,768]{3,2,1,0:T(8,128)(2,1)} reshape(bf16[1280,768]{1,0:T(8,128)(2,1)} %get-tuple-element.19) | data formatting | bytes 3932160 | tf_op jit(solution)/shard_map/reshape | solution.py:309
  90.9 4.8 %copy.24 = bf16[128,2,5,768]{3,1,2,0:T(2,128)(2,1)} copy(bf16[128,2,5,768]{3,2,1,0:T(8,128)(2,1)} %reshape.30) | data formatting | bytes 3932160 | tf_op jit(solution)/shard_map/reshape | solution.py:309
  95.8 0.0 all-to-all-done
  95.8 13.6 %all-to-all-start.1 = ((bf16[128,2,5,768]{3,1,2,0:T(2,128)(2,1)}), bf16[128,2,5,768]{3,1,2,0:T(2,128)(2,1)S(1)}, u32[]{:S(2)}, u32[]{:S(2)}) async-start(bf16[128,2,5,768]{3,1,2,0:T(2,128)(2,1)} %copy.24), calls=%async_computation.1 | async-start | bytes 3932160 | tf_op jit(solution)/shard_map/all_to_all | solution.py:276
  109.3 0.8 reshape.32.label_ref
  110.1 28.3 %all-to-all-done.1 = bf16[128,2,5,768]{3,1,2,0:T(2,128)(2,1)S(1)} async-done(((bf16[128,2,5,768]{3,1,2,0:T(2,128)(2,1)}), bf16[128,2,5,768]{3,1,2,0:T(2,128)(2,1)S(1)}, u32[]{:S(2)}, u32[]{:S(2)}) %all-to-all-start.1) | async-done | bytes 1966112 | tf_op jit(solution)/shard_map/all_to_all | solution.py:276
  138.4 1.6 %copy.26.rows_ref = bf16[2,640,768]{2,1,0:T(8,128)(2,1)} copy(bf16[2,640,768]{2,0,1:T(2,128)(2,1)S(1)} %bitcast.9) | data formatting | bytes 3932160 | tf_op jit(solution)/shard_map/reshape | solution.py:310
  140.0 9.3 %collect.1 = bf16[2,2048,768]{2,1,0:T(8,128)(2,1)} custom-call(s32[2,1,640]{2,1,0:T(1,128)} %reshape.32.label_ref, bf16[2,640,768]{2,1,0:T(8,128)(2,1)} %copy.26.rows_ref), custom_call_target="tpu_custom_call" | custom-call | tf_op jit(solution)/shard_map/collect/pallas_call | solution.py:261
  (1 shorter events, 0.0 us)
Async XLA Ops:
  0.6 6.7 %copy-start = (bf16[768,768]{1,0:T(8,128)(2,1)S(1)}, bf16[768,768]{1,0:T(8,128)(2,1)}, u32[]{:S(2)}) copy-start(bf16[768,768]{1,0:T(8,128)(2,1)} %param.20) | copy-start | bytes 3538948
  0.6 14.0 %collective-permute-start = (bf16[512,768]{1,0:T(8,128)(2,1)}, bf16[512,768]{1,0:T(8,128)(2,1)S(1)}, u32[]{:S(2)}, u32[]{:S(2)}) collective-permute-start(bf16[512,768]{1,0:T(8,128)(2,1)} %ko_ref.1), channel_id=1, source_target_pairs={{0,1},{1,2},{2,3},{3,4},{4,5},{5,6},{6,7},{7,8},{8,9},{9,10},{10,1... | collective-permute-start | bytes 2359304 | tf_op jit(solution)/shard_map/ppermute | solution.py:42
  5.4 17.7 %collective-permute-start.1 = (bf16[512,768]{1,0:T(8,128)(2,1)}, bf16[512,768]{1,0:T(8,128)(2,1)S(1)}, u32[]{:S(2)}, u32[]{:S(2)}) collective-permute-start(bf16[512,768]{1,0:T(8,128)(2,1)} %vo_ref.1), channel_id=1, source_target_pairs={{0,1},{1,2},{2,3},{3,4},{4,5},{5,6},{6,7},{7,8},{8,9},{9,10},{10,1... | collective-permute-start | bytes 2359304 | tf_op jit(solution)/shard_map/ppermute | solution.py:42
  14.6 8.4 %copy-start.5 = (bf16[512,768]{1,0:T(8,128)(2,1)}, bf16[512,768]{1,0:T(8,128)(2,1)S(1)}, u32[]{:S(2)}) copy-start(bf16[512,768]{1,0:T(8,128)(2,1)S(1)} %collective-permute-done.kp_ref) | copy-start | bytes 2359300
  23.0 0.9 copy-start.6
  23.9 31.2 %copy-start.3 = (s32[2,512]{1,0:T(2,128)S(1)}, s32[2,512]{1,0:T(2,128)}, u32[]{:S(2)}) copy-start(s32[2,512]{1,0:T(2,128)} %row_ref.1) | copy-start | bytes 12292
  23.9 50.3 %copy-start.4 = (f32[768]{0:T(1024)S(1)}, f32[768]{0:T(1024)}, u32[]{:S(2)}) copy-start(f32[768]{0:T(1024)} %param.13) | copy-start | bytes 9220
  51.3 23.5 %collective-permute-start.2 = (bf16[512,768]{1,0:T(8,128)(2,1)}, bf16[512,768]{1,0:T(8,128)(2,1)S(1)}, u32[]{:S(2)}, u32[]{:S(2)}) collective-permute-start(bf16[512,768]{1,0:T(8,128)(2,1)} %get-tuple-element.14), channel_id=1, source_target_pairs={{1,0},{2,1},{3,2},{4,3},{5,4},{6,5},{7,6},{8,7},{9,8},{10,9},{11,1... | collective-permute-start | bytes 2359304 | tf_op jit(solution)/shard_map/ppermute | solution.py:42
  53.2 21.6 %collective-permute-start.3 = (bf16[512,768]{1,0:T(8,128)(2,1)}, bf16[512,768]{1,0:T(8,128)(2,1)S(1)}, u32[]{:S(2)}, u32[]{:S(2)}) collective-permute-start(bf16[512,768]{1,0:T(8,128)(2,1)} %get-tuple-element.15), channel_id=1, source_target_pairs={{1,0},{2,1},{3,2},{4,3},{5,4},{6,5},{7,6},{8,7},{9,8},{10,9},{11,1... | collective-permute-start | bytes 2359304 | tf_op jit(solution)/shard_map/ppermute | solution.py:42
  62.0 33.8 %all-to-all-start = ((s32[128,2,5]{2,1,0:T(2,128)}), s32[128,2,5]{2,1,0:T(2,128)S(1)}, u32[]{:S(2)}, u32[]{:S(2)}) async-start(s32[128,2,5]{2,1,0:T(2,128)} %reshape.28), calls=%async_computation | async-start | bytes 262144 | tf_op jit(solution)/shard_map/all_to_all | solution.py:276
  74.8 0.9 copy-start.1
  74.8 1.2 copy-start.2
  95.8 42.7 %all-to-all-start.1 = ((bf16[128,2,5,768]{3,1,2,0:T(2,128)(2,1)}), bf16[128,2,5,768]{3,1,2,0:T(2,128)(2,1)S(1)}, u32[]{:S(2)}, u32[]{:S(2)}) async-start(bf16[128,2,5,768]{3,1,2,0:T(2,128)(2,1)} %copy.24), calls=%async_computation.1 | async-start | bytes 3932160 | tf_op jit(solution)/shard_map/all_to_all | solution.py:276

commit v2 on v1

--- a/solution.py
+++ b/solution.py
@@ -19,7 +19,7 @@
 BF16 = jnp.bfloat16
 F32 = jnp.float32
 I32 = jnp.int32
-VMEM_BYTES = 56 * 1024 * 1024
+GROUPS = (3, 3)
 
 
 def iota(shape, dim):
@@ -32,8 +32,8 @@
     )
 
 
-def params():
-    return pltpu.CompilerParams(vmem_limit_bytes=VMEM_BYTES)
+def params(mib):
+    return pltpu.CompilerParams(vmem_limit_bytes=mib * 1024 * 1024)
 
 
 def shifted(shard, by):
@@ -42,9 +42,14 @@
     return lax.ppermute(shard, AXES, pairs)
 
 
-def slots_kernel(row_ref, col_ref, slot_ref, label_ref):
+MAIN = 4
+CHUNK = 64
+
+
+def slots_kernel(first_ref, row_ref, col_ref, slot_ref, label_ref):
     count = row_ref.shape[1]
     places = label_ref.shape[1]
+    odd = lax.rem(first_ref[0] // count, 2)
     labels = jnp.full((1, places), ROWS_DEV, I32)
     sub = iota((count, count), 0)
     lane = iota((count, count), 1)
@@ -59,9 +64,12 @@
         mates = row_owner == col_owner
         place_row = jnp.sum((first_col & mates & (col < row)).astype(I32), axis=0, keepdims=True)
         place_col = jnp.sum((first_row & mates & (row < col)).astype(I32), axis=1, keepdims=True)
-        base = table * SLOTS
-        slot_ref[table : table + 1, :] = row_owner * (NG * SLOTS) + base + place_row
-        slot_col = col_owner * (NG * SLOTS) + base + place_col
+        side = lax.rem(table + odd, 2)
+        main = row_owner * (NG * MAIN) + side * MAIN + place_row
+        slot_ref[table : table + 1, :] = jnp.where(place_row < MAIN, main, -1)
+        last = row_owner * NG + table
+        slot_ref[NG + table : NG + table + 1, :] = jnp.where(place_row < MAIN, -1, last)
+        slot_col = col_owner * (NG * SLOTS) + table * SLOTS + place_col
         local_col = col - col_owner * ROWS_DEV
         hit = slot_col == iota((count, places), 1)
         labels = jnp.minimum(
@@ -70,18 +78,23 @@
     label_ref[...] = labels
 
 
-def make_slots(hash_ids, devices):
+def make_slots(first, hash_ids, devices):
     count = hash_ids.shape[1]
     places = devices * NG * SLOTS
     return pl.pallas_call(
         slots_kernel,
+        in_specs=[
+            pl.BlockSpec(memory_space=pltpu.SMEM),
+            pl.BlockSpec(memory_space=pltpu.VMEM),
+            pl.BlockSpec(memory_space=pltpu.VMEM),
+        ],
         out_shape=(
-            jax.ShapeDtypeStruct((NG, count), I32),
+            jax.ShapeDtypeStruct((2 * NG, count), I32),
             jax.ShapeDtypeStruct((1, places), I32),
         ),
-        compiler_params=params(),
+        compiler_params=params(56),
         name="slots",
-    )(hash_ids, jnp.transpose(hash_ids))
+    )(first, hash_ids, jnp.transpose(hash_ids))
 
 
 QT = 256
@@ -90,7 +103,7 @@
 
 def attention_kernel(
     first_ref, len_ref, q_ref, kp_ref, ko_ref, vp_ref, vo_ref, da_ref,
-    dq_ref, dkp_ref, dvp_ref, dko_ref, dvo_ref,
+    dq_ref, back_ref, dko_ref, dvo_ref,
     bias_ref, kx_ref, vx_ref, dk_ref, dv_ref,
 ):
     count = q_ref.shape[0]
@@ -111,9 +124,9 @@
             ok = (kpos >= low[:, cols]) & (kpos <= qpos[:, cols])
             bias_ref[tile] = jnp.where(ok, 0.0, NEG)
 
-    kx_ref[:WINDOW] = kp_ref[...]
+    kx_ref[:WINDOW] = kp_ref[0]
     kx_ref[WINDOW:] = ko_ref[...]
-    vx_ref[:WINDOW] = vp_ref[...]
+    vx_ref[:WINDOW] = vp_ref[0]
     vx_ref[WINDOW:] = vo_ref[...]
     lane = iota((QT, LANES), 1)
     scale = HD ** (-0.5)
@@ -157,18 +170,20 @@
             dv_ref[seen, :] += dv[:both]
             dk_ref[fresh, :] = dk[both:]
             dv_ref[fresh, :] = dv[both:]
-    dkp_ref[...] = dk_ref[:WINDOW].astype(BF16)
-    dvp_ref[...] = dv_ref[:WINDOW].astype(BF16)
+    back_ref[0] = dk_ref[:WINDOW].astype(BF16)
+    back_ref[1] = dv_ref[:WINDOW].astype(BF16)
     dko_ref[...] = dk_ref[WINDOW:]
     dvo_ref[...] = dv_ref[WINDOW:]
 
 
-def attention_grads(first, doc_lengths, queries, prev_keys, keys, prev_values, values, grad_attn):
-    count, width = queries.shape
+def attention_grads(first, doc_lengths, queries, halo, keys, values, grad_attn, at):
+    count = queries.shape[0]
+    width = halo.shape[2]
     pairs = width // LANES
     ext = count + WINDOW
     tiles = count // QT
-    column = lambda n: pl.BlockSpec((n, LANES), lambda i: (0, i))
+    column = pl.BlockSpec((count, LANES), lambda i: (0, i + at))
+    fresh = pl.BlockSpec((count, LANES), lambda i: (0, i))
     docs = doc_lengths.shape[0]
     return pl.pallas_call(
         attention_kernel,
@@ -176,13 +191,17 @@
         in_specs=[
             pl.BlockSpec(memory_space=pltpu.SMEM),
             pl.BlockSpec((1, docs), lambda i: (0, 0)),
-            column(count), column(WINDOW), column(count), column(WINDOW), column(count), column(count),
+            column,
+            pl.BlockSpec((1, WINDOW, LANES), lambda i: (0, 0, i)),
+            column,
+            pl.BlockSpec((1, WINDOW, LANES), lambda i: (1, 0, i)),
+            column,
+            column,
         ],
-        out_specs=[column(count), column(WINDOW), column(WINDOW), column(count), column(count)],
+        out_specs=[fresh, pl.BlockSpec((2, WINDOW, LANES), lambda i: (0, 0, i)), fresh, fresh],
         out_shape=[
             jax.ShapeDtypeStruct((count, width), BF16),
-            jax.ShapeDtypeStruct((WINDOW, width), BF16),
-            jax.ShapeDtypeStruct((WINDOW, width), BF16),
+            jax.ShapeDtypeStruct((2, WINDOW, width), BF16),
             jax.ShapeDtypeStruct((count, width), F32),
             jax.ShapeDtypeStruct((count, width), F32),
         ],
@@ -193,26 +212,33 @@
             pltpu.VMEM((ext, LANES), F32),
             pltpu.VMEM((ext, LANES), F32),
         ],
-        compiler_params=params(),
+        compiler_params=params(56),
         cost_estimate=pl.CostEstimate(
             flops=10 * count * KT * width, bytes_accessed=20 * count * width,
             transcendentals=count * KT * width // HD,
         ),
         name="attention",
-    )(first, doc_lengths.reshape(1, docs), queries, prev_keys, keys, prev_values, values, grad_attn)
-
-
-PACK = 256
-
-
-def finish_kernel(
-    dq_ref, dk_ref, dv_ref, bk_ref, bv_ref, wq_ref, wk_ref, wv_ref,
-    hidden_ref, gain_ref, out_ref, slot_ref, gh_ref, sent_ref,
-):
-    count = hidden_ref.shape[0]
-    grad_k = (dk_ref[...] + bk_ref[...].astype(F32)).astype(BF16)
-    grad_v = (dv_ref[...] + bv_ref[...].astype(F32)).astype(BF16)
-    norm = dot(dq_ref[...], wq_ref[...], 1, 1)
+    )(first, doc_lengths.reshape(1, docs), queries, halo, keys, halo, values, grad_attn)
+
+
+PACK = 32
+
+
+def finish_kernel(*refs):
+    groups = len(GROUPS)
+    parts = [refs[4 * g : 4 * g + 4] for g in range(groups)]
+    (wq_ref, wk_ref, wv_ref, hidden_ref, gain_ref, out_ref, slot_ref, gh_ref, sent_ref) = refs[
+        4 * groups :
+    ]
+    count, width = hidden_ref.shape
+    grad_q = jnp.concatenate([dq[...] for dq, _, _, _ in parts], axis=1)
+    grad_k = jnp.concatenate(
+        [(dk[...] + back[0].astype(F32)).astype(BF16) for _, back, dk, _ in parts], axis=1
+    )
+    grad_v = jnp.concatenate(
+        [(dv[...] + back[1].astype(F32)).astype(BF16) for _, back, _, dv in parts], axis=1
+    )
+    norm = dot(grad_q, wq_ref[...], 1, 1)
     norm = norm + dot(grad_k, wk_ref[...], 1, 1)
     norm = norm + dot(grad_v, wv_ref[...], 1, 1)
     full = hidden_ref[...].astype(F32)
@@ -222,54 +248,113 @@
     through = inverse * (scaled - unit * jnp.mean(scaled * unit, axis=1, keepdims=True))
     grad_hidden = (out_ref[...].astype(F32) + through).astype(BF16)
     gh_ref[...] = grad_hidden
-    slots = sent_ref.shape[0]
-    for at in range(0, slots, PACK):
-        place = at + iota((PACK, count), 0)
-        hit = place == slot_ref[0:1, :]
+
+    def hits(place, at):
+        hit = place == slot_ref[at : at + 1, :]
         for table in range(1, NG):
-            hit = hit | (place == slot_ref[table : table + 1, :])
-        sent_ref[at : at + PACK, :] = dot(
-            jnp.where(hit, 1.0, 0.0).astype(BF16), grad_hidden, 1, 0
-        ).astype(BF16)
-
-
-def finish(dq, dk, dv, bk, bv, wq, wk, wv, hidden, gain, grad_out, slot, devices):
+            hit = hit | (place == slot_ref[at + table : at + table + 1, :])
+        return jnp.where(hit, 1.0, 0.0).astype(BF16)
+
+    blocks = width // LANES
+    both = NG * MAIN
+    tail = CHUNK - blocks * both
+    cut = lambda value, c: value[:, c * LANES : (c + 1) * LANES]
+    for at in range(0, sent_ref.shape[0], PACK):
+        place = at * both + iota((PACK * both, count), 0)
+        main = dot(hits(place, 0), grad_hidden, 1, 0)
+        for c in range(0, blocks, 2):
+            pair = [cut(main, c + i).reshape(PACK, both, LANES) for i in range(2)]
+            sent_ref[at : at + PACK, c * both : (c + 2) * both, :] = jnp.concatenate(
+                pair, axis=1
+            ).astype(BF16)
+        rows = iota((PACK * tail, count), 0)
+        place = (at + rows // tail) * NG + lax.rem(rows, NG)
+        last = dot(hits(place, NG), grad_hidden, 1, 0)
+        block = lax.rem(iota((PACK * tail, LANES), 0), tail) // NG
+        value = jnp.zeros((PACK * tail, LANES), F32)
+        for c in range(blocks):
+            value = jnp.where(block == c, cut(last, c), value)
+        sent_ref[at : at + PACK, blocks * both :, :] = value.reshape(PACK, tail, LANES).astype(BF16)
+
+
+def finish(parts, wq, wk, wv, hidden, gain, grad_out, slot, devices):
     count, width = hidden.shape
-    places = devices * NG * SLOTS
     return pl.pallas_call(
         finish_kernel,
         out_shape=(
             jax.ShapeDtypeStruct((count, width), BF16),
-            jax.ShapeDtypeStruct((places, width), BF16),
+            jax.ShapeDtypeStruct((devices, CHUNK, LANES), BF16),
         ),
-        compiler_params=params(),
+        compiler_params=params(56),
         name="finish",
-    )(dq, dk, dv, bk, bv, wq, wk, wv, hidden, gain.reshape(1, width), grad_out, slot)
+    )(
+        *[array for part in parts for array in part],
+        wq, wk, wv, hidden, gain.reshape(1, width), grad_out, slot,
+    )
 
 
 COLLECT = 512
-
-
-def collect_kernel(label_ref, rows_ref, out_ref):
+APART = 16
+
+
+def collect_kernel(label_ref, got_ref, out_ref, rows_ref):
+    devices = got_ref.shape[0]
+    blocks = rows_ref.shape[2] // LANES
+    both = NG * MAIN
+    tail = CHUNK - blocks * both
+    mains = devices * MAIN
+
+    @pl.when((pl.program_id(0) == 0) & (pl.program_id(1) == 0))
+    def _():
+        low = iota((devices // 2, both, LANES), 1) < MAIN
+        for c in range(0, blocks, 2):
+            wide = got_ref[:, c * both : (c + 2) * both, :].astype(F32)
+            for i in range(2):
+                cols = slice((c + i) * LANES, (c + i + 1) * LANES)
+                piece = wide[:, i * both : (i + 1) * both, :]
+                piece = piece.reshape(devices // 2, 2, both, LANES)
+                even, odd = piece[:, 0], piece[:, 1]
+                zero = jnp.where(low, even, odd).reshape(mains, LANES)
+                one = jnp.where(low, odd, even).reshape(mains, LANES)
+                rows_ref[0, :mains, cols] = zero.astype(BF16)
+                rows_ref[1, :mains, cols] = one.astype(BF16)
+        shape = (NG * blocks * APART, APART * tail)
+        row = iota((shape[0], 1), 0)
+        device = lax.rem(row, APART)
+        block = lax.rem(row // APART, blocks)
+        table = row // (APART * blocks)
+        source = device * tail + block * NG + table
+        pick = jnp.where(source == iota(shape, 1), 1.0, 0.0).astype(BF16)
+        for at in range(0, devices, APART):
+            rest = got_ref[at : at + APART, blocks * both :, :].reshape(APART * tail, LANES)
+            rest = dot(pick, rest, 1, 0).astype(BF16)
+            for t in range(NG):
+                for c in range(blocks):
+                    start = (t * blocks + c) * APART
+                    rows_ref[t, mains + at : mains + at + APART, c * LANES : (c + 1) * LANES] = rest[
+                        start : start + APART
+                    ]
+
     place = pl.program_id(1) * COLLECT + iota((COLLECT, label_ref.shape[2]), 0)
     hit = jnp.where(place == label_ref[0], 1.0, 0.0).astype(BF16)
-    out_ref[0] = dot(hit, rows_ref[0], 1, 0).astype(BF16)
-
-
-def collect(labels, rows):
-    tables, number, width = rows.shape
+    out_ref[0] = dot(hit, rows_ref[pl.program_id(0)], 1, 0).astype(BF16)
+
+
+def collect(labels, got, width):
+    tables, _, number = labels.shape
     return pl.pallas_call(
         collect_kernel,
         grid=(tables, ROWS_DEV // COLLECT),
         in_specs=[
             pl.BlockSpec((1, 1, number), lambda t, i: (t, 0, 0)),
-            pl.BlockSpec((1, number, width), lambda t, i: (t, 0, 0)),
+            pl.BlockSpec(got.shape, lambda t, i: (0, 0, 0)),
         ],
         out_specs=pl.BlockSpec((1, COLLECT, width), lambda t, i: (t, i, 0)),
         out_shape=jax.ShapeDtypeStruct((tables, ROWS_DEV, width), BF16),
-        compiler_params=params(),
+        scratch_shapes=[pltpu.VMEM((tables, number, width), BF16)],
+        compiler_params=params(56),
         name="collect",
-    )(labels, rows)
+    )(labels, got)
 
 
 def exchanged(part):
@@ -293,22 +378,33 @@
     count, width = hidden.shape
     devices = lax.axis_size(AXES)
     first = (lax.axis_index(AXES) * count).astype(I32).reshape(1)
-    prev_keys, prev_values = shifted((keys, values), 1)
-    slot, labels = make_slots(hash_ids, devices)
+    halos = []
+    at = 0
+    for pairs in GROUPS:
+        cols = slice(at * LANES, (at + pairs) * LANES)
+        halos.append(shifted(jnp.stack([keys[:, cols], values[:, cols]]), 1))
+        at += pairs
+    grad_attn = dot(grad_out, w_out, 1, 1).astype(BF16)
+    slot, labels = make_slots(first, hash_ids, devices)
+    grad_attn, slot, labels = lax.optimization_barrier((grad_attn, slot, labels))
+    parts = []
+    at = 0
+    for pairs, halo in zip(GROUPS, halos):
+        dq, back, dk, dv = attention_grads(
+            first, doc_lengths, queries, halo, keys, values, grad_attn, at
+        )
+        parts.append((dq, shifted(back, -1), dk, dv))
+        at += pairs
+    labels, _ = lax.optimization_barrier((labels, parts[-1][0]))
     labels = exchanged(labels.reshape(devices, NG, SLOTS))
-    labels = jnp.transpose(labels, (1, 0, 2)).reshape(NG, 1, devices * SLOTS)
-    grad_attn = dot(grad_out, w_out, 1, 1).astype(BF16)
-    dq, dkp, dvp, dko, dvo = attention_grads(
-        first, doc_lengths, queries, prev_keys, keys, prev_values, values, grad_attn
-    )
-    back_keys, back_values = shifted((dkp, dvp), -1)
+    labels = jnp.transpose(labels, (1, 0, 2))
+    main = labels[:, :, :MAIN].reshape(NG, devices // 2, 2, MAIN)
+    main = jnp.stack([main[0], main[1, :, ::-1]])
+    labels = jnp.concatenate([main.reshape(NG, devices * MAIN), labels[:, :, MAIN]], axis=1)
     grad_hidden, sent = finish(
-        dq, dko, dvo, back_keys, back_values, w_query, w_key, w_value,
-        hidden, gain, grad_out, slot, devices,
-    )
-    rows = exchanged(sent.reshape(devices, NG, SLOTS, width))
-    rows = jnp.transpose(rows, (1, 0, 2, 3)).reshape(NG, devices * SLOTS, width)
-    return grad_hidden, collect(labels, rows)
+        parts, w_query, w_key, w_value, hidden, gain, grad_out, slot, devices
+    )
+    return grad_hidden, collect(labels[:, None, :], exchanged(sent), width)
 
 
 def solution(mesh):

time: 150 us -> 133 us (0.89)
  waiting for transfers between devices: 41.2 us -> 29.2 us
  local copies, waits for them, and re-layouts: 16.4 us -> 7.78 us
  Pallas kernels: 51.2 us -> 56.2 us
    ppermute x4, waiting for transfers between devices: 12.9 us -> 0.01 us  [shifted(): return lax.ppermute(shard, AXES, pairs)]
    reshape x4 -> x0, local copies, waits for them, and re-layouts: 12 us -> none  [the longest x2 9.62 us: shards(): rows = exchanged(sent.reshape(devices, NG, SLOTS, width))]
    pallas_call x1 -> x2, Pallas kernels: 27.4 us -> 29.6 us  [attention_grads(): pl.pallas_call(attention_kernel, grid=(pairs,), in_specs=[pl.BlockSpec(me...]
    another operation x0 -> x3, local copies, waits for them, and re-layouts: none -> 1.85 us  [the longest x1 1.61 us: shards(): halos.append(shifted(jnp.stack([keys[:, cols], values[:, cols]]), 1))]
    pallas_call x1, Pallas kernels: 10.1 us -> 11.9 us  [finish(): pl.pallas_call(finish_kernel, out_shape=(jax.ShapeDtypeStruct((count, wid...]
    ppermute x4, starting transfers between devices: 10.5 us -> 12 us  [shifted(): return lax.ppermute(shard, AXES, pairs)]
    unnamed x15 -> x17, local copies, waits for them, and re-layouts: 2.92 us -> 3.39 us
  transfers between devices with their start and end apart: 6 -> 6, of which waited for: 3 -> 1; matrix products, arithmetic and copies ran while one was open for 11% -> 4% of each run, Pallas kernels for 10% -> 35%
where the time goes in v2:
time: 133 us
  Pallas kernels  56.2 us (42%)
  starting transfers between devices  36.9 us (28%)
  waiting for transfers between devices  29.2 us (22%)
  local copies, waits for them, and re-layouts  7.78 us (6%)
  matrix products  1.69 us (1%)
    pallas_call x2, Pallas kernels, attention_grads(): pl.pallas_call(attention_kernel, grid=(pairs,), in_specs=[pl.BlockSpec(me...  29.6 us
    all_to_all x2, waiting for transfers between devices, exchanged(): return lax.all_to_all(part, AXES, split_axis=0, concat_axis=0, tiled=True)  29.2 us
    all_to_all x2, starting transfers between devices, exchanged(): return lax.all_to_all(part, AXES, split_axis=0, concat_axis=0, tiled=True)  24.9 us
    ppermute x4, starting transfers between devices, shifted(): return lax.ppermute(shard, AXES, pairs)  12 us
    pallas_call x1, Pallas kernels, finish(): pl.pallas_call(finish_kernel, out_shape=(jax.ShapeDtypeStruct((count, wid...  11.9 us
    pallas_call x1, Pallas kernels, collect(): pl.pallas_call(collect_kernel, grid=(tables, ROWS_DEV // COLLECT), in_spe...  10.2 us
    pallas_call x1, Pallas kernels, make_slots(): pl.pallas_call(slots_kernel, in_specs=[pl.BlockSpec(memory_space=pltpu.SM...  4.44 us
    unnamed x17, local copies, waits for them, and re-layouts  3.39 us
  transfers between devices with their start and end apart: 6, of which 1 were waited for; matrix products, arithmetic and copies ran while one was open for 4% of the time, Pallas kernels for 35%

profile of v2, /device:TPU:1, one launch (start us, length us, event | category | flops | bytes accessed | tf_op | source)
XLA Modules:
  0.0 132.8 jit_solution(16878370083260420944)
XLA Ops:
  0.6 0.0 copy-start
  0.6 1.6 %slice_bitcast_fusion = (bf16[1,512,384]{2,1,0:T(8,128)(2,1)S(1)}, bf16[1,512,384]{2,1,0:T(8,128)(2,1)S(1)}, bf16[1,512,384]{2,1,0:T(8,128)(2,1)S(1)}, bf16[1,512,384]{2,1,0:T(8,128)(2,1)S(1)}) fusion(bf16[512,768]{1,0:T(8,128)(2,1)} %vo_ref.3, bf16[512,768]{1,0:T(8,128)(2,1)} %ko_ref.3), kind=kLoop, calls=%fused_computation.3 | loop fusion | bytes 3145728 | tf_op jit(solution)/shard_map/stack | solution.py:385
  2.3 0.1 pad_maximum_fusion.1
  2.4 0.0 copy-start.5
  2.4 0.0 copy-start.2
  2.4 4.7 %collective-permute-start.2 = (bf16[2,512,384]{2,1,0:T(8,128)(2,1)S(1)}, bf16[2,512,384]{2,1,0:T(8,128)(2,1)}, u32[]{:S(2)}, u32[]{:S(2)}) collective-permute-start(bf16[2,512,384]{2,1,0:T(8,128)(2,1)S(1)} %pad_maximum_fusion.1), channel_id=1, source_target_pairs={{0,1},{1,2},{2,3},{3,4},{4,5},{5,6},{6,7},{7,8},{8,9},{9,10},{10,1... | collective-permute-start | bytes 2359304 | tf_op jit(solution)/shard_map/ppermute | solution.py:42
  7.1 0.1 pad_maximum_fusion
  7.2 1.9 %collective-permute-start = (bf16[2,512,384]{2,1,0:T(8,128)(2,1)S(1)}, bf16[2,512,384]{2,1,0:T(8,128)(2,1)}, u32[]{:S(2)}, u32[]{:S(2)}) collective-permute-start(bf16[2,512,384]{2,1,0:T(8,128)(2,1)S(1)} %pad_maximum_fusion), channel_id=1, source_target_pairs={{0,1},{1,2},{2,3},{3,4},{4,5},{5,6},{6,7},{7,8},{8,9},{9,10},{10,1... | collective-permute-start | bytes 2359304 | tf_op jit(solution)/shard_map/ppermute | solution.py:42
  9.1 0.0 copy-done.5
  9.2 0.9 copy.25
  10.0 4.4 %slots.1 = (s32[4,512]{1,0:T(4,128)}, s32[1,1280]{1,0:T(1,128)}) custom-call(s32[1]{0:T(128)} %bitcast.first_ref, s32[2,512]{1,0:T(2,128)} %row_ref.1, s32[512,2]{1,0:T(8,128)} %bitcast.17), custom_call_target="tpu_custom_call" | custom-call | tf_op jit(solution)/shard_map/slots/pallas_call | solution.py:84
  14.5 0.0 copy-done
  14.5 0.0 copy-done.2
  14.5 1.7 %convolution_convert_fusion.da_ref = bf16[512,768]{1,0:T(8,128)(2,1)} fusion(bf16[512,768]{1,0:T(8,128)(2,1)S(1)} %copy-done.2, bf16[768,768]{1,0:T(8,128)(2,1)S(1)} %copy-done), kind=kOutput, calls=%fused_computation | convolution fusion | flops 604372992 | bytes 2752512 | tf_op jit(solution)/shard_map/dot_general | solution.py:30
  16.2 0.0 collective-permute-done.2.kp_ref.vp_ref
  16.2 14.9 %attention.3 = (bf16[512,384]{1,0:T(8,128)(2,1)}, bf16[2,512,384]{2,1,0:T(8,128)(2,1)}, f32[512,384]{1,0:T(8,128)}, f32[512,384]{1,0:T(8,128)}) custom-call(s32[1]{0:T(128)} %bitcast.first_ref, s32[1,64]{1,0:T(1,128)} %bitcast.21, bf16[512,768]{1,0:T(8,128)(2,1)} %q_ref.3, bf16[2,512,384]{2,1,0:T(8,128)(2,1)} %collective-permute-done.2.kp_ref.vp_ref, ...), custom_call_target="tpu_custom_call" | custom-call | flops 1509949440 | bytes 3932160 | tf_op jit(solution)/shard_map/attention/pallas_call | solution.py:188
  31.0 0.0 copy-start.6
  31.0 0.0 copy-start.7
  31.0 3.4 %collective-permute-start.3 = (bf16[2,512,384]{2,1,0:T(8,128)(2,1)}, bf16[2,512,384]{2,1,0:T(8,128)(2,1)S(1)}, u32[]{:S(2)}, u32[]{:S(2)}) collective-permute-start(bf16[2,512,384]{2,1,0:T(8,128)(2,1)} %get-tuple-element.26), channel_id=1, source_target_pairs={{1,0},{2,1},{3,2},{4,3},{5,4},{6,5},{7,6},{8,7},{9,8},{10,9},{11,1... | collective-permute-start | bytes 2359304 | tf_op jit(solution)/shard_map/ppermute | solution.py:42
  34.5 0.0 collective-permute-done.kp_ref.vp_ref
  34.5 14.8 %attention.2 = (bf16[512,384]{1,0:T(8,128)(2,1)}, bf16[2,512,384]{2,1,0:T(8,128)(2,1)}, f32[512,384]{1,0:T(8,128)}, f32[512,384]{1,0:T(8,128)}) custom-call(s32[1]{0:T(128)} %bitcast.first_ref, s32[1,64]{1,0:T(1,128)} %bitcast.22, bf16[512,768]{1,0:T(8,128)(2,1)} %q_ref.3, bf16[2,512,384]{2,1,0:T(8,128)(2,1)} %collective-permute-done.kp_ref.vp_ref, ...), custom_call_target="tpu_custom_call" | custom-call | flops 1509949440 | bytes 3932160 | tf_op jit(solution)/shard_map/attention/pallas_call | solution.py:188
  49.3 1.9 %collective-permute-start.1 = (bf16[2,512,384]{2,1,0:T(8,128)(2,1)}, bf16[2,512,384]{2,1,0:T(8,128)(2,1)S(1)}, u32[]{:S(2)}, u32[]{:S(2)}) collective-permute-start(bf16[2,512,384]{2,1,0:T(8,128)(2,1)} %get-tuple-element.22), channel_id=1, source_target_pairs={{1,0},{2,1},{3,2},{4,3},{5,4},{6,5},{7,6},{8,7},{9,8},{10,9},{11,1... | collective-permute-start | bytes 2359304 | tf_op jit(solution)/shard_map/ppermute | solution.py:42
  51.2 0.0 copy-done.6
  51.3 0.9 reshape.27
  52.2 10.9 %all-to-all-start = ((s32[128,2,5]{2,1,0:T(2,128)}), s32[128,2,5]{2,1,0:T(2,128)S(1)}, u32[]{:S(2)}, u32[]{:S(2)}) async-start(s32[128,2,5]{2,1,0:T(2,128)} %reshape.27), calls=%async_computation | async-start | bytes 262144 | tf_op jit(solution)/shard_map/all_to_all | solution.py:361
  63.1 0.0 copy-done.7
  63.1 0.6 reshape.26.refs_12_
  63.7 0.0 collective-permute-done.3.refs_5_
  63.7 0.0 copy-start.3
  63.7 0.0 collective-permute-done.1.refs_1_
  63.7 0.0 copy-start.4
  63.7 0.9 copy-done.3
  64.6 0.3 copy-done.4
  64.9 11.9 %finish.1 = (bf16[512,768]{1,0:T(8,128)(2,1)}, bf16[128,64,128]{2,1,0:T(8,128)(2,1)}) custom-call(bf16[512,384]{1,0:T(8,128)(2,1)} %get-tuple-element.21.refs_0_, bf16[2,512,384]{2,1,0:T(8,128)(2,1)} %copy-done.4, f32[512,384]{1,0:T(8,128)} %get-tuple-element.23.refs_2_, f32[512,384]{1,0:T(8,128)} %get-tuple-element.24.refs_3_, ...), custom_call_target="tpu_custom_call" | custom-call | tf_op jit(solution)/shard_map/finish/pallas_call | solution.py:282
  76.8 0.0 all-to-all-done
  76.9 13.9 %all-to-all-start.1 = ((bf16[128,64,128]{2,1,0:T(8,128)(2,1)}), bf16[128,64,128]{2,1,0:T(8,128)(2,1)S(1)}, u32[]{:S(2)}, u32[]{:S(2)}) async-start(bf16[128,64,128]{2,1,0:T(8,128)(2,1)} %get-tuple-element.33), calls=%async_computation.1 | async-start | bytes 4194304 | tf_op jit(solution)/shard_map/all_to_all | solution.py:361
  90.8 0.1 copy.26
  90.9 0.1 copy.27
  91.0 0.1 stack.31
  91.1 0.1 copy.28
  91.2 0.1 rev.3
  91.4 0.1 stack.32
  91.5 0.6 broadcast_in_dim.3.label_ref
  92.1 29.2 %all-to-all-done.1.got_ref = bf16[128,64,128]{2,1,0:T(8,128)(2,1)S(1)} async-done(((bf16[128,64,128]{2,1,0:T(8,128)(2,1)}), bf16[128,64,128]{2,1,0:T(8,128)(2,1)S(1)}, u32[]{:S(2)}, u32[]{:S(2)}) %all-to-all-start.1) | async-done | bytes 2097184 | tf_op jit(solution)/shard_map/all_to_all | solution.py:361
  121.3 0.0 copy-start.1
  121.3 1.3 %copy-done.1 = bf16[128,64,128]{2,1,0:T(8,128)(2,1)} copy-done((bf16[128,64,128]{2,1,0:T(8,128)(2,1)}, bf16[128,64,128]{2,1,0:T(8,128)(2,1)S(1)}, u32[]{:S(2)}) %copy-start.1) | copy-done | bytes 2097176
  122.6 10.2 %collect.1 = bf16[2,2048,768]{2,1,0:T(8,128)(2,1)} custom-call(s32[2,1,640]{2,1,0:T(1,128)} %broadcast_in_dim.3.label_ref, bf16[128,64,128]{2,1,0:T(8,128)(2,1)} %copy-done.1), custom_call_target="tpu_custom_call" | custom-call | tf_op jit(solution)/shard_map/collect/pallas_call | solution.py:345
  (4 shorter events, 0.0 us)
Async XLA Ops:
  0.6 13.8 %copy-start = (bf16[768,768]{1,0:T(8,128)(2,1)S(1)}, bf16[768,768]{1,0:T(8,128)(2,1)}, u32[]{:S(2)}) copy-start(bf16[768,768]{1,0:T(8,128)(2,1)} %param.20) | copy-start | bytes 3538948
  2.4 6.8 %copy-start.5 = (s32[2,512]{1,0:T(2,128)S(1)}, s32[2,512]{1,0:T(2,128)}, u32[]{:S(2)}) copy-start(s32[2,512]{1,0:T(2,128)} %row_ref.1) | copy-start | bytes 12292
  2.4 12.1 %copy-start.2 = (bf16[512,768]{1,0:T(8,128)(2,1)S(1)}, bf16[512,768]{1,0:T(8,128)(2,1)}, u32[]{:S(2)}) copy-start(bf16[512,768]{1,0:T(8,128)(2,1)} %refs_13_.1) | copy-start | bytes 2359300
  2.4 13.8 %collective-permute-start.2 = (bf16[2,512,384]{2,1,0:T(8,128)(2,1)S(1)}, bf16[2,512,384]{2,1,0:T(8,128)(2,1)}, u32[]{:S(2)}, u32[]{:S(2)}) collective-permute-start(bf16[2,512,384]{2,1,0:T(8,128)(2,1)S(1)} %pad_maximum_fusion.1), channel_id=1, source_target_pairs={{0,1},{1,2},{2,3},{3,4},{4,5},{5,6},{6,7},{7,8},{8,9},{9,10},{10,1... | collective-permute-start | bytes 2359304 | tf_op jit(solution)/shard_map/ppermute | solution.py:42
  7.2 27.3 %collective-permute-start = (bf16[2,512,384]{2,1,0:T(8,128)(2,1)S(1)}, bf16[2,512,384]{2,1,0:T(8,128)(2,1)}, u32[]{:S(2)}, u32[]{:S(2)}) collective-permute-start(bf16[2,512,384]{2,1,0:T(8,128)(2,1)S(1)} %pad_maximum_fusion), channel_id=1, source_target_pairs={{0,1},{1,2},{2,3},{3,4},{4,5},{5,6},{6,7},{7,8},{8,9},{9,10},{10,1... | collective-permute-start | bytes 2359304 | tf_op jit(solution)/shard_map/ppermute | solution.py:42
  31.0 20.2 %copy-start.6 = (s32[1,1280]{1,0:T(1,128)S(1)}, s32[1,1280]{1,0:T(1,128)}, u32[]{:S(2)}) copy-start(s32[1,1280]{1,0:T(1,128)} %get-tuple-element.32) | copy-start | bytes 15364
  31.0 32.1 %copy-start.7 = (f32[768]{0:T(1024)S(1)}, f32[768]{0:T(1024)}, u32[]{:S(2)}) copy-start(f32[768]{0:T(1024)} %param.13) | copy-start | bytes 9220
  31.0 32.7 %collective-permute-start.3 = (bf16[2,512,384]{2,1,0:T(8,128)(2,1)}, bf16[2,512,384]{2,1,0:T(8,128)(2,1)S(1)}, u32[]{:S(2)}, u32[]{:S(2)}) collective-permute-start(bf16[2,512,384]{2,1,0:T(8,128)(2,1)} %get-tuple-element.26), channel_id=1, source_target_pairs={{1,0},{2,1},{3,2},{4,3},{5,4},{6,5},{7,6},{8,7},{9,8},{10,9},{11,1... | collective-permute-start | bytes 2359304 | tf_op jit(solution)/shard_map/ppermute | solution.py:42
  49.3 14.4 %collective-permute-start.1 = (bf16[2,512,384]{2,1,0:T(8,128)(2,1)}, bf16[2,512,384]{2,1,0:T(8,128)(2,1)S(1)}, u32[]{:S(2)}, u32[]{:S(2)}) collective-permute-start(bf16[2,512,384]{2,1,0:T(8,128)(2,1)} %get-tuple-element.22), channel_id=1, source_target_pairs={{1,0},{2,1},{3,2},{4,3},{5,4},{6,5},{7,6},{8,7},{9,8},{10,9},{11,1... | collective-permute-start | bytes 2359304 | tf_op jit(solution)/shard_map/ppermute | solution.py:42
  52.2 24.7 %all-to-all-start = ((s32[128,2,5]{2,1,0:T(2,128)}), s32[128,2,5]{2,1,0:T(2,128)S(1)}, u32[]{:S(2)}, u32[]{:S(2)}) async-start(s32[128,2,5]{2,1,0:T(2,128)} %reshape.27), calls=%async_computation | async-start | bytes 262144 | tf_op jit(solution)/shard_map/all_to_all | solution.py:361
  63.7 0.9 copy-start.3
  63.7 1.2 copy-start.4
  76.9 44.5 %all-to-all-start.1 = ((bf16[128,64,128]{2,1,0:T(8,128)(2,1)}), bf16[128,64,128]{2,1,0:T(8,128)(2,1)S(1)}, u32[]{:S(2)}, u32[]{:S(2)}) async-start(bf16[128,64,128]{2,1,0:T(8,128)(2,1)} %get-tuple-element.33), calls=%async_computation.1 | async-start | bytes 4194304 | tf_op jit(solution)/shard_map/all_to_all | solution.py:361
  121.3 1.3 %copy-start.1 = (bf16[128,64,128]{2,1,0:T(8,128)(2,1)}, bf16[128,64,128]{2,1,0:T(8,128)(2,1)S(1)}, u32[]{:S(2)}) copy-start(bf16[128,64,128]{2,1,0:T(8,128)(2,1)S(1)} %all-to-all-done.1.got_ref) | copy-start | bytes 6291460

commit v3 on v2

--- a/solution.py
+++ b/solution.py
@@ -131,34 +131,44 @@
     lane = iota((QT, LANES), 1)
     scale = HD ** (-0.5)
     zero = jnp.zeros((QT, LANES), BF16)
-    for tile in range(tiles):
+    steps = [(tile, half) for tile in range(tiles) for half in range(LANES // HD)]
+    rowlane = iota((LANES, QT), 0)
+
+    def open_step(step):
+        tile, half = step
         rows = slice(tile * QT, (tile + 1) * QT)
         span = slice(tile * QT, tile * QT + KT)
-        q = q_ref[rows, :] * jnp.asarray(scale, BF16)
-        da = da_ref[rows, :]
-        k = kx_ref[span, :]
-        v = vx_ref[span, :]
-        dq = dk = dv = None
-        for half in range(LANES // HD):
-            mine = (lane // HD) == half
-            qh = jnp.where(mine, q, zero)
-            dah = jnp.where(mine, da, zero)
-            score = dot(k, qh, 1, 1) + bias_ref[tile]
-            top = jnp.max(score, axis=0, keepdims=True)
-            expo = jnp.exp(score - top)
-            total = jnp.sum(expo, axis=0, keepdims=True)
-            prob = expo * (1.0 / total)
-            lowprob = prob.astype(BF16)
-            dprob = dot(v, dah, 1, 1)
-            delta = jnp.sum(lowprob.astype(F32) * dprob, axis=0, keepdims=True)
-            dscore = (prob * (dprob - delta)).astype(BF16)
-            dvh = dot(lowprob, dah, 1, 0)
-            dkh = dot(dscore, qh, 1, 0)
-            dqh = jnp.where(mine, dot(dscore, k, 0, 0), 0.0)
-            dv = dvh if dv is None else dv + dvh
-            dk = dkh if dk is None else dk + dkh
-            dq = dqh if dq is None else dq + dqh
-        dq_ref[rows, :] = (dq * scale).astype(BF16)
+        mine = (lane // HD) == half
+        qh = jnp.where(mine, q_ref[rows, :] * jnp.asarray(scale, BF16), zero)
+        dah = jnp.where(mine, da_ref[rows, :], zero)
+        score = dot(kx_ref[span, :], qh, 1, 1) + bias_ref[tile]
+        dprob = dot(vx_ref[span, :], dah, 1, 1)
+        return qh, dah, score, dprob
+
+    opened = {steps[0]: open_step(steps[0])}
+    held = {}
+    for n, step in enumerate(steps):
+        tile, half = step
+        rows = slice(tile * QT, (tile + 1) * QT)
+        span = slice(tile * QT, tile * QT + KT)
+        if n + 1 < len(steps):
+            opened[steps[n + 1]] = open_step(steps[n + 1])
+        qh, dah, score, dprob = opened.pop(step)
+        top = jnp.max(score, axis=0, keepdims=True)
+        expo = jnp.exp(score - top)
+        total = jnp.sum(expo, axis=0, keepdims=True)
+        prob = expo * (1.0 / total)
+        lowprob = prob.astype(BF16)
+        delta = jnp.sum(prob * dprob, axis=0, keepdims=True)
+        dscore = (prob * (dprob - delta)).astype(BF16)
+        dqh = jnp.where((rowlane // HD) == half, dot(kx_ref[span, :], dscore, 0, 0), 0.0)
+        if half == 0:
+            held = dict(lp=lowprob, ds=dscore, q=qh, da=dah, dq=dqh)
+            continue
+        dq = held["dq"] + dqh
+        dv = dot(jnp.concatenate([held["lp"], lowprob], axis=1), jnp.concatenate([held["da"], dah], axis=0), 1, 0)
+        dk = dot(jnp.concatenate([held["ds"], dscore], axis=1), jnp.concatenate([held["q"], qh], axis=0), 1, 0)
+        dq_ref[rows, :] = jnp.transpose(dq * scale).astype(BF16)
         if tile == 0:
             dk_ref[span, :] = dk
             dv_ref[span, :] = dv
@@ -222,32 +232,51 @@
 
 
 PACK = 32
+SPREAD = 16
 
 
 def finish_kernel(*refs):
     groups = len(GROUPS)
     parts = [refs[4 * g : 4 * g + 4] for g in range(groups)]
-    (wq_ref, wk_ref, wv_ref, hidden_ref, gain_ref, out_ref, slot_ref, gh_ref, sent_ref) = refs[
-        4 * groups :
-    ]
+    (
+        wq_in, wk_in, wv_in, hidden_in, out_in, gain_ref, slot_ref, gh_out, sent_out,
+        dq_ref, dk_ref, dv_ref, back_ref, wq_ref, wk_ref, wv_ref, hidden_ref, out_ref,
+        gh_ref, sent_ref, sems,
+    ) = refs[4 * groups :]
     count, width = hidden_ref.shape
-    grad_q = jnp.concatenate([dq[...] for dq, _, _, _ in parts], axis=1)
-    grad_k = jnp.concatenate(
-        [(dk[...] + back[0].astype(F32)).astype(BF16) for _, back, dk, _ in parts], axis=1
-    )
-    grad_v = jnp.concatenate(
-        [(dv[...] + back[1].astype(F32)).astype(BF16) for _, back, _, dv in parts], axis=1
-    )
-    norm = dot(grad_q, wq_ref[...], 1, 1)
-    norm = norm + dot(grad_k, wk_ref[...], 1, 1)
-    norm = norm + dot(grad_v, wv_ref[...], 1, 1)
-    full = hidden_ref[...].astype(F32)
-    inverse = lax.rsqrt(jnp.mean(full * full, axis=1, keepdims=True) + EPS)
-    unit = full * inverse
-    scaled = norm * gain_ref[...]
-    through = inverse * (scaled - unit * jnp.mean(scaled * unit, axis=1, keepdims=True))
-    grad_hidden = (out_ref[...].astype(F32) + through).astype(BF16)
-    gh_ref[...] = grad_hidden
+    devices = sent_ref.shape[0]
+    started = []
+
+    def bring(*pairs):
+        copies = []
+        for source, target in pairs:
+            copies.append(pltpu.make_async_copy(source, target, sems.at[len(started)]))
+            started.append(copies[-1])
+            copies[-1].start()
+        return copies
+
+    def arrive(copies):
+        for copy in copies:
+            copy.wait()
+
+    spans = []
+    at = 0
+    for pairs in GROUPS:
+        spans.append(slice(at * LANES, (at + pairs) * LANES))
+        at += pairs
+    need_hidden = bring((hidden_in, hidden_ref))
+    need_q = bring(*[(p[0], dq_ref.at[:, c]) for p, c in zip(parts, spans)], (wq_in, wq_ref))
+    need_k = bring(
+        *[(p[1].at[0], back_ref.at[0, :, c]) for p, c in zip(parts, spans)],
+        *[(p[2], dk_ref.at[:, c]) for p, c in zip(parts, spans)],
+        (wk_in, wk_ref),
+    )
+    need_v = bring(
+        *[(p[1].at[1], back_ref.at[1, :, c]) for p, c in zip(parts, spans)],
+        *[(p[3], dv_ref.at[:, c]) for p, c in zip(parts, spans)],
+        (wv_in, wv_ref),
+    )
+    need_out = bring((out_in, out_ref))
 
     def hits(place, at):
         hit = place == slot_ref[at : at + 1, :]
@@ -258,8 +287,32 @@
     blocks = width // LANES
     both = NG * MAIN
     tail = CHUNK - blocks * both
+    shape = (SPREAD * tail, blocks * SPREAD * NG)
+    row = iota((shape[0], 1), 0)
+    inner = lax.rem(row, tail)
+    source = (inner // NG) * (SPREAD * NG) + (row // tail) * NG + lax.rem(inner, NG)
+    lay = jnp.where((inner < blocks * NG) & (source == iota(shape, 1)), 1.0, 0.0).astype(BF16)
+
+    arrive(need_hidden)
+    full = hidden_ref[...].astype(F32)
+    inverse = lax.rsqrt(jnp.mean(full * full, axis=1, keepdims=True) + EPS)
+    arrive(need_q)
+    norm = dot(dq_ref[...], wq_ref[...], 1, 1)
+    arrive(need_k)
+    norm = norm + dot((dk_ref[...] + back_ref[0].astype(F32)).astype(BF16), wk_ref[...], 1, 1)
+    arrive(need_v)
+    norm = norm + dot((dv_ref[...] + back_ref[1].astype(F32)).astype(BF16), wv_ref[...], 1, 1)
+    arrive(need_out)
+    unit = hidden_ref[...].astype(F32) * inverse
+    scaled = norm * gain_ref[...]
+    through = inverse * (scaled - unit * jnp.mean(scaled * unit, axis=1, keepdims=True))
+    grad_hidden = (out_ref[...].astype(F32) + through).astype(BF16)
+    gh_ref[...] = grad_hidden
+    leaving = bring((gh_ref, gh_out))
+
     cut = lambda value, c: value[:, c * LANES : (c + 1) * LANES]
-    for at in range(0, sent_ref.shape[0], PACK):
+    rest = dot(hits(iota((devices * NG, count), 0), NG), grad_hidden, 1, 0).astype(BF16)
+    for at in range(0, devices, PACK):
         place = at * both + iota((PACK * both, count), 0)
         main = dot(hits(place, 0), grad_hidden, 1, 0)
         for c in range(0, blocks, 2):
@@ -267,33 +320,53 @@
             sent_ref[at : at + PACK, c * both : (c + 2) * both, :] = jnp.concatenate(
                 pair, axis=1
             ).astype(BF16)
-        rows = iota((PACK * tail, count), 0)
-        place = (at + rows // tail) * NG + lax.rem(rows, NG)
-        last = dot(hits(place, NG), grad_hidden, 1, 0)
-        block = lax.rem(iota((PACK * tail, LANES), 0), tail) // NG
-        value = jnp.zeros((PACK * tail, LANES), F32)
-        for c in range(blocks):
-            value = jnp.where(block == c, cut(last, c), value)
-        sent_ref[at : at + PACK, blocks * both :, :] = value.reshape(PACK, tail, LANES).astype(BF16)
+        for low in range(at, at + PACK, SPREAD):
+            some = rest[low * NG : (low + SPREAD) * NG]
+            some = jnp.concatenate([cut(some, c) for c in range(blocks)], axis=0)
+            sent_ref[low : low + SPREAD, blocks * both :, :] = (
+                dot(lay, some, 1, 0).reshape(SPREAD, tail, LANES).astype(BF16)
+            )
+        leaving += bring((sent_ref.at[at : at + PACK], sent_out.at[at : at + PACK]))
+    arrive(leaving)
 
 
 def finish(parts, wq, wk, wv, hidden, gain, grad_out, slot, devices):
     count, width = hidden.shape
+    groups = len(GROUPS)
+    place = pl.BlockSpec(memory_space=pl.ANY)
+    small = pl.BlockSpec(memory_space=pltpu.VMEM)
+    copies = 5 * groups + 6 + devices // PACK
     return pl.pallas_call(
         finish_kernel,
+        in_specs=[place] * (4 * groups + 5) + [small] * 2,
+        out_specs=(place, place),
         out_shape=(
             jax.ShapeDtypeStruct((count, width), BF16),
             jax.ShapeDtypeStruct((devices, CHUNK, LANES), BF16),
         ),
+        scratch_shapes=[
+            pltpu.VMEM((count, width), BF16),
+            pltpu.VMEM((count, width), F32),
+            pltpu.VMEM((count, width), F32),
+            pltpu.VMEM((2, WINDOW, width), BF16),
+            pltpu.VMEM((width, width), BF16),
+            pltpu.VMEM((width, width), BF16),
+            pltpu.VMEM((width, width), BF16),
+            pltpu.VMEM((count, width), BF16),
+            pltpu.VMEM((count, width), BF16),
+            pltpu.VMEM((count, width), BF16),
+            pltpu.VMEM((devices, CHUNK, LANES), BF16),
+            pltpu.SemaphoreType.DMA((copies,)),
+        ],
         compiler_params=params(56),
         name="finish",
     )(
         *[array for part in parts for array in part],
-        wq, wk, wv, hidden, gain.reshape(1, width), grad_out, slot,
-    )
-
-
-COLLECT = 512
+        wq, wk, wv, hidden, grad_out, gain.reshape(1, width), slot,
+    )
+
+
+COLLECT = 1024
 APART = 16
 
 

time: 133 us -> 126 us (0.947)
  Pallas kernels: 56.2 us -> 48.7 us
    pallas_call x2, Pallas kernels: 29.6 us -> 24.8 us  [attention_grads(): pl.pallas_call(attention_kernel, grid=(pairs,), in_specs=[pl.BlockSpec(me...]
    pallas_call x1, Pallas kernels: 11.9 us -> 9.92 us  [finish(): pl.pallas_call(finish_kernel, in_specs=[place] * (4 * groups + 5) + [smal...]
  transfers between devices with their start and end apart: 6 -> 6, of which waited for: 1 -> 1; matrix products, arithmetic and copies ran while one was open for 4% -> 4% of each run, Pallas kernels for 35% -> 31%
where the time goes in v3:
time: 126 us; the launch traced here: 125 us
  Pallas kernels  48.7 us (39%)
  starting transfers between devices  36.7 us (29%)
  waiting for transfers between devices  29.2 us (23%)
  local copies, waits for them, and re-layouts  7.78 us (6%)
  matrix products  1.69 us (1%)
    all_to_all x2, waiting for transfers between devices, exchanged(): return lax.all_to_all(part, AXES, split_axis=0, concat_axis=0, tiled=True)  29.2 us
    all_to_all x2, starting transfers between devices, exchanged(): return lax.all_to_all(part, AXES, split_axis=0, concat_axis=0, tiled=True)  24.9 us
    pallas_call x2, Pallas kernels, attention_grads(): pl.pallas_call(attention_kernel, grid=(pairs,), in_specs=[pl.BlockSpec(me...  24.8 us
    ppermute x4, starting transfers between devices, shifted(): return lax.ppermute(shard, AXES, pairs)  11.8 us
    pallas_call x1, Pallas kernels, finish(): pl.pallas_call(finish_kernel, in_specs=[place] * (4 * groups + 5) + [smal...  9.92 us
    pallas_call x1, Pallas kernels, collect(): pl.pallas_call(collect_kernel, grid=(tables, ROWS_DEV // COLLECT), in_spe...  9.51 us
    pallas_call x1, Pallas kernels, make_slots(): pl.pallas_call(slots_kernel, in_specs=[pl.BlockSpec(memory_space=pltpu.SM...  4.44 us
    unnamed x17, local copies, waits for them, and re-layouts  3.39 us
  transfers between devices with their start and end apart: 6, of which 1 were waited for; matrix products, arithmetic and copies ran while one was open for 4% of the time, Pallas kernels for 31%

profile of v3, /device:TPU:1, one launch (start us, length us, event | category | flops | bytes accessed | tf_op | source)
XLA Modules:
  0.0 125.1 jit_solution(5308091131319436034)
XLA Ops:
  0.6 0.0 copy-start
  0.6 1.6 %slice_bitcast_fusion = (bf16[1,512,384]{2,1,0:T(8,128)(2,1)S(1)}, bf16[1,512,384]{2,1,0:T(8,128)(2,1)S(1)}, bf16[1,512,384]{2,1,0:T(8,128)(2,1)S(1)}, bf16[1,512,384]{2,1,0:T(8,128)(2,1)S(1)}) fusion(bf16[512,768]{1,0:T(8,128)(2,1)} %vo_ref.3, bf16[512,768]{1,0:T(8,128)(2,1)} %ko_ref.3), kind=kLoop, calls=%fused_computation.3 | loop fusion | bytes 3145728 | tf_op jit(solution)/shard_map/stack | solution.py:458
  2.3 0.1 pad_maximum_fusion.1
  2.4 0.0 copy-start.5
  2.4 0.0 copy-start.2
  2.4 4.7 %collective-permute-start.2 = (bf16[2,512,384]{2,1,0:T(8,128)(2,1)S(1)}, bf16[2,512,384]{2,1,0:T(8,128)(2,1)}, u32[]{:S(2)}, u32[]{:S(2)}) collective-permute-start(bf16[2,512,384]{2,1,0:T(8,128)(2,1)S(1)} %pad_maximum_fusion.1), channel_id=1, source_target_pairs={{0,1},{1,2},{2,3},{3,4},{4,5},{5,6},{6,7},{7,8},{8,9},{9,10},{10,1... | collective-permute-start | bytes 2359304 | tf_op jit(solution)/shard_map/ppermute | solution.py:42
  7.1 0.1 pad_maximum_fusion
  7.2 1.9 %collective-permute-start = (bf16[2,512,384]{2,1,0:T(8,128)(2,1)S(1)}, bf16[2,512,384]{2,1,0:T(8,128)(2,1)}, u32[]{:S(2)}, u32[]{:S(2)}) collective-permute-start(bf16[2,512,384]{2,1,0:T(8,128)(2,1)S(1)} %pad_maximum_fusion), channel_id=1, source_target_pairs={{0,1},{1,2},{2,3},{3,4},{4,5},{5,6},{6,7},{7,8},{8,9},{9,10},{10,1... | collective-permute-start | bytes 2359304 | tf_op jit(solution)/shard_map/ppermute | solution.py:42
  9.1 0.0 copy-done.5
  9.2 0.9 copy.25
  10.0 4.4 %slots.1 = (s32[4,512]{1,0:T(4,128)}, s32[1,1280]{1,0:T(1,128)}) custom-call(s32[1]{0:T(128)} %bitcast.first_ref, s32[2,512]{1,0:T(2,128)} %row_ref.1, s32[512,2]{1,0:T(8,128)} %bitcast.17), custom_call_target="tpu_custom_call" | custom-call | tf_op jit(solution)/shard_map/slots/pallas_call | solution.py:84
  14.5 0.0 copy-done
  14.5 0.0 copy-done.2
  14.5 1.7 %convolution_convert_fusion.da_ref = bf16[512,768]{1,0:T(8,128)(2,1)} fusion(bf16[512,768]{1,0:T(8,128)(2,1)S(1)} %copy-done.2, bf16[768,768]{1,0:T(8,128)(2,1)S(1)} %copy-done), kind=kOutput, calls=%fused_computation | convolution fusion | flops 604372992 | bytes 2752512 | tf_op jit(solution)/shard_map/dot_general | solution.py:30
  16.2 0.0 collective-permute-done.2.kp_ref.vp_ref
  16.2 12.4 %attention.3 = (bf16[512,384]{1,0:T(8,128)(2,1)}, bf16[2,512,384]{2,1,0:T(8,128)(2,1)}, f32[512,384]{1,0:T(8,128)}, f32[512,384]{1,0:T(8,128)}) custom-call(s32[1]{0:T(128)} %bitcast.first_ref, s32[1,64]{1,0:T(1,128)} %bitcast.21, bf16[512,768]{1,0:T(8,128)(2,1)} %q_ref.3, bf16[2,512,384]{2,1,0:T(8,128)(2,1)} %collective-permute-done.2.kp_ref.vp_ref, ...), custom_call_target="tpu_custom_call" | custom-call | flops 1509949440 | bytes 3932160 | tf_op jit(solution)/shard_map/attention/pallas_call | solution.py:198
  28.6 0.0 copy-start.6
  28.6 0.0 copy-start.7
  28.6 3.3 %collective-permute-start.3 = (bf16[2,512,384]{2,1,0:T(8,128)(2,1)}, bf16[2,512,384]{2,1,0:T(8,128)(2,1)S(1)}, u32[]{:S(2)}, u32[]{:S(2)}) collective-permute-start(bf16[2,512,384]{2,1,0:T(8,128)(2,1)} %get-tuple-element.26), channel_id=1, source_target_pairs={{1,0},{2,1},{3,2},{4,3},{5,4},{6,5},{7,6},{8,7},{9,8},{10,9},{11,1... | collective-permute-start | bytes 2359304 | tf_op jit(solution)/shard_map/ppermute | solution.py:42
  31.9 0.0 collective-permute-done.kp_ref.vp_ref
  31.9 12.4 %attention.2 = (bf16[512,384]{1,0:T(8,128)(2,1)}, bf16[2,512,384]{2,1,0:T(8,128)(2,1)}, f32[512,384]{1,0:T(8,128)}, f32[512,384]{1,0:T(8,128)}) custom-call(s32[1]{0:T(128)} %bitcast.first_ref, s32[1,64]{1,0:T(1,128)} %bitcast.22, bf16[512,768]{1,0:T(8,128)(2,1)} %q_ref.3, bf16[2,512,384]{2,1,0:T(8,128)(2,1)} %collective-permute-done.kp_ref.vp_ref, ...), custom_call_target="tpu_custom_call" | custom-call | flops 1509949440 | bytes 3932160 | tf_op jit(solution)/shard_map/attention/pallas_call | solution.py:198
  44.3 1.9 %collective-permute-start.1 = (bf16[2,512,384]{2,1,0:T(8,128)(2,1)}, bf16[2,512,384]{2,1,0:T(8,128)(2,1)S(1)}, u32[]{:S(2)}, u32[]{:S(2)}) collective-permute-start(bf16[2,512,384]{2,1,0:T(8,128)(2,1)} %get-tuple-element.22), channel_id=1, source_target_pairs={{1,0},{2,1},{3,2},{4,3},{5,4},{6,5},{7,6},{8,7},{9,8},{10,9},{11,1... | collective-permute-start | bytes 2359304 | tf_op jit(solution)/shard_map/ppermute | solution.py:42
  46.2 0.0 copy-done.6
  46.2 0.9 reshape.27
  47.2 10.9 %all-to-all-start = ((s32[128,2,5]{2,1,0:T(2,128)}), s32[128,2,5]{2,1,0:T(2,128)S(1)}, u32[]{:S(2)}, u32[]{:S(2)}) async-start(s32[128,2,5]{2,1,0:T(2,128)} %reshape.27), calls=%async_computation | async-start | bytes 262144 | tf_op jit(solution)/shard_map/all_to_all | solution.py:434
  58.1 0.0 copy-done.7
  58.1 0.6 reshape.26.refs_13_
  58.7 0.0 collective-permute-done.3.refs_5_
  58.7 0.0 copy-start.3
  58.7 0.0 collective-permute-done.1.refs_1_
  58.7 0.0 copy-start.4
  58.7 0.9 copy-done.3
  59.6 0.3 copy-done.4
  59.9 9.9 %finish.1 = (bf16[512,768]{1,0:T(8,128)(2,1)}, bf16[128,64,128]{2,1,0:T(8,128)(2,1)}) custom-call(bf16[512,384]{1,0:T(8,128)(2,1)} %get-tuple-element.21.refs_0_, bf16[2,512,384]{2,1,0:T(8,128)(2,1)} %copy-done.4, f32[512,384]{1,0:T(8,128)} %get-tuple-element.23.refs_2_, f32[512,384]{1,0:T(8,128)} %get-tuple-element.24.refs_3_, ...), custom_call_target="tpu_custom_call" | custom-call | tf_op jit(solution)/shard_map/finish/pallas_call | solution.py:339
  69.8 0.0 all-to-all-done
  69.8 13.9 %all-to-all-start.1 = ((bf16[128,64,128]{2,1,0:T(8,128)(2,1)}), bf16[128,64,128]{2,1,0:T(8,128)(2,1)S(1)}, u32[]{:S(2)}, u32[]{:S(2)}) async-start(bf16[128,64,128]{2,1,0:T(8,128)(2,1)} %get-tuple-element.33), calls=%async_computation.1 | async-start | bytes 4194304 | tf_op jit(solution)/shard_map/all_to_all | solution.py:434
  83.8 0.1 copy.26
  83.8 0.1 copy.27
  84.0 0.1 stack.31
  84.1 0.1 copy.28
  84.2 0.1 rev.3
  84.3 0.1 stack.32
  84.5 0.6 broadcast_in_dim.3.label_ref
  85.1 29.2 %all-to-all-done.1.got_ref = bf16[128,64,128]{2,1,0:T(8,128)(2,1)S(1)} async-done(((bf16[128,64,128]{2,1,0:T(8,128)(2,1)}), bf16[128,64,128]{2,1,0:T(8,128)(2,1)S(1)}, u32[]{:S(2)}, u32[]{:S(2)}) %all-to-all-start.1) | async-done | bytes 2097184 | tf_op jit(solution)/shard_map/all_to_all | solution.py:434
  114.3 0.0 copy-start.1
  114.3 1.3 %copy-done.1 = bf16[128,64,128]{2,1,0:T(8,128)(2,1)} copy-done((bf16[128,64,128]{2,1,0:T(8,128)(2,1)}, bf16[128,64,128]{2,1,0:T(8,128)(2,1)S(1)}, u32[]{:S(2)}) %copy-start.1) | copy-done | bytes 2097176
  115.6 9.5 %collect.1 = bf16[2,2048,768]{2,1,0:T(8,128)(2,1)} custom-call(s32[2,1,640]{2,1,0:T(1,128)} %broadcast_in_dim.3.label_ref, bf16[128,64,128]{2,1,0:T(8,128)(2,1)} %copy-done.1), custom_call_target="tpu_custom_call" | custom-call | tf_op jit(solution)/shard_map/collect/pallas_call | solution.py:418
  (4 shorter events, 0.0 us)
Async XLA Ops:
  0.6 13.8 %copy-start = (bf16[768,768]{1,0:T(8,128)(2,1)S(1)}, bf16[768,768]{1,0:T(8,128)(2,1)}, u32[]{:S(2)}) copy-start(bf16[768,768]{1,0:T(8,128)(2,1)} %param.20) | copy-start | bytes 3538948
  2.4 6.8 %copy-start.5 = (s32[2,512]{1,0:T(2,128)S(1)}, s32[2,512]{1,0:T(2,128)}, u32[]{:S(2)}) copy-start(s32[2,512]{1,0:T(2,128)} %row_ref.1) | copy-start | bytes 12292
  2.4 12.1 %copy-start.2 = (bf16[512,768]{1,0:T(8,128)(2,1)S(1)}, bf16[512,768]{1,0:T(8,128)(2,1)}, u32[]{:S(2)}) copy-start(bf16[512,768]{1,0:T(8,128)(2,1)} %refs_12_.1) | copy-start | bytes 2359300
  2.4 13.8 %collective-permute-start.2 = (bf16[2,512,384]{2,1,0:T(8,128)(2,1)S(1)}, bf16[2,512,384]{2,1,0:T(8,128)(2,1)}, u32[]{:S(2)}, u32[]{:S(2)}) collective-permute-start(bf16[2,512,384]{2,1,0:T(8,128)(2,1)S(1)} %pad_maximum_fusion.1), channel_id=1, source_target_pairs={{0,1},{1,2},{2,3},{3,4},{4,5},{5,6},{6,7},{7,8},{8,9},{9,10},{10,1... | collective-permute-start | bytes 2359304 | tf_op jit(solution)/shard_map/ppermute | solution.py:42
  7.2 24.7 %collective-permute-start = (bf16[2,512,384]{2,1,0:T(8,128)(2,1)S(1)}, bf16[2,512,384]{2,1,0:T(8,128)(2,1)}, u32[]{:S(2)}, u32[]{:S(2)}) collective-permute-start(bf16[2,512,384]{2,1,0:T(8,128)(2,1)S(1)} %pad_maximum_fusion), channel_id=1, source_target_pairs={{0,1},{1,2},{2,3},{3,4},{4,5},{5,6},{6,7},{7,8},{8,9},{9,10},{10,1... | collective-permute-start | bytes 2359304 | tf_op jit(solution)/shard_map/ppermute | solution.py:42
  28.6 17.6 %copy-start.6 = (s32[1,1280]{1,0:T(1,128)S(1)}, s32[1,1280]{1,0:T(1,128)}, u32[]{:S(2)}) copy-start(s32[1,1280]{1,0:T(1,128)} %get-tuple-element.32) | copy-start | bytes 15364
  28.6 29.5 %copy-start.7 = (f32[768]{0:T(1024)S(1)}, f32[768]{0:T(1024)}, u32[]{:S(2)}) copy-start(f32[768]{0:T(1024)} %param.13) | copy-start | bytes 9220
  28.6 30.1 %collective-permute-start.3 = (bf16[2,512,384]{2,1,0:T(8,128)(2,1)}, bf16[2,512,384]{2,1,0:T(8,128)(2,1)S(1)}, u32[]{:S(2)}, u32[]{:S(2)}) collective-permute-start(bf16[2,512,384]{2,1,0:T(8,128)(2,1)} %get-tuple-element.26), channel_id=1, source_target_pairs={{1,0},{2,1},{3,2},{4,3},{5,4},{6,5},{7,6},{8,7},{9,8},{10,9},{11,1... | collective-permute-start | bytes 2359304 | tf_op jit(solution)/shard_map/ppermute | solution.py:42
  44.3 14.4 %collective-permute-start.1 = (bf16[2,512,384]{2,1,0:T(8,128)(2,1)}, bf16[2,512,384]{2,1,0:T(8,128)(2,1)S(1)}, u32[]{:S(2)}, u32[]{:S(2)}) collective-permute-start(bf16[2,512,384]{2,1,0:T(8,128)(2,1)} %get-tuple-element.22), channel_id=1, source_target_pairs={{1,0},{2,1},{3,2},{4,3},{5,4},{6,5},{7,6},{8,7},{9,8},{10,9},{11,1... | collective-permute-start | bytes 2359304 | tf_op jit(solution)/shard_map/ppermute | solution.py:42
  47.2 22.7 %all-to-all-start = ((s32[128,2,5]{2,1,0:T(2,128)}), s32[128,2,5]{2,1,0:T(2,128)S(1)}, u32[]{:S(2)}, u32[]{:S(2)}) async-start(s32[128,2,5]{2,1,0:T(2,128)} %reshape.27), calls=%async_computation | async-start | bytes 262144 | tf_op jit(solution)/shard_map/all_to_all | solution.py:434
  58.7 0.9 copy-start.3
  58.7 1.2 copy-start.4
  69.8 44.5 %all-to-all-start.1 = ((bf16[128,64,128]{2,1,0:T(8,128)(2,1)}), bf16[128,64,128]{2,1,0:T(8,128)(2,1)S(1)}, u32[]{:S(2)}, u32[]{:S(2)}) async-start(bf16[128,64,128]{2,1,0:T(8,128)(2,1)} %get-tuple-element.33), calls=%async_computation.1 | async-start | bytes 4194304 | tf_op jit(solution)/shard_map/all_to_all | solution.py:434
  114.3 1.3 %copy-start.1 = (bf16[128,64,128]{2,1,0:T(8,128)(2,1)}, bf16[128,64,128]{2,1,0:T(8,128)(2,1)S(1)}, u32[]{:S(2)}) copy-start(bf16[128,64,128]{2,1,0:T(8,128)(2,1)S(1)} %all-to-all-done.1.got_ref) | copy-start | bytes 6291460

commit v4 on v3

--- a/solution.py
+++ b/solution.py
@@ -19,7 +19,7 @@
 BF16 = jnp.bfloat16
 F32 = jnp.float32
 I32 = jnp.int32
-GROUPS = (3, 3)
+GROUPS = (4, 2)
 
 
 def iota(shape, dim):
@@ -145,29 +145,27 @@
         dprob = dot(vx_ref[span, :], dah, 1, 1)
         return qh, dah, score, dprob
 
-    opened = {steps[0]: open_step(steps[0])}
-    held = {}
-    for n, step in enumerate(steps):
-        tile, half = step
-        rows = slice(tile * QT, (tile + 1) * QT)
-        span = slice(tile * QT, tile * QT + KT)
-        if n + 1 < len(steps):
-            opened[steps[n + 1]] = open_step(steps[n + 1])
-        qh, dah, score, dprob = opened.pop(step)
+    def soften(opened):
+        qh, dah, score, dprob = opened
         top = jnp.max(score, axis=0, keepdims=True)
         expo = jnp.exp(score - top)
         total = jnp.sum(expo, axis=0, keepdims=True)
         prob = expo * (1.0 / total)
-        lowprob = prob.astype(BF16)
-        delta = jnp.sum(prob * dprob, axis=0, keepdims=True)
-        dscore = (prob * (dprob - delta)).astype(BF16)
-        dqh = jnp.where((rowlane // HD) == half, dot(kx_ref[span, :], dscore, 0, 0), 0.0)
-        if half == 0:
-            held = dict(lp=lowprob, ds=dscore, q=qh, da=dah, dq=dqh)
-            continue
-        dq = held["dq"] + dqh
-        dv = dot(jnp.concatenate([held["lp"], lowprob], axis=1), jnp.concatenate([held["da"], dah], axis=0), 1, 0)
-        dk = dot(jnp.concatenate([held["ds"], dscore], axis=1), jnp.concatenate([held["q"], qh], axis=0), 1, 0)
+        both = prob * dprob
+        delta = jnp.sum(both, axis=0, keepdims=True)
+        return qh, dah, prob.astype(BF16), (both - prob * delta).astype(BF16)
+
+    def close(tile, first_half, second_half):
+        rows = slice(tile * QT, (tile + 1) * QT)
+        span = slice(tile * QT, tile * QT + KT)
+        q0, da0, p0, s0 = first_half
+        q1, da1, p1, s1 = second_half
+        joined = lambda x, y, axis: jnp.concatenate([x, y], axis=axis)
+        dv = dot(joined(p0, p1, 1), joined(da0, da1, 0), 1, 0)
+        ds = joined(s0, s1, 1)
+        dk = dot(ds, joined(q0, q1, 0), 1, 0)
+        dq = dot(kx_ref[span, :], ds, 0, 0)
+        dq = jnp.where(rowlane < HD, dq[:, :QT], dq[:, QT:])
         dq_ref[rows, :] = jnp.transpose(dq * scale).astype(BF16)
         if tile == 0:
             dk_ref[span, :] = dk
@@ -180,6 +178,16 @@
             dv_ref[seen, :] += dv[:both]
             dk_ref[fresh, :] = dk[both:]
             dv_ref[fresh, :] = dv[both:]
+
+    opened = open_step(steps[0])
+    soft = []
+    for n, (tile, half) in enumerate(steps):
+        later = open_step(steps[n + 1]) if n + 1 < len(steps) else None
+        soft.append(soften(opened))
+        opened = later
+        if half == 1:
+            close(tile, soft[-2], soft[-1])
+    pass
     back_ref[0] = dk_ref[:WINDOW].astype(BF16)
     back_ref[1] = dv_ref[:WINDOW].astype(BF16)
     dko_ref[...] = dk_ref[WINDOW:]
@@ -425,7 +433,7 @@
         out_specs=pl.BlockSpec((1, COLLECT, width), lambda t, i: (t, i, 0)),
         out_shape=jax.ShapeDtypeStruct((tables, ROWS_DEV, width), BF16),
         scratch_shapes=[pltpu.VMEM((tables, number, width), BF16)],
-        compiler_params=params(56),
+        compiler_params=params(28),
         name="collect",
     )(labels, got)
 

time: 126 us -> 120 us (0.952)
  Pallas kernels: 48.7 us -> 44.3 us
  starting transfers between devices: 36.7 us -> 33.3 us
  waiting for transfers between devices: 29.2 us -> 30.6 us
    pallas_call x2, Pallas kernels: 24.8 us -> 22.1 us  [attention_grads(): pl.pallas_call(attention_kernel, grid=(pairs,), in_specs=[pl.BlockSpec(me...]
    all_to_all x2, starting transfers between devices: 24.9 us -> 22.9 us  [exchanged(): return lax.all_to_all(part, AXES, split_axis=0, concat_axis=0, tiled=True)]
    pallas_call x1, Pallas kernels: 9.51 us -> 7.88 us  [collect(): pl.pallas_call(collect_kernel, grid=(tables, ROWS_DEV // COLLECT), in_spe...]
    ppermute x4, starting transfers between devices: 11.8 us -> 10.5 us  [shifted(): return lax.ppermute(shard, AXES, pairs)]
  transfers between devices with their start and end apart: 6 -> 6, of which waited for: 1 -> 2; matrix products, arithmetic and copies ran while one was open for 4% -> 6% of each run, Pallas kernels for 31% -> 31%
where the time goes in v4:
time: 120 us; the launch traced here: 119 us
  Pallas kernels  44.3 us (37%)
  starting transfers between devices  33.3 us (28%)
  waiting for transfers between devices  30.6 us (26%)
  local copies, waits for them, and re-layouts  7.51 us (6%)
  matrix products  1.69 us (1%)
    all_to_all x2, waiting for transfers between devices, exchanged(): return lax.all_to_all(part, AXES, split_axis=0, concat_axis=0, tiled=True)  29.8 us
    all_to_all x2, starting transfers between devices, exchanged(): return lax.all_to_all(part, AXES, split_axis=0, concat_axis=0, tiled=True)  22.9 us
    pallas_call x2, Pallas kernels, attention_grads(): pl.pallas_call(attention_kernel, grid=(pairs,), in_specs=[pl.BlockSpec(me...  22.1 us
    ppermute x4, starting transfers between devices, shifted(): return lax.ppermute(shard, AXES, pairs)  10.5 us
    pallas_call x1, Pallas kernels, finish(): pl.pallas_call(finish_kernel, in_specs=[place] * (4 * groups + 5) + [smal...  9.92 us
    pallas_call x1, Pallas kernels, collect(): pl.pallas_call(collect_kernel, grid=(tables, ROWS_DEV // COLLECT), in_spe...  7.88 us
    pallas_call x1, Pallas kernels, make_slots(): pl.pallas_call(slots_kernel, in_specs=[pl.BlockSpec(memory_space=pltpu.SM...  4.44 us
    unnamed x17, local copies, waits for them, and re-layouts  2.83 us
  transfers between devices with their start and end apart: 6, of which 2 were waited for; matrix products, arithmetic and copies ran while one was open for 6% of the time, Pallas kernels for 31%

profile of v4, /device:TPU:1, one launch (start us, length us, event | category | flops | bytes accessed | tf_op | source)
XLA Modules:
  0.0 119.4 jit_solution(14567009556369375088)
XLA Ops:
  0.6 0.0 copy-start
  0.6 1.4 %slice_bitcast_fusion = (bf16[1,512,512]{2,1,0:T(8,128)(2,1)S(1)}, bf16[1,512,512]{2,1,0:T(8,128)(2,1)S(1)}) fusion(bf16[512,768]{1,0:T(8,128)(2,1)} %vo_ref.3, bf16[512,768]{1,0:T(8,128)(2,1)} %ko_ref.3), kind=kLoop, calls=%fused_computation.3 | loop fusion | bytes 2097152 | tf_op jit(solution)/shard_map/stack | solution.py:466
  2.0 0.1 pad_maximum_fusion
  2.1 0.0 copy-start.5
  2.1 0.0 copy-start.3
  2.1 4.7 %collective-permute-start = (bf16[2,512,512]{2,1,0:T(8,128)(2,1)S(1)}, bf16[2,512,512]{2,1,0:T(8,128)(2,1)}, u32[]{:S(2)}, u32[]{:S(2)}) collective-permute-start(bf16[2,512,512]{2,1,0:T(8,128)(2,1)S(1)} %pad_maximum_fusion), channel_id=1, source_target_pairs={{0,1},{1,2},{2,3},{3,4},{4,5},{5,6},{6,7},{7,8},{8,9},{9,10},{10,1... | collective-permute-start | bytes 3145736 | tf_op jit(solution)/shard_map/ppermute | solution.py:42
  6.9 1.1 slice_bitcast_fusion.2
  8.0 0.8 pad_maximum_fusion.1
  8.8 1.9 %collective-permute-start.2 = (bf16[2,512,256]{2,1,0:T(8,128)(2,1)}, bf16[2,512,256]{2,1,0:T(8,128)(2,1)S(1)}, u32[]{:S(2)}, u32[]{:S(2)}) collective-permute-start(bf16[2,512,256]{2,1,0:T(8,128)(2,1)} %pad_maximum_fusion.1), channel_id=1, source_target_pairs={{0,1},{1,2},{2,3},{3,4},{4,5},{5,6},{6,7},{7,8},{8,9},{9,10},{10,1... | collective-permute-start | bytes 1572872 | tf_op jit(solution)/shard_map/ppermute | solution.py:42
  10.7 0.0 copy-done.5
  10.7 0.9 copy.25
  11.6 4.4 %slots.1 = (s32[4,512]{1,0:T(4,128)}, s32[1,1280]{1,0:T(1,128)}) custom-call(s32[1]{0:T(128)} %bitcast.first_ref, s32[2,512]{1,0:T(2,128)} %row_ref.1, s32[512,2]{1,0:T(8,128)} %bitcast.17), custom_call_target="tpu_custom_call" | custom-call | tf_op jit(solution)/shard_map/slots/pallas_call | solution.py:84
  16.0 0.0 copy-done
  16.0 0.0 copy-done.3
  16.0 1.7 %convolution_convert_fusion.da_ref = bf16[512,768]{1,0:T(8,128)(2,1)} fusion(bf16[512,768]{1,0:T(8,128)(2,1)S(1)} %copy-done.3, bf16[768,768]{1,0:T(8,128)(2,1)S(1)} %copy-done), kind=kOutput, calls=%fused_computation | convolution fusion | flops 604372992 | bytes 2752512 | tf_op jit(solution)/shard_map/dot_general | solution.py:30
  17.7 0.9 collective-permute-done.kp_ref.vp_ref
  18.6 14.0 %attention.2 = (bf16[512,512]{1,0:T(8,128)(2,1)}, bf16[2,512,512]{2,1,0:T(8,128)(2,1)}, f32[512,512]{1,0:T(8,128)}, f32[512,512]{1,0:T(8,128)}) custom-call(s32[1]{0:T(128)} %bitcast.first_ref, s32[1,64]{1,0:T(1,128)} %bitcast.21, bf16[512,768]{1,0:T(8,128)(2,1)} %q_ref.3, bf16[2,512,512]{2,1,0:T(8,128)(2,1)} %collective-permute-done.kp_ref.vp_ref, ...), custom_call_target="tpu_custom_call" | custom-call | flops 2013265920 | bytes 5242880 | tf_op jit(solution)/shard_map/attention/pallas_call | solution.py:206
  32.6 0.0 copy-start.6
  32.6 0.0 copy-start.7
  32.6 1.9 %collective-permute-start.1 = (bf16[2,512,512]{2,1,0:T(8,128)(2,1)}, bf16[2,512,512]{2,1,0:T(8,128)(2,1)S(1)}, u32[]{:S(2)}, u32[]{:S(2)}) collective-permute-start(bf16[2,512,512]{2,1,0:T(8,128)(2,1)} %get-tuple-element.22), channel_id=1, source_target_pairs={{1,0},{2,1},{3,2},{4,3},{5,4},{6,5},{7,6},{8,7},{9,8},{10,9},{11,1... | collective-permute-start | bytes 3145736 | tf_op jit(solution)/shard_map/ppermute | solution.py:42
  34.5 0.0 collective-permute-done.2.kp_ref.vp_ref
  34.5 0.0 copy-start.1
  34.5 0.8 copy-done.1
  35.3 8.2 %attention.3 = (bf16[512,256]{1,0:T(8,128)(2,1)}, bf16[2,512,256]{2,1,0:T(8,128)(2,1)}, f32[512,256]{1,0:T(8,128)}, f32[512,256]{1,0:T(8,128)}) custom-call(s32[1]{0:T(128)} %bitcast.first_ref, s32[1,64]{1,0:T(1,128)} %bitcast.22, bf16[512,768]{1,0:T(8,128)(2,1)} %q_ref.3, bf16[2,512,256]{2,1,0:T(8,128)(2,1)} %copy-done.1, bf16[512,768]{1,0:T(8,128)(2,1)} %ko_ref.3, ...), custom_call_target="tpu_custom_call" | custom-call | flops 1006632960 | bytes 2621440 | tf_op jit(solution)/shard_map/attention/pallas_call | solution.py:206
  43.5 1.9 %collective-permute-start.3 = (bf16[2,512,256]{2,1,0:T(8,128)(2,1)}, bf16[2,512,256]{2,1,0:T(8,128)(2,1)S(1)}, u32[]{:S(2)}, u32[]{:S(2)}) collective-permute-start(bf16[2,512,256]{2,1,0:T(8,128)(2,1)} %get-tuple-element.26), channel_id=1, source_target_pairs={{1,0},{2,1},{3,2},{4,3},{5,4},{6,5},{7,6},{8,7},{9,8},{10,9},{11,1... | collective-permute-start | bytes 1572872 | tf_op jit(solution)/shard_map/ppermute | solution.py:42
  45.4 0.0 copy-done.6
  45.4 0.9 reshape.27
  46.4 12.4 %all-to-all-start = ((s32[128,2,5]{2,1,0:T(2,128)}), s32[128,2,5]{2,1,0:T(2,128)S(1)}, u32[]{:S(2)}, u32[]{:S(2)}) async-start(s32[128,2,5]{2,1,0:T(2,128)} %reshape.27), calls=%async_computation | async-start | bytes 262144 | tf_op jit(solution)/shard_map/all_to_all | solution.py:442
  58.8 0.0 copy-done.7
  58.8 0.6 reshape.26.refs_13_
  59.4 0.0 collective-permute-done.3.refs_5_
  59.4 0.0 copy-start.4
  59.4 0.0 collective-permute-done.1.refs_1_
  59.4 0.0 copy-start.2
  59.4 0.8 copy-done.4
  60.2 0.4 copy-done.2
  60.6 9.9 %finish.1 = (bf16[512,768]{1,0:T(8,128)(2,1)}, bf16[128,64,128]{2,1,0:T(8,128)(2,1)}) custom-call(bf16[512,512]{1,0:T(8,128)(2,1)} %get-tuple-element.21.refs_0_, bf16[2,512,512]{2,1,0:T(8,128)(2,1)} %copy-done.2, f32[512,512]{1,0:T(8,128)} %get-tuple-element.23.refs_2_, f32[512,512]{1,0:T(8,128)} %get-tuple-element.24.refs_3_, ...), custom_call_target="tpu_custom_call" | custom-call | tf_op jit(solution)/shard_map/finish/pallas_call | solution.py:347
  70.5 0.0 all-to-all-done
  70.5 10.4 %all-to-all-start.1 = ((bf16[128,64,128]{2,1,0:T(8,128)(2,1)}), bf16[128,64,128]{2,1,0:T(8,128)(2,1)S(1)}, u32[]{:S(2)}, u32[]{:S(2)}) async-start(bf16[128,64,128]{2,1,0:T(8,128)(2,1)} %get-tuple-element.33), calls=%async_computation.1 | async-start | bytes 4194304 | tf_op jit(solution)/shard_map/all_to_all | solution.py:442
  81.0 0.1 copy.26
  81.0 0.1 copy.27
  81.2 0.1 stack.31
  81.3 0.1 copy.28
  81.4 0.1 rev.3
  81.5 0.1 stack.32
  81.7 29.8 %all-to-all-done.1.got_ref = bf16[128,64,128]{2,1,0:T(8,128)(2,1)S(1)} async-done(((bf16[128,64,128]{2,1,0:T(8,128)(2,1)}), bf16[128,64,128]{2,1,0:T(8,128)(2,1)S(1)}, u32[]{:S(2)}, u32[]{:S(2)}) %all-to-all-start.1) | async-done | bytes 2097184 | tf_op jit(solution)/shard_map/all_to_all | solution.py:442
  111.5 7.9 %collect.1 = bf16[2,2048,768]{2,1,0:T(8,128)(2,1)} custom-call(s32[2,1,640]{2,1,0:T(1,128)S(1)} %broadcast_in_dim.3.label_ref, bf16[128,64,128]{2,1,0:T(8,128)(2,1)S(1)} %all-to-all-done.1.got_ref), custom_call_target="tpu_custom_call" | custom-call | tf_op jit(solution)/shard_map/collect/pallas_call | solution.py:426
  (5 shorter events, 0.0 us)
Async XLA Ops:
  0.6 15.4 %copy-start = (bf16[768,768]{1,0:T(8,128)(2,1)S(1)}, bf16[768,768]{1,0:T(8,128)(2,1)}, u32[]{:S(2)}) copy-start(bf16[768,768]{1,0:T(8,128)(2,1)} %param.20) | copy-start | bytes 3538948
  2.1 8.6 %copy-start.5 = (s32[2,512]{1,0:T(2,128)S(1)}, s32[2,512]{1,0:T(2,128)}, u32[]{:S(2)}) copy-start(s32[2,512]{1,0:T(2,128)} %row_ref.1) | copy-start | bytes 12292
  2.1 13.9 %copy-start.3 = (bf16[512,768]{1,0:T(8,128)(2,1)S(1)}, bf16[512,768]{1,0:T(8,128)(2,1)}, u32[]{:S(2)}) copy-start(bf16[512,768]{1,0:T(8,128)(2,1)} %refs_12_.1) | copy-start | bytes 2359300
  2.1 16.5 %collective-permute-start = (bf16[2,512,512]{2,1,0:T(8,128)(2,1)S(1)}, bf16[2,512,512]{2,1,0:T(8,128)(2,1)}, u32[]{:S(2)}, u32[]{:S(2)}) collective-permute-start(bf16[2,512,512]{2,1,0:T(8,128)(2,1)S(1)} %pad_maximum_fusion), channel_id=1, source_target_pairs={{0,1},{1,2},{2,3},{3,4},{4,5},{5,6},{6,7},{7,8},{8,9},{9,10},{10,1... | collective-permute-start | bytes 3145736 | tf_op jit(solution)/shard_map/ppermute | solution.py:42
  8.8 25.7 %collective-permute-start.2 = (bf16[2,512,256]{2,1,0:T(8,128)(2,1)}, bf16[2,512,256]{2,1,0:T(8,128)(2,1)S(1)}, u32[]{:S(2)}, u32[]{:S(2)}) collective-permute-start(bf16[2,512,256]{2,1,0:T(8,128)(2,1)} %pad_maximum_fusion.1), channel_id=1, source_target_pairs={{0,1},{1,2},{2,3},{3,4},{4,5},{5,6},{6,7},{7,8},{8,9},{9,10},{10,1... | collective-permute-start | bytes 1572872 | tf_op jit(solution)/shard_map/ppermute | solution.py:42
  32.6 12.8 %copy-start.6 = (s32[1,1280]{1,0:T(1,128)S(1)}, s32[1,1280]{1,0:T(1,128)}, u32[]{:S(2)}) copy-start(s32[1,1280]{1,0:T(1,128)} %get-tuple-element.32) | copy-start | bytes 15364
  32.6 26.2 %copy-start.7 = (f32[768]{0:T(1024)S(1)}, f32[768]{0:T(1024)}, u32[]{:S(2)}) copy-start(f32[768]{0:T(1024)} %param.13) | copy-start | bytes 9220
  32.6 26.8 %collective-permute-start.1 = (bf16[2,512,512]{2,1,0:T(8,128)(2,1)}, bf16[2,512,512]{2,1,0:T(8,128)(2,1)S(1)}, u32[]{:S(2)}, u32[]{:S(2)}) collective-permute-start(bf16[2,512,512]{2,1,0:T(8,128)(2,1)} %get-tuple-element.22), channel_id=1, source_target_pairs={{1,0},{2,1},{3,2},{4,3},{5,4},{6,5},{7,6},{8,7},{9,8},{10,9},{11,1... | collective-permute-start | bytes 3145736 | tf_op jit(solution)/shard_map/ppermute | solution.py:42
  34.5 0.8 copy-start.1
  43.5 15.9 %collective-permute-start.3 = (bf16[2,512,256]{2,1,0:T(8,128)(2,1)}, bf16[2,512,256]{2,1,0:T(8,128)(2,1)S(1)}, u32[]{:S(2)}, u32[]{:S(2)}) collective-permute-start(bf16[2,512,256]{2,1,0:T(8,128)(2,1)} %get-tuple-element.26), channel_id=1, source_target_pairs={{1,0},{2,1},{3,2},{4,3},{5,4},{6,5},{7,6},{8,7},{9,8},{10,9},{11,1... | collective-permute-start | bytes 1572872 | tf_op jit(solution)/shard_map/ppermute | solution.py:42
  46.4 24.2 %all-to-all-start = ((s32[128,2,5]{2,1,0:T(2,128)}), s32[128,2,5]{2,1,0:T(2,128)S(1)}, u32[]{:S(2)}, u32[]{:S(2)}) async-start(s32[128,2,5]{2,1,0:T(2,128)} %reshape.27), calls=%async_computation | async-start | bytes 262144 | tf_op jit(solution)/shard_map/all_to_all | solution.py:442
  59.4 0.8 copy-start.4
  59.4 1.2 copy-start.2
  70.5 40.9 %all-to-all-start.1 = ((bf16[128,64,128]{2,1,0:T(8,128)(2,1)}), bf16[128,64,128]{2,1,0:T(8,128)(2,1)S(1)}, u32[]{:S(2)}, u32[]{:S(2)}) async-start(bf16[128,64,128]{2,1,0:T(8,128)(2,1)} %get-tuple-element.33), calls=%async_computation.1 | async-start | bytes 4194304 | tf_op jit(solution)/shard_map/all_to_all | solution.py:442

commit v5 on v4

--- a/solution.py
+++ b/solution.py
@@ -19,7 +19,7 @@
 BF16 = jnp.bfloat16
 F32 = jnp.float32
 I32 = jnp.int32
-GROUPS = (4, 2)
+GROUPS = (3, 3)
 
 
 def iota(shape, dim):
@@ -44,13 +44,14 @@
 
 MAIN = 4
 CHUNK = 64
-
-
-def slots_kernel(first_ref, row_ref, col_ref, slot_ref, label_ref):
+MARK = 64
+
+
+def slots_kernel(first_ref, row_ref, col_ref, slot_ref, mark_ref):
     count = row_ref.shape[1]
-    places = label_ref.shape[1]
+    devices = mark_ref.shape[1]
     odd = lax.rem(first_ref[0] // count, 2)
-    labels = jnp.full((1, places), ROWS_DEV, I32)
+    high = low = jnp.zeros((devices, LANES), F32)
     sub = iota((count, count), 0)
     lane = iota((count, count), 1)
     for table in range(NG):
@@ -69,18 +70,18 @@
         slot_ref[table : table + 1, :] = jnp.where(place_row < MAIN, main, -1)
         last = row_owner * NG + table
         slot_ref[NG + table : NG + table + 1, :] = jnp.where(place_row < MAIN, -1, last)
-        slot_col = col_owner * (NG * SLOTS) + table * SLOTS + place_col
-        local_col = col - col_owner * ROWS_DEV
-        hit = slot_col == iota((count, places), 1)
-        labels = jnp.minimum(
-            labels, jnp.min(jnp.where(hit, local_col, ROWS_DEV), axis=0, keepdims=True)
-        )
-    label_ref[...] = labels
+        value = col - col_owner * ROWS_DEV + 1
+        here = first_col & (iota((count, LANES), 1) == table * SLOTS + place_col)
+        owned = jnp.where(row_owner == iota((devices, count), 0), 1.0, 0.0).astype(BF16)
+        part = lambda x: jnp.where(here, x.astype(F32), 0.0).astype(BF16)
+        high = high + dot(owned, part(value // MARK), 1, 0)
+        low = low + dot(owned, part(lax.rem(value, MARK)), 1, 0)
+    mark_ref[0] = high.astype(BF16)
+    mark_ref[1] = low.astype(BF16)
 
 
 def make_slots(first, hash_ids, devices):
     count = hash_ids.shape[1]
-    places = devices * NG * SLOTS
     return pl.pallas_call(
         slots_kernel,
         in_specs=[
@@ -90,7 +91,7 @@
         ],
         out_shape=(
             jax.ShapeDtypeStruct((2 * NG, count), I32),
-            jax.ShapeDtypeStruct((1, places), I32),
+            jax.ShapeDtypeStruct((2, devices, LANES), BF16),
         ),
         compiler_params=params(56),
         name="slots",
@@ -245,12 +246,12 @@
 
 def finish_kernel(*refs):
     groups = len(GROUPS)
-    parts = [refs[4 * g : 4 * g + 4] for g in range(groups)]
+    parts = [refs[3 * g : 3 * g + 3] for g in range(groups)]
     (
-        wq_in, wk_in, wv_in, hidden_in, out_in, gain_ref, slot_ref, gh_out, sent_out,
-        dq_ref, dk_ref, dv_ref, back_ref, wq_ref, wk_ref, wv_ref, hidden_ref, out_ref,
+        norm_in, wk_in, wv_in, hidden_in, out_in, gain_ref, slot_ref, mark_ref, gh_out, sent_out,
+        norm_ref, dk_ref, dv_ref, back_ref, wk_ref, wv_ref, hidden_ref, out_ref,
         gh_ref, sent_ref, sems,
-    ) = refs[4 * groups :]
+    ) = refs[3 * groups :]
     count, width = hidden_ref.shape
     devices = sent_ref.shape[0]
     started = []
@@ -273,15 +274,15 @@
         spans.append(slice(at * LANES, (at + pairs) * LANES))
         at += pairs
     need_hidden = bring((hidden_in, hidden_ref))
-    need_q = bring(*[(p[0], dq_ref.at[:, c]) for p, c in zip(parts, spans)], (wq_in, wq_ref))
     need_k = bring(
-        *[(p[1].at[0], back_ref.at[0, :, c]) for p, c in zip(parts, spans)],
-        *[(p[2], dk_ref.at[:, c]) for p, c in zip(parts, spans)],
+        *[(p[0].at[0], back_ref.at[0, :, c]) for p, c in zip(parts, spans)],
+        *[(p[1], dk_ref.at[:, c]) for p, c in zip(parts, spans)],
         (wk_in, wk_ref),
     )
+    need_norm = bring((norm_in, norm_ref))
     need_v = bring(
-        *[(p[1].at[1], back_ref.at[1, :, c]) for p, c in zip(parts, spans)],
-        *[(p[3], dv_ref.at[:, c]) for p, c in zip(parts, spans)],
+        *[(p[0].at[1], back_ref.at[1, :, c]) for p, c in zip(parts, spans)],
+        *[(p[2], dv_ref.at[:, c]) for p, c in zip(parts, spans)],
         (wv_in, wv_ref),
     )
     need_out = bring((out_in, out_ref))
@@ -295,19 +296,25 @@
     blocks = width // LANES
     both = NG * MAIN
     tail = CHUNK - blocks * both
-    shape = (SPREAD * tail, blocks * SPREAD * NG)
+    lasts = blocks * NG
+    shape = (SPREAD * tail, (lasts + 2) * SPREAD)
     row = iota((shape[0], 1), 0)
     inner = lax.rem(row, tail)
-    source = (inner // NG) * (SPREAD * NG) + (row // tail) * NG + lax.rem(inner, NG)
-    lay = jnp.where((inner < blocks * NG) & (source == iota(shape, 1)), 1.0, 0.0).astype(BF16)
+    owner = row // tail
+    source = jnp.where(
+        inner < lasts,
+        (inner // NG) * (SPREAD * NG) + owner * NG + lax.rem(inner, NG),
+        inner * SPREAD + owner,
+    )
+    lay = jnp.where((inner < lasts + 2) & (source == iota(shape, 1)), 1.0, 0.0).astype(BF16)
 
     arrive(need_hidden)
     full = hidden_ref[...].astype(F32)
     inverse = lax.rsqrt(jnp.mean(full * full, axis=1, keepdims=True) + EPS)
-    arrive(need_q)
-    norm = dot(dq_ref[...], wq_ref[...], 1, 1)
     arrive(need_k)
-    norm = norm + dot((dk_ref[...] + back_ref[0].astype(F32)).astype(BF16), wk_ref[...], 1, 1)
+    norm = dot((dk_ref[...] + back_ref[0].astype(F32)).astype(BF16), wk_ref[...], 1, 1)
+    arrive(need_norm)
+    norm = norm_ref[...] + norm
     arrive(need_v)
     norm = norm + dot((dv_ref[...] + back_ref[1].astype(F32)).astype(BF16), wv_ref[...], 1, 1)
     arrive(need_out)
@@ -330,7 +337,11 @@
             ).astype(BF16)
         for low in range(at, at + PACK, SPREAD):
             some = rest[low * NG : (low + SPREAD) * NG]
-            some = jnp.concatenate([cut(some, c) for c in range(blocks)], axis=0)
+            some = jnp.concatenate(
+                [cut(some, c) for c in range(blocks)]
+                + [mark_ref[part, low : low + SPREAD, :] for part in range(2)],
+                axis=0,
+            )
             sent_ref[low : low + SPREAD, blocks * both :, :] = (
                 dot(lay, some, 1, 0).reshape(SPREAD, tail, LANES).astype(BF16)
             )
@@ -338,26 +349,26 @@
     arrive(leaving)
 
 
-def finish(parts, wq, wk, wv, hidden, gain, grad_out, slot, devices):
+def finish(parts, norm, wk, wv, hidden, gain, grad_out, slot, mark):
     count, width = hidden.shape
+    devices = mark.shape[1]
     groups = len(GROUPS)
     place = pl.BlockSpec(memory_space=pl.ANY)
     small = pl.BlockSpec(memory_space=pltpu.VMEM)
-    copies = 5 * groups + 6 + devices // PACK
+    copies = 4 * groups + 6 + devices // PACK
     return pl.pallas_call(
         finish_kernel,
-        in_specs=[place] * (4 * groups + 5) + [small] * 2,
+        in_specs=[place] * (3 * groups + 5) + [small] * 3,
         out_specs=(place, place),
         out_shape=(
             jax.ShapeDtypeStruct((count, width), BF16),
             jax.ShapeDtypeStruct((devices, CHUNK, LANES), BF16),
         ),
         scratch_shapes=[
-            pltpu.VMEM((count, width), BF16),
+            pltpu.VMEM((count, width), F32),
             pltpu.VMEM((count, width), F32),
             pltpu.VMEM((count, width), F32),
             pltpu.VMEM((2, WINDOW, width), BF16),
-            pltpu.VMEM((width, width), BF16),
             pltpu.VMEM((width, width), BF16),
             pltpu.VMEM((width, width), BF16),
             pltpu.VMEM((count, width), BF16),
@@ -370,7 +381,7 @@
         name="finish",
     )(
         *[array for part in parts for array in part],
-        wq, wk, wv, hidden, grad_out, gain.reshape(1, width), slot,
+        norm, wk, wv, hidden, grad_out, gain.reshape(1, width), slot, mark,
     )
 
 
@@ -378,7 +389,7 @@
 APART = 16
 
 
-def collect_kernel(label_ref, got_ref, out_ref, rows_ref):
+def collect_kernel(got_ref, out_ref, rows_ref, mark_ref, label_ref):
     devices = got_ref.shape[0]
     blocks = rows_ref.shape[2] // LANES
     both = NG * MAIN
@@ -399,12 +410,13 @@
                 one = jnp.where(low, odd, even).reshape(mains, LANES)
                 rows_ref[0, :mains, cols] = zero.astype(BF16)
                 rows_ref[1, :mains, cols] = one.astype(BF16)
-        shape = (NG * blocks * APART, APART * tail)
+        lasts = NG * blocks
+        shape = ((lasts + 2) * APART, APART * tail)
         row = iota((shape[0], 1), 0)
         device = lax.rem(row, APART)
         block = lax.rem(row // APART, blocks)
         table = row // (APART * blocks)
-        source = device * tail + block * NG + table
+        source = device * tail + jnp.where(table < NG, block * NG + table, row // APART)
         pick = jnp.where(source == iota(shape, 1), 1.0, 0.0).astype(BF16)
         for at in range(0, devices, APART):
             rest = got_ref[at : at + APART, blocks * both :, :].reshape(APART * tail, LANES)
@@ -415,27 +427,44 @@
                     rows_ref[t, mains + at : mains + at + APART, c * LANES : (c + 1) * LANES] = rest[
                         start : start + APART
                     ]
+            for part in range(2):
+                start = (lasts + part) * APART
+                mark_ref[part, at : at + APART, :] = rest[start : start + APART]
+        number = label_ref.shape[2]
+        k = iota((1, number), 1)
+        for t in range(NG):
+            source = k // MAIN
+            if t == 1:
+                source = source + 1 - 2 * lax.rem(source, 2)
+            source = jnp.where(k < mains, source, k - mains)
+            slot = t * SLOTS + jnp.where(k < mains, lax.rem(k, MAIN), MAIN)
+            take = jnp.where(slot == iota((LANES, number), 0), 1.0, 0.0).astype(BF16)
+            value = MARK * dot(mark_ref[0], take, 1, 0) + dot(mark_ref[1], take, 1, 0)
+            value = jnp.where(source == iota((devices, number), 0), value, 0.0)
+            label_ref[t] = jnp.sum(value, axis=0, keepdims=True).astype(I32) - 1
 
     place = pl.program_id(1) * COLLECT + iota((COLLECT, label_ref.shape[2]), 0)
-    hit = jnp.where(place == label_ref[0], 1.0, 0.0).astype(BF16)
+    hit = jnp.where(place == label_ref[pl.program_id(0)], 1.0, 0.0).astype(BF16)
     out_ref[0] = dot(hit, rows_ref[pl.program_id(0)], 1, 0).astype(BF16)
 
 
-def collect(labels, got, width):
-    tables, _, number = labels.shape
+def collect(got, width):
+    devices = got.shape[0]
+    number = devices * SLOTS
     return pl.pallas_call(
         collect_kernel,
-        grid=(tables, ROWS_DEV // COLLECT),
-        in_specs=[
-            pl.BlockSpec((1, 1, number), lambda t, i: (t, 0, 0)),
-            pl.BlockSpec(got.shape, lambda t, i: (0, 0, 0)),
+        grid=(NG, ROWS_DEV // COLLECT),
+        in_specs=[pl.BlockSpec(got.shape, lambda t, i: (0, 0, 0))],
+        out_specs=pl.BlockSpec((1, COLLECT, width), lambda t, i: (t, i, 0)),
+        out_shape=jax.ShapeDtypeStruct((NG, ROWS_DEV, width), BF16),
+        scratch_shapes=[
+            pltpu.VMEM((NG, number, width), BF16),
+            pltpu.VMEM((2, devices, LANES), BF16),
+            pltpu.VMEM((NG, 1, number), I32),
         ],
-        out_specs=pl.BlockSpec((1, COLLECT, width), lambda t, i: (t, i, 0)),
-        out_shape=jax.ShapeDtypeStruct((tables, ROWS_DEV, width), BF16),
-        scratch_shapes=[pltpu.VMEM((tables, number, width), BF16)],
         compiler_params=params(28),
         name="collect",
-    )(labels, got)
+    )(got)
 
 
 def exchanged(part):
@@ -466,26 +495,24 @@
         halos.append(shifted(jnp.stack([keys[:, cols], values[:, cols]]), 1))
         at += pairs
     grad_attn = dot(grad_out, w_out, 1, 1).astype(BF16)
-    slot, labels = make_slots(first, hash_ids, devices)
-    grad_attn, slot, labels = lax.optimization_barrier((grad_attn, slot, labels))
+    slot, mark = make_slots(first, hash_ids, devices)
+    grad_attn, slot, mark = lax.optimization_barrier((grad_attn, slot, mark))
     parts = []
+    queries_part = []
     at = 0
     for pairs, halo in zip(GROUPS, halos):
         dq, back, dk, dv = attention_grads(
             first, doc_lengths, queries, halo, keys, values, grad_attn, at
         )
-        parts.append((dq, shifted(back, -1), dk, dv))
+        queries_part.append(dq)
+        parts.append((shifted(back, -1), dk, dv))
         at += pairs
-    labels, _ = lax.optimization_barrier((labels, parts[-1][0]))
-    labels = exchanged(labels.reshape(devices, NG, SLOTS))
-    labels = jnp.transpose(labels, (1, 0, 2))
-    main = labels[:, :, :MAIN].reshape(NG, devices // 2, 2, MAIN)
-    main = jnp.stack([main[0], main[1, :, ::-1]])
-    labels = jnp.concatenate([main.reshape(NG, devices * MAIN), labels[:, :, MAIN]], axis=1)
+    grad_q = jnp.concatenate(lax.optimization_barrier(queries_part), axis=1)
+    norm = dot(grad_q, w_query, 1, 1)
     grad_hidden, sent = finish(
-        parts, w_query, w_key, w_value, hidden, gain, grad_out, slot, devices
-    )
-    return grad_hidden, collect(labels[:, None, :], exchanged(sent), width)
+        parts, norm, w_key, w_value, hidden, gain, grad_out, slot, mark
+    )
+    return grad_hidden, collect(exchanged(sent), width)
 
 
 def solution(mesh):

time: 120 us -> 118 us (0.983)
  blocking collectives: 0 us -> 44.5 us
  waiting for transfers between devices: 30.6 us -> 8.07 us
  starting transfers between devices: 33.3 us -> 11.9 us
  local copies, waits for them, and re-layouts: 7.51 us -> 4.01 us
  matrix products: 1.69 us -> 4.67 us
    all_to_all x0 -> x1, blocking collectives: none -> 44.5 us  [exchanged(): return lax.all_to_all(part, AXES, split_axis=0, concat_axis=0, tiled=True)]
    all_to_all x2 -> x0, waiting for transfers between devices: 29.8 us -> none  [exchanged(): return lax.all_to_all(part, AXES, split_axis=0, concat_axis=0, tiled=True)]
    all_to_all x2 -> x0, starting transfers between devices: 22.9 us -> none  [exchanged(): return lax.all_to_all(part, AXES, split_axis=0, concat_axis=0, tiled=True)]
    ppermute x4, waiting for transfers between devices: 0.89 us -> 8.07 us  [shifted(): return lax.ppermute(shard, AXES, pairs)]
    dot_general x1 -> x2, matrix products: 1.69 us -> 4.67 us  [dot(): lax.dot_general(left, right, (((left_dim,), (right_dim,)), ((), ())), pre...]
    ppermute x4, starting transfers between devices: 10.5 us -> 11.9 us  [shifted(): return lax.ppermute(shard, AXES, pairs)]
    another operation x2 -> x1, local copies, waits for them, and re-layouts: 2.44 us -> 1.61 us  [shards(): halos.append(shifted(jnp.stack([keys[:, cols], values[:, cols]]), 1))]
  transfers between devices with their start and end apart: 6 -> 4, of which waited for: 2 -> 2; matrix products, arithmetic and copies ran while one was open for 6% -> 5% of each run, Pallas kernels for 31% -> 22%
where the time goes in v5:
time: 118 us; the launch traced here: 117 us
  blocking collectives  44.5 us (38%)
  Pallas kernels  43.2 us (37%)
  starting transfers between devices  11.9 us (10%)
  waiting for transfers between devices  8.07 us (7%)
  matrix products  4.67 us (4%)
  local copies, waits for them, and re-layouts  4.01 us (3%)
    all_to_all x1, blocking collectives, exchanged(): return lax.all_to_all(part, AXES, split_axis=0, concat_axis=0, tiled=True)  44.5 us
    pallas_call x2, Pallas kernels, attention_grads(): pl.pallas_call(attention_kernel, grid=(pairs,), in_specs=[pl.BlockSpec(me...  22.1 us
    ppermute x4, starting transfers between devices, shifted(): return lax.ppermute(shard, AXES, pairs)  11.9 us
    pallas_call x1, Pallas kernels, finish(): pl.pallas_call(finish_kernel, in_specs=[place] * (3 * groups + 5) + [smal...  8.83 us
    pallas_call x1, Pallas kernels, collect(): pl.pallas_call(collect_kernel, grid=(NG, ROWS_DEV // COLLECT), in_specs=[...  8.21 us
    ppermute x4, waiting for transfers between devices, shifted(): return lax.ppermute(shard, AXES, pairs)  8.07 us
    dot_general x2, matrix products, dot(): lax.dot_general(left, right, (((left_dim,), (right_dim,)), ((), ())), pre...  4.67 us
    pallas_call x1, Pallas kernels, make_slots(): pl.pallas_call(slots_kernel, in_specs=[pl.BlockSpec(memory_space=pltpu.SM...  4.06 us
  transfers between devices with their start and end apart: 4, of which 2 were waited for; matrix products, arithmetic and copies ran while one was open for 5% of the time, Pallas kernels for 22%

profile of v5, /device:TPU:1, one launch (start us, length us, event | category | flops | bytes accessed | tf_op | source)
XLA Modules:
  0.0 117.4 jit_solution(13361712752951711283)
XLA Ops:
  0.6 0.0 copy-start
  0.6 1.6 %slice_bitcast_fusion = (bf16[1,512,384]{2,1,0:T(8,128)(2,1)S(1)}, bf16[1,512,384]{2,1,0:T(8,128)(2,1)S(1)}, bf16[1,512,384]{2,1,0:T(8,128)(2,1)S(1)}, bf16[1,512,384]{2,1,0:T(8,128)(2,1)S(1)}) fusion(bf16[512,768]{1,0:T(8,128)(2,1)} %vo_ref.3, bf16[512,768]{1,0:T(8,128)(2,1)} %ko_ref.3), kind=kLoop, calls=%fused_computation.7 | loop fusion | bytes 3145728 | tf_op jit(solution)/shard_map/stack | solution.py:495
  2.3 0.1 pad_maximum_fusion.1
  2.4 0.0 copy-start.4
  2.4 0.0 copy-start.1
  2.4 4.7 %collective-permute-start.2 = (bf16[2,512,384]{2,1,0:T(8,128)(2,1)S(1)}, bf16[2,512,384]{2,1,0:T(8,128)(2,1)}, u32[]{:S(2)}, u32[]{:S(2)}) collective-permute-start(bf16[2,512,384]{2,1,0:T(8,128)(2,1)S(1)} %pad_maximum_fusion.1), channel_id=1, source_target_pairs={{0,1},{1,2},{2,3},{3,4},{4,5},{5,6},{6,7},{7,8},{8,9},{9,10},{10,1... | collective-permute-start | bytes 2359304 | tf_op jit(solution)/shard_map/ppermute | solution.py:42
  7.1 0.1 pad_maximum_fusion
  7.2 1.9 %collective-permute-start = (bf16[2,512,384]{2,1,0:T(8,128)(2,1)S(1)}, bf16[2,512,384]{2,1,0:T(8,128)(2,1)}, u32[]{:S(2)}, u32[]{:S(2)}) collective-permute-start(bf16[2,512,384]{2,1,0:T(8,128)(2,1)S(1)} %pad_maximum_fusion), channel_id=1, source_target_pairs={{0,1},{1,2},{2,3},{3,4},{4,5},{5,6},{6,7},{7,8},{8,9},{9,10},{10,1... | collective-permute-start | bytes 2359304 | tf_op jit(solution)/shard_map/ppermute | solution.py:42
  9.1 0.0 copy-done.4
  9.2 0.9 copy.14
  10.0 4.1 %slots.1 = (s32[4,512]{1,0:T(4,128)}, bf16[2,128,128]{2,1,0:T(8,128)(2,1)}) custom-call(s32[1]{0:T(128)} %bitcast.first_ref, s32[2,512]{1,0:T(2,128)} %row_ref.1, s32[512,2]{1,0:T(8,128)} %bitcast.14), custom_call_target="tpu_custom_call" | custom-call | tf_op jit(solution)/shard_map/slots/pallas_call | solution.py:85
  14.1 0.0 copy-done
  14.1 0.0 copy-done.1
  14.1 1.7 %convolution_convert_fusion.da_ref = bf16[512,768]{1,0:T(8,128)(2,1)} fusion(bf16[512,768]{1,0:T(8,128)(2,1)S(1)} %copy-done.1, bf16[768,768]{1,0:T(8,128)(2,1)S(1)} %copy-done), kind=kOutput, calls=%fused_computation | convolution fusion | flops 604372992 | bytes 2752512 | tf_op jit(solution)/shard_map/dot_general | solution.py:30
  15.8 0.3 collective-permute-done.2.kp_ref.vp_ref
  16.0 11.0 %attention.3 = (bf16[512,384]{1,0:T(8,128)(2,1)}, bf16[2,512,384]{2,1,0:T(8,128)(2,1)}, f32[512,384]{1,0:T(8,128)}, f32[512,384]{1,0:T(8,128)}) custom-call(s32[1]{0:T(128)} %bitcast.first_ref, s32[1,64]{1,0:T(1,128)} %bitcast.15, bf16[512,768]{1,0:T(8,128)(2,1)} %q_ref.3, bf16[2,512,384]{2,1,0:T(8,128)(2,1)} %collective-permute-done.2.kp_ref.vp_ref, ...), custom_call_target="tpu_custom_call" | custom-call | flops 1509949440 | bytes 3932160 | tf_op jit(solution)/shard_map/attention/pallas_call | solution.py:207
  27.1 0.0 copy-start.5
  27.1 0.0 copy-start.6
  27.1 0.0 copy-start.7
  27.1 3.2 %collective-permute-start.3 = (bf16[2,512,384]{2,1,0:T(8,128)(2,1)}, bf16[2,512,384]{2,1,0:T(8,128)(2,1)S(1)}, u32[]{:S(2)}, u32[]{:S(2)}) collective-permute-start(bf16[2,512,384]{2,1,0:T(8,128)(2,1)} %get-tuple-element.25), channel_id=1, source_target_pairs={{1,0},{2,1},{3,2},{4,3},{5,4},{6,5},{7,6},{8,7},{9,8},{10,9},{11,1... | collective-permute-start | bytes 2359304 | tf_op jit(solution)/shard_map/ppermute | solution.py:42
  30.3 0.0 collective-permute-done.kp_ref.vp_ref
  30.3 11.1 %attention.2 = (bf16[512,384]{1,0:T(8,128)(2,1)}, bf16[2,512,384]{2,1,0:T(8,128)(2,1)}, f32[512,384]{1,0:T(8,128)}, f32[512,384]{1,0:T(8,128)}) custom-call(s32[1]{0:T(128)} %bitcast.first_ref, s32[1,64]{1,0:T(1,128)} %bitcast.16, bf16[512,768]{1,0:T(8,128)(2,1)} %q_ref.3, bf16[2,512,384]{2,1,0:T(8,128)(2,1)} %collective-permute-done.kp_ref.vp_ref, ...), custom_call_target="tpu_custom_call" | custom-call | flops 1509949440 | bytes 3932160 | tf_op jit(solution)/shard_map/attention/pallas_call | solution.py:207
  41.4 2.1 %collective-permute-start.1 = (bf16[2,512,384]{2,1,0:T(8,128)(2,1)}, bf16[2,512,384]{2,1,0:T(8,128)(2,1)S(1)}, u32[]{:S(2)}, u32[]{:S(2)}) collective-permute-start(bf16[2,512,384]{2,1,0:T(8,128)(2,1)} %get-tuple-element.22), channel_id=1, source_target_pairs={{1,0},{2,1},{3,2},{4,3},{5,4},{6,5},{7,6},{8,7},{9,8},{10,9},{11,1... | collective-permute-start | bytes 2359304 | tf_op jit(solution)/shard_map/ppermute | solution.py:42
  43.5 0.0 copy-done.5
  43.5 0.6 reshape.16.refs_11_
  44.1 0.0 copy-done.6
  44.1 0.0 copy-done.7
  44.1 3.0 %fusion.refs_6_ = f32[512,768]{1,0:T(8,128)} fusion(bf16[768,768]{1,0:T(8,128)(2,1)S(1)} %copy-done.6, bf16[512,384]{1,0:T(8,128)(2,1)S(1)} %copy-done.7, bf16[512,384]{1,0:T(8,128)(2,1)} %get-tuple-element.30), kind=kOutput, calls=%fused_computation.3 | convolution fusion | flops 605552640 | bytes 3538944 | tf_op jit(solution)/shard_map/dot_general | solution.py:30
  47.1 0.0 collective-permute-done.3.refs_3_
  47.1 0.0 copy-start.2
  47.1 7.8 %collective-permute-done.1.refs_0_ = bf16[2,512,384]{2,1,0:T(8,128)(2,1)S(1)} collective-permute-done((bf16[2,512,384]{2,1,0:T(8,128)(2,1)}, bf16[2,512,384]{2,1,0:T(8,128)(2,1)S(1)}, u32[]{:S(2)}, u32[]{:S(2)}) %collective-permute-start.1) | collective-permute-done | bytes 786464 | tf_op jit(solution)/shard_map/ppermute | solution.py:42
  54.9 0.0 copy-start.3
  54.9 0.0 copy-done.2
  54.9 0.9 copy-done.3
  55.8 8.8 %finish.1 = (bf16[512,768]{1,0:T(8,128)(2,1)}, bf16[128,64,128]{2,1,0:T(8,128)(2,1)}) custom-call(bf16[2,512,384]{2,1,0:T(8,128)(2,1)} %copy-done.3, f32[512,384]{1,0:T(8,128)} %get-tuple-element.23.refs_1_, f32[512,384]{1,0:T(8,128)} %get-tuple-element.24.refs_2_, bf16[2,512,384]{2,1,0:T(8,128)(2,1)} %copy-done.2, f32[512,384]{1,0:T(8,128)} %get-tuple-element.26.refs_4_, ...), custom_call_target="tpu_custom_call" | custom-call | tf_op jit(solution)/shard_map/finish/pallas_call | solution.py:359
  64.6 44.5 %all_to_all.5.got_ref = bf16[128,64,128]{2,1,0:T(8,128)(2,1)S(1)} all-to-all(bf16[128,64,128]{2,1,0:T(8,128)(2,1)} %get-tuple-element.35), channel_id=1, replica_groups=mesh['seq'=16,'table'=8] {'seq','table'}, dimensions={0} | all-to-all | bytes 4194304 | tf_op jit(solution)/shard_map/all_to_all | solution.py:471
  109.2 8.2 %collect.1 = bf16[2,2048,768]{2,1,0:T(8,128)(2,1)} custom-call(bf16[128,64,128]{2,1,0:T(8,128)(2,1)S(1)} %all_to_all.5.got_ref), custom_call_target="tpu_custom_call" | custom-call | tf_op jit(solution)/shard_map/collect/pallas_call | solution.py:454
Async XLA Ops:
  0.6 13.5 %copy-start = (bf16[768,768]{1,0:T(8,128)(2,1)S(1)}, bf16[768,768]{1,0:T(8,128)(2,1)}, u32[]{:S(2)}) copy-start(bf16[768,768]{1,0:T(8,128)(2,1)} %param.20) | copy-start | bytes 3538948
  2.4 6.8 %copy-start.4 = (s32[2,512]{1,0:T(2,128)S(1)}, s32[2,512]{1,0:T(2,128)}, u32[]{:S(2)}) copy-start(s32[2,512]{1,0:T(2,128)} %row_ref.1) | copy-start | bytes 12292
  2.4 11.7 %copy-start.1 = (bf16[512,768]{1,0:T(8,128)(2,1)S(1)}, bf16[512,768]{1,0:T(8,128)(2,1)}, u32[]{:S(2)}) copy-start(bf16[512,768]{1,0:T(8,128)(2,1)} %refs_10_.1) | copy-start | bytes 2359300
  2.4 13.6 %collective-permute-start.2 = (bf16[2,512,384]{2,1,0:T(8,128)(2,1)S(1)}, bf16[2,512,384]{2,1,0:T(8,128)(2,1)}, u32[]{:S(2)}, u32[]{:S(2)}) collective-permute-start(bf16[2,512,384]{2,1,0:T(8,128)(2,1)S(1)} %pad_maximum_fusion.1), channel_id=1, source_target_pairs={{0,1},{1,2},{2,3},{3,4},{4,5},{5,6},{6,7},{7,8},{8,9},{9,10},{10,1... | collective-permute-start | bytes 2359304 | tf_op jit(solution)/shard_map/ppermute | solution.py:42
  7.2 23.1 %collective-permute-start = (bf16[2,512,384]{2,1,0:T(8,128)(2,1)S(1)}, bf16[2,512,384]{2,1,0:T(8,128)(2,1)}, u32[]{:S(2)}, u32[]{:S(2)}) collective-permute-start(bf16[2,512,384]{2,1,0:T(8,128)(2,1)S(1)} %pad_maximum_fusion), channel_id=1, source_target_pairs={{0,1},{1,2},{2,3},{3,4},{4,5},{5,6},{6,7},{7,8},{8,9},{9,10},{10,1... | collective-permute-start | bytes 2359304 | tf_op jit(solution)/shard_map/ppermute | solution.py:42
  27.1 16.4 %copy-start.5 = (f32[768]{0:T(1024)S(1)}, f32[768]{0:T(1024)}, u32[]{:S(2)}) copy-start(f32[768]{0:T(1024)} %param.13) | copy-start | bytes 9220
  27.1 17.0 %copy-start.6 = (bf16[768,768]{1,0:T(8,128)(2,1)S(1)}, bf16[768,768]{1,0:T(8,128)(2,1)}, u32[]{:S(2)}) copy-start(bf16[768,768]{1,0:T(8,128)(2,1)} %param.17) | copy-start | bytes 3538948
  27.1 17.0 %copy-start.7 = (bf16[512,384]{1,0:T(8,128)(2,1)S(1)}, bf16[512,384]{1,0:T(8,128)(2,1)}, u32[]{:S(2)}) copy-start(bf16[512,384]{1,0:T(8,128)(2,1)} %get-tuple-element.31) | copy-start | bytes 1179652
  27.1 20.0 %collective-permute-start.3 = (bf16[2,512,384]{2,1,0:T(8,128)(2,1)}, bf16[2,512,384]{2,1,0:T(8,128)(2,1)S(1)}, u32[]{:S(2)}, u32[]{:S(2)}) collective-permute-start(bf16[2,512,384]{2,1,0:T(8,128)(2,1)} %get-tuple-element.25), channel_id=1, source_target_pairs={{1,0},{2,1},{3,2},{4,3},{5,4},{6,5},{7,6},{8,7},{9,8},{10,9},{11,1... | collective-permute-start | bytes 2359304 | tf_op jit(solution)/shard_map/ppermute | solution.py:42
  41.4 13.5 %collective-permute-start.1 = (bf16[2,512,384]{2,1,0:T(8,128)(2,1)}, bf16[2,512,384]{2,1,0:T(8,128)(2,1)S(1)}, u32[]{:S(2)}, u32[]{:S(2)}) collective-permute-start(bf16[2,512,384]{2,1,0:T(8,128)(2,1)} %get-tuple-element.22), channel_id=1, source_target_pairs={{1,0},{2,1},{3,2},{4,3},{5,4},{6,5},{7,6},{8,7},{9,8},{10,9},{11,1... | collective-permute-start | bytes 2359304 | tf_op jit(solution)/shard_map/ppermute | solution.py:42
  47.1 7.8 %copy-start.2 = (bf16[2,512,384]{2,1,0:T(8,128)(2,1)}, bf16[2,512,384]{2,1,0:T(8,128)(2,1)S(1)}, u32[]{:S(2)}) copy-start(bf16[2,512,384]{2,1,0:T(8,128)(2,1)S(1)} %collective-permute-done.3.refs_3_) | copy-start | bytes 2359300
  54.9 0.9 copy-start.3

commit v6 on v5

--- a/solution.py
+++ b/solution.py
@@ -396,27 +396,19 @@
     tail = CHUNK - blocks * both
     mains = devices * MAIN
 
-    @pl.when((pl.program_id(0) == 0) & (pl.program_id(1) == 0))
+    table = pl.program_id(0)
+    opening = (table == 0) & (pl.program_id(1) == 0)
+    place = pl.program_id(1) * COLLECT + iota((COLLECT, label_ref.shape[2]), 0)
+
+    @pl.when(opening)
     def _():
-        low = iota((devices // 2, both, LANES), 1) < MAIN
-        for c in range(0, blocks, 2):
-            wide = got_ref[:, c * both : (c + 2) * both, :].astype(F32)
-            for i in range(2):
-                cols = slice((c + i) * LANES, (c + i + 1) * LANES)
-                piece = wide[:, i * both : (i + 1) * both, :]
-                piece = piece.reshape(devices // 2, 2, both, LANES)
-                even, odd = piece[:, 0], piece[:, 1]
-                zero = jnp.where(low, even, odd).reshape(mains, LANES)
-                one = jnp.where(low, odd, even).reshape(mains, LANES)
-                rows_ref[0, :mains, cols] = zero.astype(BF16)
-                rows_ref[1, :mains, cols] = one.astype(BF16)
         lasts = NG * blocks
         shape = ((lasts + 2) * APART, APART * tail)
         row = iota((shape[0], 1), 0)
         device = lax.rem(row, APART)
         block = lax.rem(row // APART, blocks)
-        table = row // (APART * blocks)
-        source = device * tail + jnp.where(table < NG, block * NG + table, row // APART)
+        which = row // (APART * blocks)
+        source = device * tail + jnp.where(which < NG, block * NG + which, row // APART)
         pick = jnp.where(source == iota(shape, 1), 1.0, 0.0).astype(BF16)
         for at in range(0, devices, APART):
             rest = got_ref[at : at + APART, blocks * both :, :].reshape(APART * tail, LANES)
@@ -442,10 +434,26 @@
             value = MARK * dot(mark_ref[0], take, 1, 0) + dot(mark_ref[1], take, 1, 0)
             value = jnp.where(source == iota((devices, number), 0), value, 0.0)
             label_ref[t] = jnp.sum(value, axis=0, keepdims=True).astype(I32) - 1
-
-    place = pl.program_id(1) * COLLECT + iota((COLLECT, label_ref.shape[2]), 0)
-    hit = jnp.where(place == label_ref[pl.program_id(0)], 1.0, 0.0).astype(BF16)
-    out_ref[0] = dot(hit, rows_ref[pl.program_id(0)], 1, 0).astype(BF16)
+        hit = jnp.where(place == label_ref[0], 1.0, 0.0).astype(BF16)
+        low = iota((devices // 2, both, LANES), 1) < MAIN
+        for c in range(0, blocks, 2):
+            wide = got_ref[:, c * both : (c + 2) * both, :].astype(F32)
+            for i in range(2):
+                cols = slice((c + i) * LANES, (c + i + 1) * LANES)
+                piece = wide[:, i * both : (i + 1) * both, :]
+                piece = piece.reshape(devices // 2, 2, both, LANES)
+                even, odd = piece[:, 0], piece[:, 1]
+                zero = jnp.where(low, even, odd).reshape(mains, LANES)
+                one = jnp.where(low, odd, even).reshape(mains, LANES)
+                rows_ref[0, :mains, cols] = zero.astype(BF16)
+                rows_ref[1, :mains, cols] = one.astype(BF16)
+            cols = slice(c * LANES, (c + 2) * LANES)
+            out_ref[0, :, cols] = dot(hit, rows_ref[0, :, cols], 1, 0).astype(BF16)
+
+    @pl.when(jnp.logical_not(opening))
+    def _():
+        hit = jnp.where(place == label_ref[table], 1.0, 0.0).astype(BF16)
+        out_ref[0] = dot(hit, rows_ref[table], 1, 0).astype(BF16)
 
 
 def collect(got, width):

time: 118 us -> 117 us (level)
  no operation moved by 1% of the time
where the time goes in v6:
time: 117 us
  blocking collectives  44.5 us (38%)
  Pallas kernels  42.8 us (37%)
  starting transfers between devices  11.9 us (10%)
  waiting for transfers between devices  8.07 us (7%)
  matrix products  4.67 us (4%)
  local copies, waits for them, and re-layouts  4.01 us (3%)
    all_to_all x1, blocking collectives, exchanged(): return lax.all_to_all(part, AXES, split_axis=0, concat_axis=0, tiled=True)  44.5 us
    pallas_call x2, Pallas kernels, attention_grads(): pl.pallas_call(attention_kernel, grid=(pairs,), in_specs=[pl.BlockSpec(me...  22.1 us
    ppermute x4, starting transfers between devices, shifted(): return lax.ppermute(shard, AXES, pairs)  11.9 us
    pallas_call x1, Pallas kernels, finish(): pl.pallas_call(finish_kernel, in_specs=[place] * (3 * groups + 5) + [smal...  8.83 us
    ppermute x4, waiting for transfers between devices, shifted(): return lax.ppermute(shard, AXES, pairs)  8.07 us
    pallas_call x1, Pallas kernels, collect(): pl.pallas_call(collect_kernel, grid=(NG, ROWS_DEV // COLLECT), in_specs=[...  7.83 us
    dot_general x2, matrix products, dot(): lax.dot_general(left, right, (((left_dim,), (right_dim,)), ((), ())), pre...  4.67 us
    pallas_call x1, Pallas kernels, make_slots(): pl.pallas_call(slots_kernel, in_specs=[pl.BlockSpec(memory_space=pltpu.SM...  4.06 us
  transfers between devices with their start and end apart: 4, of which 2 were waited for; matrix products, arithmetic and copies ran while one was open for 5% of the time, Pallas kernels for 22%

profile of v6, /device:TPU:1, one launch (start us, length us, event | category | flops | bytes accessed | tf_op | source)
XLA Modules:
  0.0 117.0 jit_solution(10390325963576183386)
XLA Ops:
  0.6 0.0 copy-start
  0.6 1.6 %slice_bitcast_fusion = (bf16[1,512,384]{2,1,0:T(8,128)(2,1)S(1)}, bf16[1,512,384]{2,1,0:T(8,128)(2,1)S(1)}, bf16[1,512,384]{2,1,0:T(8,128)(2,1)S(1)}, bf16[1,512,384]{2,1,0:T(8,128)(2,1)S(1)}) fusion(bf16[512,768]{1,0:T(8,128)(2,1)} %vo_ref.3, bf16[512,768]{1,0:T(8,128)(2,1)} %ko_ref.3), kind=kLoop, calls=%fused_computation.7 | loop fusion | bytes 3145728 | tf_op jit(solution)/shard_map/stack | solution.py:503
  2.3 0.1 pad_maximum_fusion.1
  2.4 0.0 copy-start.4
  2.4 0.0 copy-start.1
  2.4 4.7 %collective-permute-start.2 = (bf16[2,512,384]{2,1,0:T(8,128)(2,1)S(1)}, bf16[2,512,384]{2,1,0:T(8,128)(2,1)}, u32[]{:S(2)}, u32[]{:S(2)}) collective-permute-start(bf16[2,512,384]{2,1,0:T(8,128)(2,1)S(1)} %pad_maximum_fusion.1), channel_id=1, source_target_pairs={{0,1},{1,2},{2,3},{3,4},{4,5},{5,6},{6,7},{7,8},{8,9},{9,10},{10,1... | collective-permute-start | bytes 2359304 | tf_op jit(solution)/shard_map/ppermute | solution.py:42
  7.1 0.1 pad_maximum_fusion
  7.2 1.9 %collective-permute-start = (bf16[2,512,384]{2,1,0:T(8,128)(2,1)S(1)}, bf16[2,512,384]{2,1,0:T(8,128)(2,1)}, u32[]{:S(2)}, u32[]{:S(2)}) collective-permute-start(bf16[2,512,384]{2,1,0:T(8,128)(2,1)S(1)} %pad_maximum_fusion), channel_id=1, source_target_pairs={{0,1},{1,2},{2,3},{3,4},{4,5},{5,6},{6,7},{7,8},{8,9},{9,10},{10,1... | collective-permute-start | bytes 2359304 | tf_op jit(solution)/shard_map/ppermute | solution.py:42
  9.1 0.0 copy-done.4
  9.2 0.9 copy.14
  10.0 4.1 %slots.1 = (s32[4,512]{1,0:T(4,128)}, bf16[2,128,128]{2,1,0:T(8,128)(2,1)}) custom-call(s32[1]{0:T(128)} %bitcast.first_ref, s32[2,512]{1,0:T(2,128)} %row_ref.1, s32[512,2]{1,0:T(8,128)} %bitcast.14), custom_call_target="tpu_custom_call" | custom-call | tf_op jit(solution)/shard_map/slots/pallas_call | solution.py:85
  14.1 0.0 copy-done
  14.1 0.0 copy-done.1
  14.1 1.7 %convolution_convert_fusion.da_ref = bf16[512,768]{1,0:T(8,128)(2,1)} fusion(bf16[512,768]{1,0:T(8,128)(2,1)S(1)} %copy-done.1, bf16[768,768]{1,0:T(8,128)(2,1)S(1)} %copy-done), kind=kOutput, calls=%fused_computation | convolution fusion | flops 604372992 | bytes 2752512 | tf_op jit(solution)/shard_map/dot_general | solution.py:30
  15.8 0.3 collective-permute-done.2.kp_ref.vp_ref
  16.0 11.0 %attention.3 = (bf16[512,384]{1,0:T(8,128)(2,1)}, bf16[2,512,384]{2,1,0:T(8,128)(2,1)}, f32[512,384]{1,0:T(8,128)}, f32[512,384]{1,0:T(8,128)}) custom-call(s32[1]{0:T(128)} %bitcast.first_ref, s32[1,64]{1,0:T(1,128)} %bitcast.15, bf16[512,768]{1,0:T(8,128)(2,1)} %q_ref.3, bf16[2,512,384]{2,1,0:T(8,128)(2,1)} %collective-permute-done.2.kp_ref.vp_ref, ...), custom_call_target="tpu_custom_call" | custom-call | flops 1509949440 | bytes 3932160 | tf_op jit(solution)/shard_map/attention/pallas_call | solution.py:207
  27.1 0.0 copy-start.5
  27.1 0.0 copy-start.6
  27.1 0.0 copy-start.7
  27.1 3.2 %collective-permute-start.3 = (bf16[2,512,384]{2,1,0:T(8,128)(2,1)}, bf16[2,512,384]{2,1,0:T(8,128)(2,1)S(1)}, u32[]{:S(2)}, u32[]{:S(2)}) collective-permute-start(bf16[2,512,384]{2,1,0:T(8,128)(2,1)} %get-tuple-element.25), channel_id=1, source_target_pairs={{1,0},{2,1},{3,2},{4,3},{5,4},{6,5},{7,6},{8,7},{9,8},{10,9},{11,1... | collective-permute-start | bytes 2359304 | tf_op jit(solution)/shard_map/ppermute | solution.py:42
  30.3 0.0 collective-permute-done.kp_ref.vp_ref
  30.3 11.1 %attention.2 = (bf16[512,384]{1,0:T(8,128)(2,1)}, bf16[2,512,384]{2,1,0:T(8,128)(2,1)}, f32[512,384]{1,0:T(8,128)}, f32[512,384]{1,0:T(8,128)}) custom-call(s32[1]{0:T(128)} %bitcast.first_ref, s32[1,64]{1,0:T(1,128)} %bitcast.16, bf16[512,768]{1,0:T(8,128)(2,1)} %q_ref.3, bf16[2,512,384]{2,1,0:T(8,128)(2,1)} %collective-permute-done.kp_ref.vp_ref, ...), custom_call_target="tpu_custom_call" | custom-call | flops 1509949440 | bytes 3932160 | tf_op jit(solution)/shard_map/attention/pallas_call | solution.py:207
  41.4 2.1 %collective-permute-start.1 = (bf16[2,512,384]{2,1,0:T(8,128)(2,1)}, bf16[2,512,384]{2,1,0:T(8,128)(2,1)S(1)}, u32[]{:S(2)}, u32[]{:S(2)}) collective-permute-start(bf16[2,512,384]{2,1,0:T(8,128)(2,1)} %get-tuple-element.22), channel_id=1, source_target_pairs={{1,0},{2,1},{3,2},{4,3},{5,4},{6,5},{7,6},{8,7},{9,8},{10,9},{11,1... | collective-permute-start | bytes 2359304 | tf_op jit(solution)/shard_map/ppermute | solution.py:42
  43.5 0.0 copy-done.5
  43.5 0.6 reshape.16.refs_11_
  44.1 0.0 copy-done.6
  44.1 0.0 copy-done.7
  44.1 3.0 %fusion.refs_6_ = f32[512,768]{1,0:T(8,128)} fusion(bf16[768,768]{1,0:T(8,128)(2,1)S(1)} %copy-done.6, bf16[512,384]{1,0:T(8,128)(2,1)S(1)} %copy-done.7, bf16[512,384]{1,0:T(8,128)(2,1)} %get-tuple-element.30), kind=kOutput, calls=%fused_computation.3 | convolution fusion | flops 605552640 | bytes 3538944 | tf_op jit(solution)/shard_map/dot_general | solution.py:30
  47.1 0.0 collective-permute-done.3.refs_3_
  47.1 0.0 copy-start.2
  47.1 7.8 %collective-permute-done.1.refs_0_ = bf16[2,512,384]{2,1,0:T(8,128)(2,1)S(1)} collective-permute-done((bf16[2,512,384]{2,1,0:T(8,128)(2,1)}, bf16[2,512,384]{2,1,0:T(8,128)(2,1)S(1)}, u32[]{:S(2)}, u32[]{:S(2)}) %collective-permute-start.1) | collective-permute-done | bytes 786464 | tf_op jit(solution)/shard_map/ppermute | solution.py:42
  54.9 0.0 copy-start.3
  54.9 0.0 copy-done.2
  54.9 0.9 copy-done.3
  55.8 8.8 %finish.1 = (bf16[512,768]{1,0:T(8,128)(2,1)}, bf16[128,64,128]{2,1,0:T(8,128)(2,1)}) custom-call(bf16[2,512,384]{2,1,0:T(8,128)(2,1)} %copy-done.3, f32[512,384]{1,0:T(8,128)} %get-tuple-element.23.refs_1_, f32[512,384]{1,0:T(8,128)} %get-tuple-element.24.refs_2_, bf16[2,512,384]{2,1,0:T(8,128)(2,1)} %copy-done.2, f32[512,384]{1,0:T(8,128)} %get-tuple-element.26.refs_4_, ...), custom_call_target="tpu_custom_call" | custom-call | tf_op jit(solution)/shard_map/finish/pallas_call | solution.py:359
  64.6 44.5 %all_to_all.5.got_ref = bf16[128,64,128]{2,1,0:T(8,128)(2,1)S(1)} all-to-all(bf16[128,64,128]{2,1,0:T(8,128)(2,1)} %get-tuple-element.35), channel_id=1, replica_groups=mesh['seq'=16,'table'=8] {'seq','table'}, dimensions={0} | all-to-all | bytes 4194304 | tf_op jit(solution)/shard_map/all_to_all | solution.py:479
  109.2 7.8 %collect.1 = bf16[2,2048,768]{2,1,0:T(8,128)(2,1)} custom-call(bf16[128,64,128]{2,1,0:T(8,128)(2,1)S(1)} %all_to_all.5.got_ref), custom_call_target="tpu_custom_call" | custom-call | tf_op jit(solution)/shard_map/collect/pallas_call | solution.py:462
Async XLA Ops:
  0.6 13.5 %copy-start = (bf16[768,768]{1,0:T(8,128)(2,1)S(1)}, bf16[768,768]{1,0:T(8,128)(2,1)}, u32[]{:S(2)}) copy-start(bf16[768,768]{1,0:T(8,128)(2,1)} %param.20) | copy-start | bytes 3538948
  2.4 6.8 %copy-start.4 = (s32[2,512]{1,0:T(2,128)S(1)}, s32[2,512]{1,0:T(2,128)}, u32[]{:S(2)}) copy-start(s32[2,512]{1,0:T(2,128)} %row_ref.1) | copy-start | bytes 12292
  2.4 11.7 %copy-start.1 = (bf16[512,768]{1,0:T(8,128)(2,1)S(1)}, bf16[512,768]{1,0:T(8,128)(2,1)}, u32[]{:S(2)}) copy-start(bf16[512,768]{1,0:T(8,128)(2,1)} %refs_10_.1) | copy-start | bytes 2359300
  2.4 13.6 %collective-permute-start.2 = (bf16[2,512,384]{2,1,0:T(8,128)(2,1)S(1)}, bf16[2,512,384]{2,1,0:T(8,128)(2,1)}, u32[]{:S(2)}, u32[]{:S(2)}) collective-permute-start(bf16[2,512,384]{2,1,0:T(8,128)(2,1)S(1)} %pad_maximum_fusion.1), channel_id=1, source_target_pairs={{0,1},{1,2},{2,3},{3,4},{4,5},{5,6},{6,7},{7,8},{8,9},{9,10},{10,1... | collective-permute-start | bytes 2359304 | tf_op jit(solution)/shard_map/ppermute | solution.py:42
  7.2 23.1 %collective-permute-start = (bf16[2,512,384]{2,1,0:T(8,128)(2,1)S(1)}, bf16[2,512,384]{2,1,0:T(8,128)(2,1)}, u32[]{:S(2)}, u32[]{:S(2)}) collective-permute-start(bf16[2,512,384]{2,1,0:T(8,128)(2,1)S(1)} %pad_maximum_fusion), channel_id=1, source_target_pairs={{0,1},{1,2},{2,3},{3,4},{4,5},{5,6},{6,7},{7,8},{8,9},{9,10},{10,1... | collective-permute-start | bytes 2359304 | tf_op jit(solution)/shard_map/ppermute | solution.py:42
  27.1 16.4 %copy-start.5 = (f32[768]{0:T(1024)S(1)}, f32[768]{0:T(1024)}, u32[]{:S(2)}) copy-start(f32[768]{0:T(1024)} %param.13) | copy-start | bytes 9220
  27.1 17.0 %copy-start.6 = (bf16[768,768]{1,0:T(8,128)(2,1)S(1)}, bf16[768,768]{1,0:T(8,128)(2,1)}, u32[]{:S(2)}) copy-start(bf16[768,768]{1,0:T(8,128)(2,1)} %param.17) | copy-start | bytes 3538948
  27.1 17.0 %copy-start.7 = (bf16[512,384]{1,0:T(8,128)(2,1)S(1)}, bf16[512,384]{1,0:T(8,128)(2,1)}, u32[]{:S(2)}) copy-start(bf16[512,384]{1,0:T(8,128)(2,1)} %get-tuple-element.31) | copy-start | bytes 1179652
  27.1 20.0 %collective-permute-start.3 = (bf16[2,512,384]{2,1,0:T(8,128)(2,1)}, bf16[2,512,384]{2,1,0:T(8,128)(2,1)S(1)}, u32[]{:S(2)}, u32[]{:S(2)}) collective-permute-start(bf16[2,512,384]{2,1,0:T(8,128)(2,1)} %get-tuple-element.25), channel_id=1, source_target_pairs={{1,0},{2,1},{3,2},{4,3},{5,4},{6,5},{7,6},{8,7},{9,8},{10,9},{11,1... | collective-permute-start | bytes 2359304 | tf_op jit(solution)/shard_map/ppermute | solution.py:42
  41.4 13.5 %collective-permute-start.1 = (bf16[2,512,384]{2,1,0:T(8,128)(2,1)}, bf16[2,512,384]{2,1,0:T(8,128)(2,1)S(1)}, u32[]{:S(2)}, u32[]{:S(2)}) collective-permute-start(bf16[2,512,384]{2,1,0:T(8,128)(2,1)} %get-tuple-element.22), channel_id=1, source_target_pairs={{1,0},{2,1},{3,2},{4,3},{5,4},{6,5},{7,6},{8,7},{9,8},{10,9},{11,1... | collective-permute-start | bytes 2359304 | tf_op jit(solution)/shard_map/ppermute | solution.py:42
  47.1 7.8 %copy-start.2 = (bf16[2,512,384]{2,1,0:T(8,128)(2,1)}, bf16[2,512,384]{2,1,0:T(8,128)(2,1)S(1)}, u32[]{:S(2)}) copy-start(bf16[2,512,384]{2,1,0:T(8,128)(2,1)S(1)} %collective-permute-done.3.refs_3_) | copy-start | bytes 2359300
  54.9 0.9 copy-start.3
